TPU v7x, 32 devices: a whole 2x2x4 slice. The times are simulated.
32 devices in a mesh: section: 2 (over core), fsdp: 2 (over x), context: 2 (over y), tensor: 4 (over z).
Axes of the slice: x: 2, y: 2, z: 4, core: 2. Of those that a mesh axis runs over, the one named last changes fastest.
Arguments:
- block_input: bfloat16 [4, 1024, 1536], P('fsdp', 'context'), may hold values from -6 to 6
- doc_start: int32 [4, 1024], P('fsdp', 'context'), may hold values from 0 to 1, as said below
- cotangent: bfloat16 [4, 1024, 1536], P('fsdp', 'context'), may hold values from -6 to 6
- norm_gain: float32 [2, 1536], P('section'), may hold values from 0.5 to 1.5
- proj_main: bfloat16 [2, 1536, 2, 3072], P('section', 'fsdp', None, 'tensor'), may hold values from -0.15625 to 0.15625
- proj_states: bfloat16 [2, 1536, 256], P('section', 'fsdp'), may hold values from -0.15625 to 0.15625
- proj_step: bfloat16 [2, 1536, 48], P('section', 'fsdp', 'tensor'), may hold values from -0.15625 to 0.15625
- conv_main: float32 [2, 4, 3072], P('section', None, 'tensor'), may hold values from -3 to 3
- conv_main_bias: float32 [2, 3072], P('section', 'tensor'), may hold values from -1.5 to 1.5
- conv_states: float32 [2, 4, 256], P('section'), may hold values from -3 to 3
- conv_states_bias: float32 [2, 256], P('section'), may hold values from -1.5 to 1.5
- step_bias: float32 [2, 48], P('section', 'tensor'), may hold values from -6 to -4
- log_decay: float32 [2, 48], P('section', 'tensor'), may hold values from -3.9 to 1.4
- skip_gain: float32 [2, 48], P('section', 'tensor'), may hold values from 0.5 to 1.5
- gated_gain: float32 [2, 3072], P('section', 'tensor'), may hold values from 0.5 to 1.5
- proj_out: bfloat16 [2, 1536, 3072], P('section', 'fsdp', 'tensor'), may hold values from -0.109375 to 0.109375
Outputs:
- layer_out: float32 [2, 4, 1024, 1536], P('section', 'fsdp', 'context')
- layer_in_grad: float32 [2, 4, 1024, 1536], P('section', 'fsdp', 'context')
- grad_norm_gain: float32 [2, 1536], P('section')
- grad_proj_main: float32 [2, 1536, 2, 3072], P('section', ('fsdp', 'context'), None, 'tensor')
- grad_proj_states: float32 [2, 1536, 256], P('section', ('fsdp', 'context'))
- grad_proj_step: float32 [2, 1536, 48], P('section', ('fsdp', 'context'), 'tensor')
- grad_conv_main: float32 [2, 4, 3072], P('section', None, 'tensor')
- grad_conv_main_bias: float32 [2, 3072], P('section', 'tensor')
- grad_conv_states: float32 [2, 4, 256], P('section')
- grad_conv_states_bias: float32 [2, 256], P('section')
- grad_step_bias: float32 [2, 48], P('section', 'tensor')
- grad_log_decay: float32 [2, 48], P('section', 'tensor')
- grad_skip_gain: float32 [2, 48], P('section', 'tensor')
- grad_gated_gain: float32 [2, 3072], P('section', 'tensor')
- grad_proj_out: float32 [2, 1536, 3072], P('section', ('fsdp', 'context'), 'tensor')
Inputs may be any that keep to these rules, and one draw needn't show every extreme that they name: `doc_start`: 1 at the first token of each document and 0 elsewhere; position 0 of every sequence is 1; documents have 60 to 800 tokens unless cut by their sequence's end; among the 2 sequences of each fsdp index one is a single document.
All inputs are finite; a program needn't handle non-finite values.
Results may differ from a plain program's by a relative error of at most 0.01.
Values may be sent and summed in bfloat16 or wider, within the bound.
No kernel may reach another device: no remote copies, remote signals or barrier semaphores. Data moves between devices by JAX's collectives and lax.ppermute only.
A program may use at most 256 MiB of HBM per device.

v0:
```python
import jax
import jax.numpy as jnp
from jax import lax
from jax.sharding import PartitionSpec as P

HEAD_DIM = 64
NSTATE = 128
CONV = 4
SPAN = 256
INNER = 3072


EPS = 1e-05
HIGH = lax.Precision.HIGHEST


def passed_along(value, axis, steps):
    count = lax.axis_size(axis)
    initial, last = (max(0, -steps), min(count, count - steps))
    return lax.ppermute(value, axis, [(source, source + steps) for source in range(initial, last)])


def carried_in(array, axis, combine, identity, reverse):
    count, here = (lax.axis_size(axis), lax.axis_index(axis))
    everything = jax.tree.map(lambda part: lax.all_gather(part, axis), array)
    start = jax.tree.map(
        lambda part, zero: jnp.broadcast_to(jnp.asarray(zero, part.dtype), part.shape),
        array,
        identity,
    )

    def lap(k, before):
        at = count - 1 - k if reverse else k
        reached = at > here if reverse else at < here
        new = combine(before, jax.tree.map(lambda part: part[at], everything))
        return jax.tree.map(lambda a, b: jnp.where(reached, a, b), new, before)

    return lax.fori_loop(0, count, lap, start)


def mixer_inputs(
    full_rows,
    start_marks,
    conv_main,
    conv_main_bias,
    conv_states,
    conv_states_bias,
    step_raw,
    step_bias,
    log_decay,
):
    weight = jnp.concatenate([conv_main, conv_states], axis=1)
    bias_all = jnp.concatenate([conv_main_bias, conv_states_bias])
    length = full_rows.shape[0] - (CONV - 1)
    counts = jnp.cumsum(start_marks)
    conv_sum = jnp.zeros((length, weight.shape[1]), jnp.float32) + bias_all[None, :]
    for offset in range(CONV):
        start_row = CONV - 1 - offset
        window = full_rows[start_row : start_row + length]
        same_doc = counts[CONV - 1 :] - counts[start_row : start_row + length] == 0.0
        conv_sum = conv_sum + weight[offset][None, :] * window * same_doc[:, None].astype(
            jnp.float32
        )
    active = jax.nn.silu(conv_sum)
    inner_width = conv_main.shape[1]
    state_width = conv_states.shape[1] // 2
    values = active[:, :inner_width].reshape(length, -1, HEAD_DIM)
    b_proj = active[:, inner_width : inner_width + state_width]
    c_proj = active[:, inner_width + state_width :]
    step_size = jax.nn.softplus(step_raw + step_bias[None, :])
    decay_rate = -jnp.exp(log_decay)[None, :] * step_size
    return (values, b_proj, c_proj, step_size, decay_rate)


def span_step(state_now, pieces):
    values, b_proj, c_proj, step_size, decay_rate, starts = pieces
    counts = jnp.cumsum(starts)
    cumulative = jnp.cumsum(decay_rate, axis=0)
    final_sum = cumulative[-1]
    position = jnp.arange(starts.shape[0])
    same_doc = (counts[:, None] == counts[None, :]) & (position[:, None] >= position[None, :])
    decay_gap = jnp.where(
        same_doc[:, :, None], cumulative[:, None, :] - cumulative[None, :, :], 0.0
    )
    weights = jnp.where(same_doc[:, :, None], jnp.exp(decay_gap), 0.0)
    scores = jnp.dot(c_proj, b_proj.T, precision=HIGH)
    mixing = scores[:, :, None] * weights * step_size[None, :, :]
    output = jnp.einsum("tsh,shp->thp", mixing, values, precision=HIGH)
    entry_rate = jnp.where((counts == 0)[:, None], jnp.exp(cumulative), 0.0)
    output = output + entry_rate[:, :, None] * jnp.einsum(
        "tn,hpn->thp", c_proj, state_now, precision=HIGH
    )
    carried = (
        jnp.where((counts == counts[-1])[:, None], jnp.exp(final_sum[None, :] - cumulative), 0.0)
        * step_size
    )
    keep_rate = jnp.where(counts[-1] == 0, jnp.exp(final_sum), 0.0)
    new_state = keep_rate[:, None, None] * state_now + jnp.einsum(
        "th,thp,tn->hpn", carried, values, b_proj, precision=HIGH
    )
    return (new_state, output)


def state_step(state_now, pieces):
    values, b_proj, step_size, decay_rate, starts = pieces
    counts = jnp.cumsum(starts).astype(jnp.int32)
    cumulative = jnp.cumsum(decay_rate, axis=0)
    final_sum = cumulative[-1]
    carried = (
        jnp.where((counts == counts[-1])[:, None], jnp.exp(final_sum[None, :] - cumulative), 0.0)
        * step_size
    )
    keep_rate = jnp.where(counts[-1] == 0, jnp.exp(final_sum), 0.0)
    new_state = keep_rate[:, None, None] * state_now + jnp.einsum(
        "th,thp,tn->hpn", carried, values, b_proj, precision=HIGH
    )
    return (new_state, keep_rate)


def scan_spans(values, b_proj, c_proj, step_size, decay_rate, starts, state_in):
    length = values.shape[0]
    block = min(SPAN, length)
    span_count = length // block
    head_count = values.shape[1]
    pieces = (
        values.reshape(span_count, block, head_count, HEAD_DIM),
        b_proj.reshape(span_count, block, -1),
        c_proj.reshape(span_count, block, -1),
        step_size.reshape(span_count, block, head_count),
        decay_rate.reshape(span_count, block, head_count),
        starts.reshape(span_count, block),
    )
    state_out, outputs = lax.scan(span_step, state_in, pieces)
    return (outputs.reshape(length, head_count, HEAD_DIM), state_out)


def states_only(values, b_proj, step_size, decay_rate, starts, state_in):
    length = values.shape[0]
    block = min(SPAN, length)
    span_count = length // block
    head_count = values.shape[1]
    pieces = (
        values.reshape(span_count, block, head_count, HEAD_DIM),
        b_proj.reshape(span_count, block, -1),
        step_size.reshape(span_count, block, head_count),
        decay_rate.reshape(span_count, block, head_count),
        starts.reshape(span_count, block),
    )
    state_out, rates = lax.scan(state_step, state_in, pieces)
    return (state_out, jnp.prod(rates, axis=0))


def gated_part(mixed_out, values, gate_z, skip_gain):
    length = values.shape[0]
    combined = (mixed_out + skip_gain[None, :, None] * values).reshape(length, -1)
    return combined * jax.nn.silu(gate_z)


def chain_combine(earlier, later_part):
    rate_early, state_early = earlier
    rate_late, state_late = later_part
    return (rate_early * rate_late, rate_late[:, None, None] * state_early + state_late)


def tensor_sum(value):
    return lax.psum(value, "tensor")


def send_back(grad_inputs):
    return passed_along(grad_inputs, "section", -1)


def tail_mask(start_marks_local, length):
    tail_marks = start_marks_local[length - CONV + 1 :]
    after_count = jnp.cumsum(tail_marks[::-1])[::-1] - tail_marks
    return (after_count == 0.0).astype(jnp.float32)


def weight_terms(operands):
    normed, grad_main, grad_cols, grad_step_low, grad_low, scaled = operands
    grad_weight_main = jnp.einsum(
        "ld,lki->dki", normed, grad_main, preferred_element_type=jnp.float32
    )
    grad_weight_states = jnp.einsum(
        "ld,ln->dn", normed, grad_cols, preferred_element_type=jnp.float32
    )
    grad_weight_step = jnp.einsum(
        "ld,lh->dh", normed, grad_step_low, preferred_element_type=jnp.float32
    )
    grad_weight_out = jnp.einsum("ld,li->di", grad_low, scaled, preferred_element_type=jnp.float32)
    return (grad_weight_main, grad_weight_states, grad_weight_step, grad_weight_out)


def shards(
    block_input,
    doc_start,
    cotangent,
    norm_gain,
    proj_main,
    proj_states,
    proj_step,
    conv_main,
    conv_main_bias,
    conv_states,
    conv_states_bias,
    step_bias,
    log_decay,
    skip_gain,
    gated_gain,
    proj_out,
):
    section_index = lax.axis_index("section")
    on_second = section_index == 1
    first_tensor = (lax.axis_index("tensor") == 0).astype(jnp.float32)
    micro_count = block_input.shape[0]
    length = block_input.shape[1]
    model_width = block_input.shape[2]
    head_count = proj_step.shape[2]
    gain_vector = norm_gain[0]
    conv_first = conv_main[0]
    bias_first = conv_main_bias[0]
    conv_second = conv_states[0]
    bias_second = conv_states_bias[0]
    step_offset = step_bias[0]
    decay_log = log_decay[0]
    skip_vector = skip_gain[0]
    gated_vector = gated_gain[0]
    local_weights = (proj_main[0], proj_states[0], proj_step[0], proj_out[0])
    zero_state = jnp.zeros((head_count, HEAD_DIM, NSTATE), jnp.float32)
    unit_rate = jnp.ones((head_count,), jnp.float32)

    def fetch_weights():
        return (
            lax.all_gather(local_weights[0], "fsdp", axis=0, tiled=True),
            lax.all_gather(local_weights[1], "fsdp", axis=0, tiled=True),
            lax.all_gather(local_weights[2], "fsdp", axis=0, tiled=True),
            lax.all_gather(local_weights[3], "fsdp", axis=0, tiled=True),
        )

    def backward(grad_out, kept_values, weights):
        (
            inputs,
            inv_rms,
            normed,
            main_cols,
            step_raw,
            full_rows,
            start_marks,
            starts,
            state_in,
            inv_rms_gated,
            tail_keep,
        ) = kept_values
        weight_main, weight_states, weight_step, weight_out = weights

        def mixing_inputs(
            row_block,
            conv_a_taps,
            conv_a_bias,
            conv_b_taps,
            conv_b_bias,
            step_input,
            step_shift,
            decay_logs,
        ):
            return mixer_inputs(
                row_block,
                start_marks,
                conv_a_taps,
                conv_a_bias,
                conv_b_taps,
                conv_b_bias,
                step_input,
                step_shift,
                decay_logs,
            )

        mixer_out, pull_mixer = jax.vjp(
            mixing_inputs,
            full_rows,
            conv_first,
            bias_first,
            conv_second,
            bias_second,
            step_raw,
            step_offset,
            decay_log,
        )
        values, b_proj, c_proj, step_size, decay_rate = mixer_out

        def outputs_only(values_in, b_in, c_in, step_in, decay_in, state_start):
            return scan_spans(values_in, b_in, c_in, step_in, decay_in, starts, state_start)[0]

        def states_with_rate(values_in, b_in, step_in, decay_in, state_start):
            return states_only(values_in, b_in, step_in, decay_in, starts, state_start)

        mixed_out, pull_outputs = jax.vjp(
            outputs_only, values, b_proj, c_proj, step_size, decay_rate, state_in
        )
        gated, pull_gated = jax.vjp(gated_part, mixed_out, values, main_cols[:, 0], skip_vector)
        scaled = (gated * inv_rms_gated[:, None] * gated_vector[None, :]).astype(jnp.bfloat16)
        grad_low = grad_out.astype(jnp.bfloat16)
        grad_scaled = jnp.einsum(
            "ld,di->li", grad_low, weight_out, preferred_element_type=jnp.float32
        )
        grad_gated_gain = jnp.sum(grad_scaled * gated * inv_rms_gated[:, None], axis=0)
        weighted = grad_scaled * gated_vector[None, :]
        dot_gated = tensor_sum(jnp.sum(weighted * gated, axis=-1))
        cube_gated = inv_rms_gated * inv_rms_gated * inv_rms_gated
        grad_gated = (
            inv_rms_gated[:, None] * weighted - gated * (cube_gated * dot_gated / INNER)[:, None]
        )
        grad_mixed, grad_values_skip, grad_gate_z, grad_skip = pull_gated(grad_gated)
        grad_values, grad_b, grad_c, grad_step, grad_decay, grad_state_local = pull_outputs(
            grad_mixed
        )
        state_out, pull_states, local_rate = jax.vjp(
            states_with_rate, values, b_proj, step_size, decay_rate, state_in, has_aux=True
        )
        suffix = carried_in(
            (local_rate, grad_state_local), "context", chain_combine, (unit_rate, zero_state), True
        )
        state_values, state_b, state_step_grad, state_decay, state_unused = pull_states(suffix[1])
        grad_values = grad_values + grad_values_skip + state_values
        grad_b = grad_b + state_b
        grad_step = grad_step + state_step_grad
        grad_decay = grad_decay + state_decay
        shared = tensor_sum(jnp.concatenate([grad_b, grad_c], axis=1))
        (
            grad_rows,
            grad_conv_first,
            grad_bias_first,
            grad_conv_second,
            grad_bias_second,
            grad_raw,
            grad_step_offset,
            grad_decay_log,
        ) = pull_mixer((grad_values, shared[:, :NSTATE], shared[:, NSTATE:], grad_step, grad_decay))
        back_rows = passed_along(grad_rows[: CONV - 1], "context", -1)
        inner_width = main_cols.shape[2]
        padding = jnp.zeros((length - CONV + 1, grad_rows.shape[1]), jnp.float32)
        grad_pre = grad_rows[CONV - 1 :] + jnp.concatenate(
            [padding, back_rows * tail_keep[:, None]], axis=0
        )
        grad_main = jnp.stack([grad_gate_z, grad_pre[:, :inner_width]], axis=1).astype(jnp.bfloat16)
        grad_cols = grad_pre[:, inner_width:].astype(jnp.bfloat16)
        grad_step_low = grad_raw.astype(jnp.bfloat16)
        grad_normed = jnp.einsum(
            "lki,dki->ld", grad_main, weight_main, preferred_element_type=jnp.float32
        )
        grad_normed = grad_normed + jnp.einsum(
            "lh,dh->ld", grad_step_low, weight_step, preferred_element_type=jnp.float32
        )
        grad_normed = grad_normed + first_tensor * jnp.einsum(
            "ln,dn->ld", grad_cols, weight_states, preferred_element_type=jnp.float32
        )
        grad_normed = lax.psum(grad_normed, "tensor")
        grad_gain = jnp.sum(grad_normed * inputs * inv_rms[:, None], axis=0)
        weighted_in = grad_normed * gain_vector[None, :]
        dot_input = jnp.mean(weighted_in * inputs, axis=-1)
        cube_input = inv_rms * inv_rms * inv_rms
        grad_inputs = (
            grad_out + inv_rms[:, None] * weighted_in - inputs * (cube_input * dot_input)[:, None]
        )
        small_grads = (
            grad_gain,
            grad_conv_first,
            grad_bias_first,
            grad_conv_second,
            grad_bias_second,
            grad_step_offset,
            grad_decay_log,
            grad_skip,
            grad_gated_gain,
        )
        operands = (normed, grad_main, grad_cols, grad_step_low, grad_low, scaled)
        return (grad_inputs, small_grads, operands)

    weights = fetch_weights()
    rounds = micro_count + 1
    slot_index = jnp.arange(micro_count)[:, None, None]
    received = jnp.zeros((length, model_width), jnp.float32)
    out_buffer = jnp.zeros((micro_count, length, model_width), jnp.float32)
    kept_list = []
    for round_index in range(rounds):
        batch_index = round_index - section_index
        own_input = block_input[min(round_index, micro_count - 1)].astype(jnp.float32)
        inputs = jnp.where(on_second, received, own_input)
        starts = lax.dynamic_index_in_dim(
            doc_start, jnp.clip(batch_index, 0, micro_count - 1), 0, keepdims=False
        )
        forward_weight_main, forward_weight_states, forward_weight_step, forward_weight_out = (
            weights
        )
        forward_inv_rms = lax.rsqrt(jnp.mean(inputs * inputs, axis=-1) + EPS)
        forward_normed = (inputs * forward_inv_rms[:, None] * gain_vector[None, :]).astype(
            jnp.bfloat16
        )
        forward_main_cols = jnp.einsum(
            "ld,dki->lki", forward_normed, forward_weight_main, preferred_element_type=jnp.float32
        )
        state_cols = jnp.dot(
            forward_normed, forward_weight_states, preferred_element_type=jnp.float32
        )
        forward_step_raw = jnp.dot(
            forward_normed, forward_weight_step, preferred_element_type=jnp.float32
        )
        pre_conv = jnp.concatenate([forward_main_cols[:, 1], state_cols], axis=1)
        marks_local = starts.astype(jnp.float32)
        forward_tail_keep = tail_mask(marks_local, length)
        prev_rows = passed_along(
            pre_conv[length - CONV + 1 :] * forward_tail_keep[:, None], "context", 1
        )
        forward_full_rows = jnp.concatenate([prev_rows, pre_conv], axis=0)
        forward_start_marks = jnp.concatenate([jnp.zeros((CONV - 1,), jnp.float32), marks_local])
        forward_values, forward_b_proj, forward_c_proj, forward_step_size, forward_decay_rate = (
            mixer_inputs(
                forward_full_rows,
                forward_start_marks,
                conv_first,
                bias_first,
                conv_second,
                bias_second,
                forward_step_raw,
                step_offset,
                decay_log,
            )
        )
        local_state, forward_local_rate = states_only(
            forward_values,
            forward_b_proj,
            forward_step_size,
            forward_decay_rate,
            starts,
            zero_state,
        )
        prefix = carried_in(
            (forward_local_rate, local_state),
            "context",
            chain_combine,
            (unit_rate, zero_state),
            False,
        )
        forward_state_in = prefix[1]
        forward_mixed_out, state_end = scan_spans(
            forward_values,
            forward_b_proj,
            forward_c_proj,
            forward_step_size,
            forward_decay_rate,
            starts,
            forward_state_in,
        )
        forward_gated = gated_part(
            forward_mixed_out, forward_values, forward_main_cols[:, 0], skip_vector
        )
        forward_inv_rms_gated = lax.rsqrt(
            tensor_sum(jnp.sum(forward_gated * forward_gated, axis=-1)) / INNER + EPS
        )
        forward_scaled = (
            forward_gated * forward_inv_rms_gated[:, None] * gated_vector[None, :]
        ).astype(jnp.bfloat16)
        partial_out = jnp.einsum(
            "li,di->ld", forward_scaled, forward_weight_out, preferred_element_type=jnp.float32
        )
        branch = lax.psum(partial_out, "tensor")
        forward_kept_values = (
            inputs,
            forward_inv_rms,
            forward_normed,
            forward_main_cols,
            forward_step_raw,
            forward_full_rows,
            forward_start_marks,
            starts,
            forward_state_in,
            forward_inv_rms_gated,
            forward_tail_keep,
        )
        result = inputs + branch
        kept_values = forward_kept_values
        kept_list.append(kept_values)
        out_buffer = jnp.where(slot_index == batch_index, result[None], out_buffer)
        if round_index < micro_count:
            received = passed_along(result, "section", 1)
    weights = fetch_weights()
    received = jnp.zeros((length, model_width), jnp.float32)
    grad_buffer = jnp.zeros((micro_count, length, model_width), jnp.float32)
    small_totals = None
    matrix_totals = None
    for round_index in range(rounds):
        batch_index = round_index - 1 + section_index
        is_valid = (batch_index >= 0) & (batch_index < micro_count)
        own_grad = cotangent[min(round_index, micro_count - 1)].astype(jnp.float32)
        grad_out = jnp.where(is_valid, jnp.where(on_second, own_grad, received), 0.0)
        upper_kept = kept_list[min(round_index + 1, micro_count)]
        lower_kept = kept_list[max(round_index - 1, 0)]
        kept_values = jax.tree.map(
            lambda upper_value, lower_value: jnp.where(on_second, upper_value, lower_value),
            upper_kept,
            lower_kept,
        )
        grad_inputs, small_grads, operands = backward(grad_out, kept_values, weights)
        small_totals = (
            small_grads
            if small_totals is None
            else jax.tree.map(jnp.add, small_totals, small_grads)
        )
        grad_buffer = jnp.where(slot_index == batch_index, grad_inputs[None], grad_buffer)
        terms = weight_terms(operands)
        matrix_totals = (
            terms if matrix_totals is None else jax.tree.map(jnp.add, matrix_totals, terms)
        )
        if round_index < micro_count:
            received = send_back(grad_inputs)
    reduced = (
        lax.psum_scatter(matrix_totals[0], ("fsdp", "context"), scatter_dimension=0, tiled=True),
        lax.psum_scatter(matrix_totals[1], ("fsdp", "context"), scatter_dimension=0, tiled=True),
        lax.psum_scatter(matrix_totals[2], ("fsdp", "context"), scatter_dimension=0, tiled=True),
        lax.psum_scatter(matrix_totals[3], ("fsdp", "context"), scatter_dimension=0, tiled=True),
    )
    vectors = lax.psum(
        (
            small_totals[0],
            small_totals[1],
            small_totals[2],
            small_totals[3],
            small_totals[4],
            small_totals[5],
            small_totals[6],
            small_totals[7],
            small_totals[8],
        ),
        ("fsdp", "context"),
    )
    return (
        out_buffer[None],
        grad_buffer[None],
        vectors[0][None],
        reduced[0][None],
        reduced[1][None],
        reduced[2][None],
        vectors[1][None],
        vectors[2][None],
        vectors[3][None],
        vectors[4][None],
        vectors[5][None],
        vectors[6][None],
        vectors[7][None],
        vectors[8][None],
        reduced[3][None],
    )


def solution(mesh):
    placed = (
        P("fsdp", "context", None),
        P("fsdp", "context"),
        P("fsdp", "context", None),
        P("section", None),
        P("section", "fsdp", None, "tensor"),
        P("section", "fsdp", None),
        P("section", "fsdp", "tensor"),
        P("section", None, "tensor"),
        P("section", "tensor"),
        P("section", None, None),
        P("section", None),
        P("section", "tensor"),
        P("section", "tensor"),
        P("section", "tensor"),
        P("section", "tensor"),
        P("section", "fsdp", "tensor"),
    )
    return jax.shard_map(
        shards,
        mesh=mesh,
        in_specs=placed,
        out_specs=(
            P("section", "fsdp", "context", None),
            P("section", "fsdp", "context", None),
            P("section", None),
            P("section", ("fsdp", "context"), None, "tensor"),
            P("section", ("fsdp", "context"), None),
            P("section", ("fsdp", "context"), "tensor"),
            P("section", None, "tensor"),
            P("section", "tensor"),
            P("section", None, None),
            P("section", None),
            P("section", "tensor"),
            P("section", "tensor"),
            P("section", "tensor"),
            P("section", "tensor"),
            P("section", ("fsdp", "context"), "tensor"),
        ),
        check_vma=False,
    )
```

profile of v0, /device:TPU:0, one launch (start us, length us, event | category | flops | bytes accessed | tf_op | source)
XLA Modules:
  0.0 2782.9 jit_solution(2826411264154232071)
XLA Ops:
  22.1 21.6 all-gather.2
  59.2 25.8 all-gather.19.cloned.1.call-done
  136.2 58.2 %while.579 = (s32[]{:T(128)}, f32[12,64,128]{2,1,0:T(8,128)S(1)}, f32[2,256,12,64]{1,0,3,2:T(2,128)}, s32[2,256]{1,0:T(2,128)S(1)}, f32[2,256,12]{1,2,0:T(8,128)...) while((s32[]{:T(128)}, f32[12,64,128]{2,1,0:T(8,128)S(1)}, ...), condition=%wide.region_18.19_spmd, body=%wide.region_13.18_spmd.sunk | while | flops 1313976832 | bytes 9798831 | solution.py:133
  147.0 16.7 dynamic_update_slice.1199
  176.1 16.7 dynamic_update_slice.1199
  220.9 118.2 %all-reduce.66.cloned.1.call-done = f32[512,1536]{1,0:T(8,128)} async-done(((f32[512,1536]{1,0:T(8,128)}), f32[512,1536]{1,0:T(8,128)}) %all-reduce.66.cloned.1.call-update) | async-done | bytes 3145744 | tf_op jit(solution)/shard_map/psum | solution.py:466
  424.9 67.3 %while.580 = (s32[]{:T(128)}, f32[12,64,128]{2,1,0:T(8,128)S(1)}, f32[2,256,12,64]{1,0,3,2:T(2,128)}, s32[2,256]{1,0:T(2,128)}, f32[2,256,12]{1,2,0:T(8,128)}, /...) while((s32[]{:T(128)}, f32[12,64,128]{2,1,0:T(8,128)S(1)}, ...), condition=%wide.region_40.41_spmd, body=%wide.region_35.40_spmd.sunk | while | flops 1313976832 | bytes 9794779 | solution.py:133
  439.0 16.7 dynamic_update_slice.1200
  472.7 16.7 dynamic_update_slice.1200
  521.2 114.9 %all-reduce.68.cloned.1.call-done = f32[512,1536]{1,0:T(8,128)} async-done(((f32[512,1536]{1,0:T(8,128)}), f32[512,1536]{1,0:T(8,128)}) %all-reduce.68.cloned.1.call-update) | async-done | bytes 3145744 | tf_op jit(solution)/shard_map/psum | solution.py:466
  734.9 66.0 %while.581 = (s32[]{:T(128)}, f32[12,64,128]{2,1,0:T(8,128)S(1)}, f32[2,256,12,64]{1,0,3,2:T(2,128)}, s32[2,256]{1,0:T(2,128)}, f32[2,256,12]{1,2,0:T(8,128)S(1)...) while((s32[]{:T(128)}, f32[12,64,128]{2,1,0:T(8,128)S(1)}, ...), condition=%wide.region_62.63_spmd, body=%wide.region_57.62_spmd.sunk | while | flops 1313976832 | bytes 10847191 | solution.py:133
  747.7 16.8 dynamic_update_slice.1201
  780.8 16.8 dynamic_update_slice.1201
  835.0 88.8 %while.588 = (s32[]{:T(128)}, f32[12,64,128]{2,1,0:T(8,128)S(1)}, f32[2,256,12,64]{1,0,3,2:T(2,128)}, pred[2,256,256,12]{2,1,3,0:T(32,128)(4,1)}, f32[2,256,256,...) while((s32[]{:T(128)}, f32[12,64,128]{2,1,0:T(8,128)S(1)}, ...), condition=%wide.region_73.75_spmd.clone, body=%wide.region_68.74_spmd.clone.sunk | while | flops 1318105600 | bytes 44546440 | solution.py:133
  853.5 16.7 dynamic_update_slice.1250
  897.8 16.7 dynamic_update_slice.1250
  966.9 151.9 %while.597 = (s32[]{:T(128)}, f32[12,64,128]{2,1,0:T(8,128)S(1)}, f32[2,256,12,64]{1,0,3,2:T(2,128)}, f32[2,256,128]{2,1,0:T(8,128)}, f32[2,256,128]{2,1,0:T(8,1...) while((s32[]{:T(128)}, f32[12,64,128]{2,1,0:T(8,128)S(1)}, ...), condition=%wide.region_86.88_spmd.clone, body=%wide.region_76.87_spmd.clone.sunk | while | flops 2628676608 | bytes 46134472 | solution.py:133
  1016.2 16.7 dynamic_update_slice.1290
  1091.9 16.7 dynamic_update_slice.1290
  1158.8 81.1 %while.583 = (s32[]{:T(128)}, f32[12,64,128]{2,1,0:T(8,128)S(1)}, f32[2,256,12,64]{1,0,3,2:T(2,128)}, f32[2,256,128]{2,1,0:T(8,128)}, f32[2,256,12]{2,1,0:T(8,12...) while((s32[]{:T(128)}, f32[12,64,128]{2,1,0:T(8,128)S(1)}, ...), condition=%wide.region_100.102_spmd, body=%wide.region_95.101_spmd.sunk | while | flops 605276288 | bytes 22673968 | solution.py:149
  1182.6 16.7 dynamic_update_slice.1213
  1223.2 16.7 dynamic_update_slice.1213
  1264.4 19.3 all-reduce.70.cloned.1.call-done
  1342.3 90.6 %while.589 = (s32[]{:T(128)}, f32[12,64,128]{2,1,0:T(8,128)S(1)}, f32[2,256,12,64]{1,0,3,2:T(2,128)}, pred[2,256,256,12]{2,1,3,0:T(32,128)(4,1)}, f32[2,256,256,...) while((s32[]{:T(128)}, f32[12,64,128]{2,1,0:T(8,128)S(1)}, ...), condition=%wide.region_111.113_spmd.clone, body=%wide.region_106.112_spmd.clone.sunk | while | flops 1318105600 | bytes 43575568 | solution.py:133
  1362.4 16.7 dynamic_update_slice.1265
  1407.6 16.7 dynamic_update_slice.1265
  1511.0 152.7 %while.599 = (s32[]{:T(128)}, f32[12,64,128]{2,1,0:T(8,128)S(1)}, f32[2,256,12,64]{1,0,3,2:T(2,128)}, f32[2,256,128]{2,1,0:T(8,128)}, f32[2,256,128]{2,1,0:T(8,1...) while((s32[]{:T(128)}, f32[12,64,128]{2,1,0:T(8,128)S(1)}, ...), condition=%wide.region_124.126_spmd.clone, body=%wide.region_114.125_spmd.clone.sunk | while | flops 2628676608 | bytes 50205352 | solution.py:133
  1560.6 16.8 dynamic_update_slice.1295
  1636.7 16.8 dynamic_update_slice.1295
  1679.7 77.5 %while.585 = (s32[]{:T(128)}, f32[12,64,128]{2,1,0:T(8,128)S(1)}, f32[2,256,12,64]{1,0,3,2:T(2,128)}, f32[2,256,128]{2,1,0:T(8,128)}, f32[2,256,12]{2,1,0:T(8,12...) while((s32[]{:T(128)}, f32[12,64,128]{2,1,0:T(8,128)S(1)}, ...), condition=%wide.region_138.140_spmd, body=%wide.region_133.139_spmd.sunk | while | flops 605276288 | bytes 19528212 | solution.py:149
  1701.8 16.7 dynamic_update_slice.1225
  1740.5 16.7 dynamic_update_slice.1225
  1771.6 28.1 %all-reduce.74.cloned.1.call-done = f32[512,256]{1,0:T(8,128)} async-done(((f32[512,256]{1,0:T(8,128)}), f32[512,256]{1,0:T(8,128)}) %all-reduce.74.cloned.1.call-update) | async-done | bytes 524304 | tf_op jit(solution)/shard_map/psum | solution.py:166
  1855.1 91.7 %while.590 = (s32[]{:T(128)}, f32[12,64,128]{2,1,0:T(8,128)}, f32[2,256,12,64]{1,0,3,2:T(2,128)}, pred[2,256,256,12]{2,1,3,0:T(32,128)(4,1)}, f32[2,256,256,12]{...) while((s32[]{:T(128)}, f32[12,64,128]{2,1,0:T(8,128)}, ...), condition=%wide.region_149.151_spmd.clone, body=%wide.region_144.150_spmd.clone.sunk | while | flops 1318105600 | bytes 49264648 | solution.py:133
  1874.6 16.7 dynamic_update_slice.1280
  1920.4 16.7 dynamic_update_slice.1280
  1964.5 17.7 while.586
  2028.5 152.4 %while.601 = (s32[]{:T(128)}, f32[12,64,128]{2,1,0:T(8,128)S(1)}, f32[2,256,12,64]{1,0,3,2:T(2,128)}, f32[2,256,128]{2,1,0:T(8,128)}, f32[2,256,128]{2,1,0:T(8,1...) while((s32[]{:T(128)}, f32[12,64,128]{2,1,0:T(8,128)S(1)}, ...), condition=%wide.region_162.164_spmd.clone, body=%wide.region_152.163_spmd.clone.sunk | while | flops 2628676608 | bytes 46478592 | solution.py:133
  2078.0 16.7 dynamic_update_slice.1300
  2199.3 90.0 %while.587 = (s32[]{:T(128)}, f32[12,64,128]{2,1,0:T(8,128)}, f32[2,256,12,64]{1,0,3,2:T(2,128)}, f32[2,256,128]{2,1,0:T(8,128)}, f32[2,256,12]{2,1,0:T(8,128)},...) while((s32[]{:T(128)}, f32[12,64,128]{2,1,0:T(8,128)}, ...), condition=%wide.region_176.178_spmd, body=%wide.region_171.177_spmd.sunk | while | flops 605276288 | bytes 18716204 | solution.py:149
  2224.4 16.7 dynamic_update_slice.1237
  2269.4 16.7 dynamic_update_slice.1237
  2305.4 24.8 all-reduce.78.cloned.1.call-done
  2383.8 198.7 %all-reduce.80.cloned.1.call-done = (f32[512,1536]{1,0:T(8,128)}, f32[512,1536]{1,0:T(8,128)}) async-done(((f32[512,1536]{1,0:T(8,128)}, f32[512,1536]{1,0:T(8,128)}), (f32[512,1536]{1,0:T(8,128)}, f32[512,1536]{1,0:T(8,128)})) %all-reduce.80.cloned.1.call-update) | async-done | bytes 6291472 | tf_op jit(solution)/shard_map/psum | solution.py:466
  2590.0 17.5 all-reduce.56
  2627.2 53.4 %reduce-scatter.5.cloned.1.call-done = f32[384,2,768]{2,0,1:T(8,128)} async-done(((f32[1536,2,768]{2,0,1:T(8,128)}), f32[384,2,768]{2,0,1:T(8,128)}) %reduce-scatter.5.cloned.1.call-update) | async-done | bytes 2359312 | tf_op jit(solution)/shard_map/reduce_scatter | solution.py:517
  2685.5 29.9 %reduce-scatter.7.cloned.1.call-done = f32[384,256]{1,0:T(8,128)} async-done(((f32[1536,256]{1,0:T(8,128)}), f32[384,256]{1,0:T(8,128)}) %reduce-scatter.7.cloned.1.call-update) | async-done | bytes 393232 | tf_op jit(solution)/shard_map/reduce_scatter | solution.py:518
  2715.4 60.8 %reduce-scatter.11.cloned.1.call-done = f32[384,768]{1,0:T(8,128)} async-done(((f32[1536,768]{1,0:T(8,128)}), f32[384,768]{1,0:T(8,128)}) %reduce-scatter.11.cloned.1.call-update) | async-done | bytes 1179664 | tf_op jit(solution)/shard_map/reduce_scatter | solution.py:520
  (2918 shorter events, 1725.4 us)
Async XLA Ops:
  7.2 77.9 %all-gather.19.cloned.1.call-start = ((), (), s32[]{:S(2)}) async-start(), calls=%async_computation.15 | async-start | bytes 7077888 | tf_op jit(solution)/shard_map/all_gather | solution.py:234
  10.6 204.9 %all-gather.21.cloned.1.call-start = ((), (), s32[]{:S(2)}) async-start(), calls=%async_computation.16 | async-start | bytes 3538944 | tf_op jit(solution)/shard_map/all_gather | solution.py:237
  11.4 327.7 %all-reduce.66.cloned.1.call-start = ((), (), s32[]{:S(2)}) async-start(), calls=%async_computation.4 | async-start | bytes 6291456 | tf_op jit(solution)/shard_map/psum | solution.py:466
  44.4 623.9 %copy-start.167 = (f32[1536]{0:T(1024)}, f32[1536]{0:T(1024)S(1)}, u32[]{:S(2)}) copy-start(f32[1536]{0:T(1024)S(1)} %reduce.62) | copy-start | bytes 18436
  55.4 594.6 %copy-start.216 = (f32[1,1024]{1,0:T(1,128)}, f32[1,1024]{1,0:T(1,128)S(1)}, u32[]{:S(2)}) copy-start(f32[1,1024]{1,0:T(1,128)S(1)} %get-tuple-element.10027) | copy-start | bytes 12292
  91.7 5.0 collective-permute-start
  95.4 402.5 %copy-start.205 = (f32[768]{0:T(1024)}, f32[768]{0:T(1024)S(1)}, u32[]{:S(2)}) copy-start(f32[768]{0:T(1024)S(1)} %mul.3013) | copy-start | bytes 9220
  95.4 120.2 %copy-start.245 = (f32[768]{0:T(1024)}, f32[768]{0:T(1024)S(1)}, u32[]{:S(2)}) copy-start(f32[768]{0:T(1024)S(1)} %reduce.65) | copy-start | bytes 9220
  220.8 118.3 %copy-start.16 = (bf16[2,512,1536]{2,1,0:T(8,128)(2,1)S(1)}, bf16[2,512,1536]{2,1,0:T(8,128)(2,1)}, u32[]{:S(2)}) copy-start(bf16[2,512,1536]{2,1,0:T(8,128)(2,1)} %param.65) | copy-start | bytes 9437188
  220.8 415.3 %all-reduce.68.cloned.1.call-start = ((), (), s32[]{:S(2)}) async-start(), calls=%async_computation.5 | async-start | bytes 6291456 | tf_op jit(solution)/shard_map/psum | solution.py:466
  343.1 12.3 collective-permute-start.1
  365.3 5.9 collective-permute-start.2
  373.8 276.2 %copy-start.6 = (f32[515,1024]{1,0:T(8,128)}, f32[515,1024]{1,0:T(8,128)S(1)}, u32[]{:S(2)}) copy-start(f32[515,1024]{1,0:T(8,128)S(1)} %get-tuple-element.9979) | copy-start | bytes 6328324
  517.7 766.0 %all-reduce.70.cloned.1.call-start = ((), (), s32[]{:S(2)}) async-start(), calls=%async_computation.6 | async-start | bytes 1048576 | tf_op jit(solution)/shard_map/psum | solution.py:166
  521.2 123.7 %copy-start.390 = (f32[3]{0:T(128)S(1)}, f32[3]{0:T(128)}, u32[]{:S(2)}) copy-start(f32[3]{0:T(128)} %copy-done.389) | copy-start | bytes 40
  521.2 123.7 %copy-start.394 = (f32[3]{0:T(128)S(1)}, f32[3]{0:T(128)}, u32[]{:S(2)}) copy-start(f32[3]{0:T(128)} %get-tuple-element.9851) | copy-start | bytes 40
  521.2 124.5 %copy-start.267 = (s32[2,256]{1,0:T(2,128)S(1)}, s32[2,256]{1,0:T(2,128)}, u32[]{:S(2)}) copy-start(s32[2,256]{1,0:T(2,128)} %copy-done.266) | copy-start | bytes 6148
  521.2 127.9 %copy-start.215 = (f32[512,12]{0,1:T(8,128)S(1)}, f32[512,12]{0,1:T(8,128)}, u32[]{:S(2)}) copy-start(f32[512,12]{0,1:T(8,128)} %get-tuple-element.9868) | copy-start | bytes 73732
  521.2 128.8 %copy-start.261 = (f32[512,12]{0,1:T(8,128)S(1)}, f32[512,12]{0,1:T(8,128)}, u32[]{:S(2)}) copy-start(f32[512,12]{0,1:T(8,128)} %get-tuple-element.9867) | copy-start | bytes 73732
  521.2 128.8 %copy-start.223 = (f32[1,1024]{1,0:T(1,128)S(1)}, f32[1,1024]{1,0:T(1,128)}, u32[]{:S(2)}) copy-start(f32[1,1024]{1,0:T(1,128)} %copy-done.221) | copy-start | bytes 12292
  521.2 128.8 %copy-start.229 = (f32[1,1024]{1,0:T(1,128)S(1)}, f32[1,1024]{1,0:T(1,128)}, u32[]{:S(2)}) copy-start(f32[1,1024]{1,0:T(1,128)} %copy-done.227) | copy-start | bytes 12292
  521.2 128.8 %copy-start.235 = (f32[1,1024]{1,0:T(1,128)S(1)}, f32[1,1024]{1,0:T(1,128)}, u32[]{:S(2)}) copy-start(f32[1,1024]{1,0:T(1,128)} %copy-done.233) | copy-start | bytes 12292
  521.2 128.8 %copy-start.241 = (f32[1024]{0:T(1024)S(1)}, f32[1024]{0:T(1024)}, u32[]{:S(2)}) copy-start(f32[1024]{0:T(1024)} %copy-done.239) | copy-start | bytes 12292
  641.3 22.0 collective-permute-start.3
  675.0 4.8 collective-permute-start.4
  1158.8 83.3 %copy-start.361 = (f32[1,12]{1,0:T(1,128)S(1)}, f32[1,12]{1,0:T(1,128)}, u32[]{:S(2)}) copy-start(f32[1,12]{1,0:T(1,128)} %param.76) | copy-start | bytes 148
  1158.8 83.3 %copy-start.367 = (f32[12]{0:T(128)S(1)}, f32[12]{0:T(128)}, u32[]{:S(2)}) copy-start(f32[12]{0:T(128)} %copy-done.364) | copy-start | bytes 148
  1247.1 189.8 %all-reduce.72.cloned.1.call-start = ((), (), s32[]{:S(2)}) async-start(), calls=%async_computation.7 | async-start | bytes 6291456 | tf_op jit(solution)/shard_map/psum | solution.py:357
  1293.3 11.5 collective-permute-start.5
  1314.5 485.2 %all-reduce.74.cloned.1.call-start = ((), (), s32[]{:S(2)}) async-start(), calls=%async_computation.8 | async-start | bytes 1048576 | tf_op jit(solution)/shard_map/psum | solution.py:166
  1342.3 94.6 %copy-start.168 = (f32[1536]{0:T(1024)S(1)}, f32[1536]{0:T(1024)}, u32[]{:S(2)}) copy-start(f32[1536]{0:T(1024)} %copy-done.167) | copy-start | bytes 18436
  1446.3 28.4 %collective-permute-start.6 = (f32[512,1536]{1,0:T(8,128)}, f32[512,1536]{1,0:T(8,128)}, u32[]{:S(2)}, u32[]{:S(2)}) collective-permute-start(f32[512,1536]{1,0:T(8,128)} %fusion.590), channel_id=1, source_target_pairs={{16,0},{17,1},{18,2},{19,3},{20,4},{21,5},{22,6},{23,7},{24,8},{25... | collective-permute-start | bytes 9437192 | tf_op jit(solution)/shard_map/ppermute | solution.py:20
  1511.0 163.3 %copy-start.8 = (f32[12,64,128]{2,1,0:T(8,128)S(1)}, f32[12,64,128]{2,1,0:T(8,128)}, u32[]{:S(2)}) copy-start(f32[12,64,128]{2,1,0:T(8,128)} %custom-call.9) | copy-start | bytes 1179652
  1679.7 79.7 %copy-start.368 = (f32[12]{0:T(128)S(1)}, f32[12]{0:T(128)}, u32[]{:S(2)}) copy-start(f32[12]{0:T(128)} %copy-done.364) | copy-start | bytes 148
  1762.9 186.9 %all-reduce.76.cloned.1.call-start = ((), (), s32[]{:S(2)}) async-start(), calls=%async_computation.9 | async-start | bytes 6291456 | tf_op jit(solution)/shard_map/psum | solution.py:357
  1809.7 6.3 collective-permute-start.7
  1827.4 502.9 %all-reduce.78.cloned.1.call-start = ((), (), s32[]{:S(2)}) async-start(), calls=%async_computation.10 | async-start | bytes 1048576 | tf_op jit(solution)/shard_map/psum | solution.py:166
  1855.1 94.6 %copy-start.169 = (f32[1536]{0:T(1024)S(1)}, f32[1536]{0:T(1024)}, u32[]{:S(2)}) copy-start(f32[1536]{0:T(1024)} %copy-done.167) | copy-start | bytes 18436
  1959.2 33.1 %collective-permute-start.8 = (f32[512,1536]{1,0:T(8,128)}, f32[512,1536]{1,0:T(8,128)}, u32[]{:S(2)}, u32[]{:S(2)}) collective-permute-start(f32[512,1536]{1,0:T(8,128)} %multiply_subtract_fusion.1), channel_id=1, source_target_pairs={{16,0},{17,1},{18,2},{19,3},{20,4},{21,5},{22,6},{23,7},{24,8},{25... | collective-permute-start | bytes 9437192 | tf_op jit(solution)/shard_map/ppermute | solution.py:20
  2293.4 88.9 %reduce-scatter.9.cloned.1.call-start = ((), (), s32[]{:S(2)}) async-start(), calls=%async_computation.13 | async-start | bytes 122880 | tf_op jit(solution)/shard_map/reduce_scatter | solution.py:519
  2301.4 281.1 %all-reduce.80.cloned.1.call-start = ((), (), s32[]{:S(2)}) async-start(), calls=%async_computation.17 | async-start | bytes 12582912 | tf_op jit(solution)/shard_map/psum | solution.py:466
  2336.4 5.9 collective-permute-start.9
  2349.9 330.7 %reduce-scatter.5.cloned.1.call-start = ((), (), s32[]{:S(2)}) async-start(), calls=%async_computation.11 | async-start | bytes 11796480 | tf_op jit(solution)/shard_map/reduce_scatter | solution.py:517
  2365.6 349.8 %reduce-scatter.7.cloned.1.call-start = ((), (), s32[]{:S(2)}) async-start(), calls=%async_computation.12 | async-start | bytes 1966080 | tf_op jit(solution)/shard_map/reduce_scatter | solution.py:518
  2371.9 404.3 %reduce-scatter.11.cloned.1.call-start = ((), (), s32[]{:S(2)}) async-start(), calls=%async_computation.14 | async-start | bytes 5898240 | tf_op jit(solution)/shard_map/reduce_scatter | solution.py:520
  2380.9 201.5 %copy-start.12 = (f32[512,1536]{1,0:T(8,128)S(1)}, f32[512,1536]{1,0:T(8,128)}, u32[]{:S(2)}) copy-start(f32[512,1536]{1,0:T(8,128)} %copy-done.10) | copy-start | bytes 9437188
  2381.0 201.5 %copy-start.170 = (f32[1536]{0:T(1024)S(1)}, f32[1536]{0:T(1024)}, u32[]{:S(2)}) copy-start(f32[1536]{0:T(1024)} %copy-done.167) | copy-start | bytes 18436
  2381.0 201.5 %copy-start.332 = (f32[512]{0:T(512)S(1)}, f32[512]{0:T(512)}, u32[]{:S(2)}) copy-start(f32[512]{0:T(512)} %get-tuple-element.10063) | copy-start | bytes 6148
  (532 other events, 3841.7 us)
Sparse Core Ops, SparseCore 0:
  10.7 74.2 all-gather.18
  86.6 36.0 all-gather.20
  221.0 118.0 all-reduce.65
  517.8 118.3 all-reduce.67
  1247.2 36.3 all-reduce.69
  1314.6 122.2 all-reduce.71
  1763.0 36.6 all-reduce.73
  1827.5 122.2 all-reduce.75
  2293.5 36.6 all-reduce.77
  2332.8 23.2 reduce-scatter.8
  2359.2 223.2 all-reduce.79
  2585.7 94.8 reduce-scatter.4
  2684.4 30.9 reduce-scatter.6
  2719.1 57.0 reduce-scatter.10
where the time goes:
time: 2830 us; the launch traced here: 2780 us
  local copies, waits for them, and re-layouts  1020 us (36%)
  waiting for transfers between devices  685 us (24%)
  other arithmetic  445 us (16%)
  matrix products  383 us (14%)
  blocking collectives  184 us (7%)
    dynamic_update_slice x126, local copies, waits for them, and re-layouts, scan_spans(): state_out, outputs = lax.scan(span_step, state_in, pieces)  465 us
    psum x3, waiting for transfers between devices, shards(): branch = lax.psum(partial_out, 'tensor')  432 us
    another operation x386, local copies, waits for them, and re-layouts  164 us
    dot_general x24, matrix products, span_step(): output = jnp.einsum('tsh,shp->thp', mixing, values, precision=HIGH)  119 us
    dynamic_slice x90, local copies, waits for them, and re-layouts, states_only(): state_out, rates = lax.scan(state_step, state_in, pieces)  85.2 us
    another operation x198, other arithmetic  77.9 us
    unnamed x702, local copies, waits for them, and re-layouts  77.3 us
    all_gather x9, blocking collectives, carried_in(): everything = jax.tree.map(lambda part: lax.all_gather(part, axis), array)  73.4 us
  transfers between devices with their start and end apart: 24, of which 14 were waited for; matrix products, arithmetic and copies ran while one was open for 20% of the time, Pallas kernels for 0%

commit v1 on v0

v1 whole, which is shorter than its diff:
```python
import functools

import jax
import jax.numpy as jnp
import numpy as np
from jax import lax
from jax.experimental import pallas as pl
from jax.experimental.pallas import tpu as pltpu
from jax.sharding import PartitionSpec as P

HEAD_DIM = 64
NSTATE = 128
CONV = 4
SPAN = 128
INNER = 3072
LANES = 128
EPS = 1e-05
BREAK = 128.0
HIGH = lax.Precision.HIGHEST
F32 = jnp.float32
BF16 = jnp.bfloat16
VMEM_BYTES = 24 * 1024 * 1024

NT = (((1,), (1,)), ((), ()))
TN = (((0,), (0,)), ((), ()))


def mm(a, b, dims=(((1,), (0,)), ((), ()))):
    return lax.dot_general(a, b, dims, preferred_element_type=F32)


def exact(a, b):
    return lax.dot_general(a, b, (((1,), (0,)), ((), ())), precision=HIGH, preferred_element_type=F32)


def halves(a):
    top = a.astype(BF16)
    return top, (a - top.astype(F32)).astype(BF16)


def spread(a, spread_matrix):
    top, rest = halves(a)
    return mm(jnp.concatenate([top, rest], axis=1), spread_matrix)


def gather_heads(a, gather_matrix):
    top, rest = halves(a)
    return mm(jnp.concatenate([top, rest], axis=1), gather_matrix)


def logistic(v):
    return 0.5 * jnp.tanh(0.5 * v) + 0.5


def softplus(v):
    u = jnp.exp(-jnp.abs(v))
    small = u * (1.0 - u * (0.5 - u * (1.0 / 3.0)))
    return jnp.maximum(v, 0.0) + jnp.where(u < 1e-3, small, jnp.log(1.0 + u))


def lower_ones(rows):
    t = lax.broadcasted_iota(jnp.int32, (rows, rows), 0)
    s = lax.broadcasted_iota(jnp.int32, (rows, rows), 1)
    return t >= s


def pair_masks():
    lane = lax.broadcasted_iota(jnp.int32, (1, LANES), 1)
    first = (lane < HEAD_DIM).astype(BF16)
    return first, (1.0 - first.astype(F32)).astype(BF16)


def both_halves(a):
    top, rest = halves(a)
    return jnp.concatenate([top, rest], axis=1)


def triple(a, b):
    a_top, a_rest = halves(a)
    b_top, b_rest = halves(b)
    return (
        jnp.concatenate([a_top, a_rest, a_top], axis=1),
        jnp.concatenate([b_top, b_top, b_rest], axis=1),
    )


def twice(a):
    return jnp.concatenate([a, a], axis=0)


def chunk_of(rows, width, reverse=0):
    if reverse:
        return pl.BlockSpec((rows, width), lambda c: (reverse - 1 - c, 0))
    return pl.BlockSpec((rows, width), lambda c: (c, 0))


def lanes_of(rows, reverse=0):
    if reverse:
        return pl.BlockSpec((8, rows), lambda c: (0, reverse - 1 - c))
    return pl.BlockSpec((8, rows), lambda c: (0, c))


def stack_of(rows, width, reverse=0):
    if reverse:
        return pl.BlockSpec((1, rows, width), lambda c: (reverse - 1 - c, 0, 0))
    return pl.BlockSpec((1, rows, width), lambda c: (c, 0, 0))


def whole_of(rows, width):
    return pl.BlockSpec((rows, width), lambda c: (0, 0))


def scalars_of():
    return pl.BlockSpec(memory_space=pltpu.SMEM)


def anywhere(count):
    return [pl.BlockSpec(memory_space=pl.ANY)] * count


def params_of():
    return pltpu.CompilerParams(dimension_semantics=("arbitrary",), vmem_limit_bytes=VMEM_BYTES)


def shape(*dims, dtype=F32):
    return jax.ShapeDtypeStruct(dims, dtype)


def cost(flops, moved):
    return pl.CostEstimate(flops=int(flops), bytes_accessed=int(moved), transcendentals=0)


def weight_copies(where_ref, refs, buffer, sems):
    first, core = where_ref[1], where_ref[2]
    rows = buffer.shape[0] // 2
    width = buffer.shape[1]
    near_at = pl.ds(pl.multiple_of((1 - first) * rows, rows), rows)
    far = first * rows
    step = rows // 2
    *near, far_mine, far_other = refs
    pairs = []
    column = 0
    for (start, size), held, other in near:
        part = buffer.at[near_at, column : column + size]
        sem = sems.at[len(pairs)]
        pairs.append(
            (
                pltpu.make_async_copy(held.at[:, start : start + size], part, sem),
                pltpu.make_async_copy(other.at[:, start : start + size], part, sem),
            )
        )
        column += size
    for ref, which in ((far_mine, core), (far_other, 1 - core)):
        part = buffer.at[pl.ds(pl.multiple_of(far + which * step, step), step)]
        copy = pltpu.make_async_copy(ref, part, sems.at[len(pairs)])
        pairs.append((copy, copy))
    return pairs


def start_weights(where_ref, refs, buffer, sems):
    pairs = weight_copies(where_ref, refs, buffer, sems)

    @pl.when(where_ref[0] == 1)
    def _():
        for held, _ in pairs:
            held.start()

    @pl.when(where_ref[0] == 0)
    def _():
        for _, other in pairs:
            other.start()


def wait_weights(where_ref, refs, buffer, sems):
    for held, _ in weight_copies(where_ref, refs, buffer, sems):
        held.wait()


def load_weights(where_ref, refs, buffer, sems):
    start_weights(where_ref, refs, buffer, sems)
    wait_weights(where_ref, refs, buffer, sems)


def front_refs(refs):
    main, main_other, rest, rest_other, mine, other = refs
    width = main.shape[1] // 2
    return ((width, width), main, main_other), ((0, rest.shape[1]), rest, rest_other), mine, other


def gate_refs(refs):
    main, main_other, mine, other = refs
    return ((0, main.shape[1] // 2), main, main_other), mine, other


def out_refs(refs):
    held, held_other, mine, other = refs
    return ((0, held.shape[1]), held, held_other), mine, other


def weight_scratch(weights):
    rows, width = weights[-1].shape
    return [pltpu.VMEM((4 * rows, width), BF16), pltpu.SemaphoreType.DMA((4,))]


TAPS, BIAS, SKIP, GATED, NORM, STEP, DECAY, PACK = 0, 4, 8, 9, 10, 12, 13, 16


def pack_kernel(taps_a, taps_b, bias_a, bias_b, skip, gated, norm, step, decay, pack_ref):
    width = taps_a.shape[1]
    half = norm.shape[1] // 2
    pack_ref[...] = jnp.zeros_like(pack_ref)
    pack_ref[TAPS : TAPS + CONV, :width] = taps_a[...]
    pack_ref[TAPS : TAPS + CONV, width:] = taps_b[...]
    pack_ref[BIAS : BIAS + 1, :width] = bias_a[...]
    pack_ref[BIAS : BIAS + 1, width:] = bias_b[...]
    pack_ref[SKIP : SKIP + 1, :width] = skip[...]
    pack_ref[GATED : GATED + 1, :width] = gated[...]
    pack_ref[NORM : NORM + 1, :half] = norm[:, :half]
    pack_ref[NORM + 1 : NORM + 2, :half] = norm[:, half:]
    pack_ref[STEP : STEP + 1, :LANES] = step[...]
    pack_ref[DECAY : DECAY + 1, :LANES] = decay[...]


def norm_row(pack_ref, half):
    return jnp.concatenate([pack_ref[NORM : NORM + 1, :half], pack_ref[NORM + 1 : NORM + 2, :half]], axis=1)


def front_kernel(
    where_ref,
    x_ref,
    halo_ref,
    tok_ref,
    pack_ref,
    spread_ref,
    w0,
    w1,
    w2,
    w3,
    w4,
    w5,
    normed_ref,
    inv_ref,
    pre_ref,
    conv_x_ref,
    conv_s_ref,
    raw_ref,
    step_ref,
    cum_ref,
    entry_ref,
    rate_ref,
    end_ref,
    end_rate_ref,
    weights,
    sems,
    ext,
    cols,
    state,
    total,
):
    rows, width = conv_x_ref.shape
    length, model = x_ref.shape
    both = width + 2 * NSTATE
    chunk = pl.program_id(0)
    held = front_refs((w0, w1, w2, w3, w4, w5))

    @pl.when(chunk == 0)
    def _():
        start_weights(where_ref, held, weights, sems)
        gain = norm_row(pack_ref, model // 2)

        def normalize(v):
            inv = lax.rsqrt(jnp.mean(v * v, axis=-1, keepdims=True) + EPS)
            return (v * inv * gain).astype(BF16), inv

        for r in range(length // rows):
            at = slice(r * rows, (r + 1) * rows)
            normed, inv = normalize(x_ref[at, :].astype(F32))
            normed_ref[at, :] = normed
            inv_ref[at, :] = jnp.broadcast_to(inv, (rows, LANES))
        halo, _ = normalize(halo_ref[...].astype(F32))
        wait_weights(where_ref, held, weights, sems)
        ext[0:8, :] = mm(halo, weights[:, :both])
        cols[...] = mm(normed_ref[...], weights[...])
        state[...] = jnp.zeros_like(state)
        total[...] = jnp.ones_like(total)

    @pl.when(chunk > 0)
    def _():
        ext[0:8, :] = ext[rows : rows + 8, :]

    here = pl.ds(pl.multiple_of(chunk * rows, rows), rows)
    pre = cols[here, :both]
    raw = cols[here, both:]
    pre_ref[...] = pre
    raw_ref[...] = raw
    ext[8 : 8 + rows, :] = pre
    conv = pack_ref[BIAS : BIAS + 1, :] + pack_ref[TAPS : TAPS + 1, :] * pre
    for k in range(1, CONV):
        conv = conv + tok_ref[:, k : k + 1] * (
            pack_ref[TAPS + k : TAPS + k + 1, :] * ext[8 - k : 8 - k + rows, :]
        )
    conv_x_ref[...] = conv[:, :width]
    conv_s_ref[...] = conv[:, width:]
    conv_x = conv[:, :width]
    conv_b = conv[:, width : width + NSTATE]
    values = conv_x * logistic(conv_x)
    b_part = conv_b * logistic(conv_b)
    step = softplus(raw + pack_ref[STEP : STEP + 1, :LANES])
    decay = -jnp.exp(pack_ref[DECAY : DECAY + 1, :LANES]) * step
    cum = exact(lower_ones(rows).astype(F32), decay - BREAK * tok_ref[:, 0:1])
    step_ref[...] = step
    cum_ref[...] = cum
    last = cum[rows - 1 : rows, :]
    spread_matrix = spread_ref[...]
    carried = (spread(jnp.exp(last - cum) * step, spread_matrix) * values).astype(BF16)
    before = state[...]
    entry_ref[0] = before
    rate_ref[0] = total[...]
    kept = spread(jnp.exp(cum[rows - 8 : rows, :]), spread_matrix)[7:8, :]
    grown = mm(both_halves(b_part), carried, TN)
    new_state = kept * before + (grown[:NSTATE] + grown[NSTATE:])
    state[...] = new_state
    end_ref[...] = new_state
    new_total = total[...] * jnp.exp(last)
    total[...] = new_total
    end_rate_ref[...] = new_total


def front_call(where, x, halo, tok, pack, spread_matrix, weights):
    length, model = x.shape
    all_width = weights[-1].shape[1]
    both = all_width - LANES
    width = both - 2 * NSTATE
    rows = min(SPAN, length)
    chunks = length // rows
    return pl.pallas_call(
        front_kernel,
        grid=(chunks,),
        in_specs=[
            scalars_of(),
            whole_of(length, model),
            whole_of(8, model),
            chunk_of(rows, LANES),
            whole_of(PACK, both),
            whole_of(2 * LANES, width),
        ]
        + anywhere(6),
        out_specs=[
            whole_of(length, model),
            whole_of(length, LANES),
            chunk_of(rows, both),
            chunk_of(rows, width),
            chunk_of(rows, 2 * NSTATE),
            chunk_of(rows, LANES),
            chunk_of(rows, LANES),
            chunk_of(rows, LANES),
            stack_of(NSTATE, width),
            stack_of(8, LANES),
            whole_of(NSTATE, width),
            whole_of(8, LANES),
        ],
        out_shape=[
            shape(length, model, dtype=BF16),
            shape(length, LANES),
            shape(length, both),
            shape(length, width),
            shape(length, 2 * NSTATE),
            shape(length, LANES),
            shape(length, LANES),
            shape(length, LANES),
            shape(chunks, NSTATE, width),
            shape(chunks, 8, LANES),
            shape(NSTATE, width),
            shape(8, LANES),
        ],
        scratch_shapes=weight_scratch(weights)
        + [
            pltpu.VMEM((rows + 8, both), F32),
            pltpu.VMEM((length, all_width), F32),
            pltpu.VMEM((NSTATE, width), F32),
            pltpu.VMEM((8, LANES), F32),
        ],
        compiler_params=params_of(),
        cost_estimate=cost(2 * length * model * all_width, 24 * length * width),
        name="front",
    )(where, x, halo, tok, pack, spread_matrix, *weights)


def project_kernel(kind, where_ref, a_ref, w0, w1, w2, w3, out_ref, weights, sems):
    tile = out_ref.shape[1]

    @pl.when(pl.program_id(0) == 0)
    def _():
        load_weights(where_ref, kind((w0, w1, w2, w3)), weights, sems)

    at = pl.ds(pl.multiple_of(pl.program_id(0) * tile, tile), tile)
    out_ref[...] = mm(a_ref[...], weights[:, at])


def project_call(where, a, kind, weights):
    length, model = a.shape
    width = weights[-1].shape[1]
    tile = 2 * LANES
    return pl.pallas_call(
        functools.partial(project_kernel, kind),
        grid=(width // tile,),
        in_specs=[scalars_of(), whole_of(length, model)] + anywhere(4),
        out_specs=pl.BlockSpec((length, tile), lambda n: (0, n)),
        out_shape=shape(length, width),
        scratch_shapes=weight_scratch(weights),
        compiler_params=params_of(),
        cost_estimate=cost(2 * length * model * width, 4 * length * width),
        name="project",
    )(where, a, *weights)


def mix_kernel(conv_x_ref, conv_s_ref, step_ref, cum_ref, entry_ref, spread_ref, y_ref):
    rows, width = conv_x_ref.shape
    conv_x = conv_x_ref[...]
    conv_s = conv_s_ref[...]
    values = conv_x * logistic(conv_x)
    bc = conv_s * logistic(conv_s)
    b_part, c_part = bc[:, :NSTATE], bc[:, NSTATE:]
    cum = cum_ref[...]
    spread_matrix = spread_ref[...]
    grown = spread(jnp.exp(cum), spread_matrix)
    stepped = (spread(step_ref[...], spread_matrix) * values).astype(BF16)
    from_entry = grown * mm(both_halves(c_part), twice(entry_ref[0].astype(BF16)))
    scores = jnp.where(lower_ones(rows), mm(*triple(c_part, b_part), NT), 0.0)
    cum_t = cum.T
    first, second = pair_masks()
    for j in range(width // LANES):
        parts = []
        for h in (2 * j, 2 * j + 1):
            gap = jnp.minimum(cum[:, h : h + 1] - cum_t[h : h + 1, :], 0.0)
            parts.append((scores * jnp.exp(gap)).astype(BF16))
        pair = stepped[:, j * LANES : (j + 1) * LANES]
        y_ref[:, j * LANES : (j + 1) * LANES] = from_entry[:, j * LANES : (j + 1) * LANES] + mm(
            jnp.concatenate(parts, axis=1), jnp.concatenate([pair * first, pair * second], axis=0)
        )


def mix_call(conv_x, conv_s, step, cum, entry, spread_matrix):
    length, width = conv_x.shape
    rows = min(SPAN, length)
    return pl.pallas_call(
        mix_kernel,
        grid=(length // rows,),
        in_specs=[
            chunk_of(rows, width),
            chunk_of(rows, 2 * NSTATE),
            chunk_of(rows, LANES),
            chunk_of(rows, LANES),
            stack_of(NSTATE, width),
            whole_of(2 * LANES, width),
        ],
        out_specs=chunk_of(rows, width),
        out_shape=shape(length, width),
        compiler_params=params_of(),
        cost_estimate=cost(16 * length * rows * width, 12 * length * width),
        name="mix",
    )(conv_x, conv_s, step, cum, entry, spread_matrix)


def gate_kernel(
    with_dot,
    y_ref,
    z_ref,
    conv_x_ref,
    conv_s_ref,
    cum_ref,
    rate_ref,
    entry_ref,
    pack_ref,
    spread_ref,
    *refs,
):
    comb_ref, gated_ref, sums_ref = refs[-3:]
    rows, width = y_ref.shape
    spread_matrix = spread_ref[...]
    c_part = conv_s_ref[:, NSTATE:]
    c_part = c_part * logistic(c_part)
    reach = spread(rate_ref[0], spread_matrix)[0:1, :]
    grown = spread(jnp.exp(cum_ref[...]), spread_matrix)
    mixed = y_ref[...] + grown * mm(
        both_halves(c_part), twice((reach * entry_ref[...]).astype(BF16))
    )
    conv = conv_x_ref[...]
    comb = mixed + pack_ref[SKIP : SKIP + 1, :width] * (conv * logistic(conv))
    comb_ref[...] = comb
    z = z_ref[...]
    gated = comb * (z * logistic(z))
    gated_ref[...] = gated
    square = jnp.sum(gated * gated, axis=1, keepdims=True)
    lane = lax.broadcasted_iota(jnp.int32, (rows, LANES), 1)
    sums = jnp.where(lane == 0, square, 0.0)
    if with_dot:
        gain = pack_ref[GATED : GATED + 1, :width]
        dot = jnp.sum(gated * gain * refs[0][...], axis=1, keepdims=True)
        sums = jnp.where(lane == 1, dot, sums)
    sums_ref[...] = sums.T[0:8, :]


def gate_call(y, z, conv_x, conv_s, cum, rate, entry, pack, spread_matrix, *grad_scaled):
    length, width = y.shape
    rows = min(SPAN, length)
    chunks = length // rows
    return pl.pallas_call(
        functools.partial(gate_kernel, bool(grad_scaled)),
        grid=(chunks,),
        in_specs=[
            chunk_of(rows, width),
            chunk_of(rows, width),
            chunk_of(rows, width),
            chunk_of(rows, 2 * NSTATE),
            chunk_of(rows, LANES),
            stack_of(8, LANES),
            whole_of(NSTATE, width),
            whole_of(*pack.shape),
            whole_of(2 * LANES, width),
        ]
        + [chunk_of(rows, width)] * len(grad_scaled),
        out_specs=[chunk_of(rows, width), chunk_of(rows, width), lanes_of(rows)],
        out_shape=[shape(length, width), shape(length, width), shape(8, length)],
        compiler_params=params_of(),
        cost_estimate=cost(4 * length * NSTATE * width, 28 * length * width),
        name="gate",
    )(y, z, conv_x, conv_s, cum, rate, entry, pack, spread_matrix, *grad_scaled)


def columns(lanes):
    rows = lanes.shape[1]
    return jnp.concatenate([lanes, jnp.zeros((LANES - 8, rows), F32)], axis=0).T


def out_kernel(
    where_ref, gated_ref, sums_ref, pack_ref, w0, w1, w2, w3, low_ref, other_ref, branch_ref, weights, sems, full
):
    tile = branch_ref.shape[1]
    length, width = gated_ref.shape
    half = width // 2

    @pl.when(pl.program_id(0) == 0)
    def _():
        start_weights(where_ref, out_refs((w0, w1, w2, w3)), weights, sems)
        gain = pack_ref[GATED : GATED + 1, :width]
        rows = min(SPAN, length)
        for r in range(length // rows):
            at = slice(r * rows, (r + 1) * rows)
            inv = lax.rsqrt(columns(sums_ref[:, at])[:, 0:1] * (1.0 / INNER) + EPS)
            full[at, :] = (gated_ref[at, :] * inv * gain).astype(BF16)
        low_ref[...] = full[:, pl.ds(pl.multiple_of(where_ref[2] * half, LANES), half)]
        other_ref[...] = full[:, pl.ds(pl.multiple_of((1 - where_ref[2]) * half, LANES), half)]
        wait_weights(where_ref, out_refs((w0, w1, w2, w3)), weights, sems)

    at = pl.ds(pl.multiple_of(pl.program_id(0) * tile, tile), tile)
    branch_ref[...] = mm(full[...], weights[at, :], NT)


def out_call(where, gated, sums, pack, weights):
    length, width = gated.shape
    model = 4 * weights[-1].shape[0]
    tile = model // 4
    half = width // 2
    return pl.pallas_call(
        out_kernel,
        grid=(model // tile,),
        in_specs=[scalars_of(), whole_of(length, width), whole_of(8, length), whole_of(*pack.shape)]
        + anywhere(4),
        out_specs=[
            whole_of(length, half),
            whole_of(length, half),
            pl.BlockSpec((length, tile), lambda n: (0, n)),
        ],
        out_shape=[
            shape(length, half, dtype=BF16),
            shape(length, half, dtype=BF16),
            shape(length, model),
        ],
        scratch_shapes=weight_scratch(weights) + [pltpu.VMEM((length, width), BF16)],
        compiler_params=params_of(),
        cost_estimate=cost(2 * length * model * width, 8 * length * width),
        name="out",
    )(where, gated, sums, pack, *weights)


def finish_kernel(last, where_ref, grad_ref, g_ref, x_ref, inv_ref, pack_ref, *refs):
    rows, model = grad_ref.shape
    chunk = pl.program_id(0)
    gain = norm_row(pack_ref, model // 2)
    x = x_ref[...].astype(F32)
    inv = inv_ref[:, 0:1]
    weighted = grad_ref[...].astype(F32) * gain
    mean = jnp.mean(weighted * x, axis=-1, keepdims=True)
    result = g_ref[...].astype(F32) + inv * weighted - x * (inv * inv * inv * mean)
    if last:
        refs[0][...] = result
        return
    branch_ref, sums_ref, w0, w1, w2, w3, out_ref, low_ref, scaled_ref, new_sums_ref, weights, sems = refs
    candidates = out_refs((w0, w1, w2, w3))

    @pl.when(chunk == 0)
    def _():
        start_weights(where_ref, candidates, weights, sems)

    out_ref[...] = result
    low = result.astype(BF16)
    low_ref[pl.ds(pl.multiple_of(chunk * rows, rows), rows), :] = low
    dot = jnp.sum(low.astype(F32) * branch_ref[...], axis=1, keepdims=True)
    square = columns(sums_ref[...])[:, 0:1]
    dot = dot / lax.rsqrt(square * (1.0 / INNER) + EPS)
    lane = lax.broadcasted_iota(jnp.int32, (rows, LANES), 1)
    sums = jnp.where(lane == 0, square, jnp.where(lane == 1, dot, 0.0))
    new_sums_ref[...] = sums.T[0:8, :]

    @pl.when(chunk == pl.num_programs(0) - 1)
    def _():
        wait_weights(where_ref, candidates, weights, sems)
        scaled_ref[...] = mm(low_ref[...], weights[...])


def finish_call(where, grad, g, x, inv, pack, *more):
    length, model = grad.shape
    rows = min(SPAN, length)
    last = not more
    in_specs = [
        scalars_of(),
        chunk_of(rows, model),
        chunk_of(rows, model),
        chunk_of(rows, model),
        chunk_of(rows, LANES),
        whole_of(*pack.shape),
    ]
    out_specs = [chunk_of(rows, model)]
    out_shape = [shape(length, model)]
    scratch = []
    if more:
        branch, sums, *weights = more
        width = weights[-1].shape[1]
        in_specs += [chunk_of(rows, model), lanes_of(rows)] + anywhere(4)
        out_specs += [whole_of(length, model), whole_of(length, width), lanes_of(rows)]
        out_shape += [shape(length, model, dtype=BF16), shape(length, width), shape(8, length)]
        scratch = weight_scratch(weights)
    return pl.pallas_call(
        functools.partial(finish_kernel, last),
        grid=(length // rows,),
        in_specs=in_specs,
        out_specs=out_specs,
        out_shape=out_shape,
        scratch_shapes=scratch,
        compiler_params=params_of(),
        cost_estimate=cost(length * model * 800, 16 * length * model),
        name="finish",
    )(where, grad, g, x, inv, pack, *more)


def gate_back_kernel(
    scaled_ref,
    comb_ref,
    z_ref,
    conv_s_ref,
    cum_ref,
    sums_ref,
    pack_ref,
    spread_ref,
    dmix_ref,
    dz_ref,
    adj_ref,
    rate_ref,
    begin_ref,
    gain_ref,
    state,
    total,
):
    chunk = pl.program_id(0)
    rows, width = z_ref.shape

    @pl.when(chunk == 0)
    def _():
        state[...] = jnp.zeros_like(state)
        total[...] = jnp.ones_like(total)
        gain_ref[...] = jnp.zeros_like(gain_ref)

    sums = columns(sums_ref[...])
    inv = lax.rsqrt(sums[:, 0:1] * (1.0 / INNER) + EPS)
    dot = sums[:, 1:2]
    grad_scaled = scaled_ref[...]
    comb = comb_ref[...]
    z = z_ref[...]
    sig = logistic(z)
    act = z * sig
    gated = comb * act
    gain_ref[0:1, :] += jnp.sum(grad_scaled * (gated * inv), axis=0, keepdims=True)
    grad_gated = inv * (grad_scaled * pack_ref[GATED : GATED + 1, :width]) - gated * (inv * inv * inv * dot * (1.0 / INNER))
    dmix = grad_gated * act
    dmix_ref[...] = dmix
    dz_ref[...] = (grad_gated * comb * (sig * (1.0 + z * (1.0 - sig)))).astype(BF16)
    c_part = conv_s_ref[:, NSTATE:]
    c_part = c_part * logistic(c_part)
    cum = cum_ref[...]
    grown = spread(jnp.exp(cum), spread_ref[...])
    held = state[...]
    adj_ref[0] = held
    rate_ref[0] = total[...]
    added = mm(both_halves(c_part), (grown * dmix).astype(BF16), TN)
    new_state = grown[rows - 1 : rows, :] * held + (added[:NSTATE] + added[NSTATE:])
    state[...] = new_state
    begin_ref[...] = new_state
    total[...] = total[...] * jnp.exp(cum[rows - 1 : rows, :])


def gate_back_call(grad_scaled, comb, z, conv_s, cum, sums, pack, spread_matrix):
    length, width = z.shape
    rows = min(SPAN, length)
    chunks = length // rows
    return pl.pallas_call(
        gate_back_kernel,
        grid=(chunks,),
        in_specs=[
            chunk_of(rows, width, chunks),
            chunk_of(rows, width, chunks),
            chunk_of(rows, width, chunks),
            chunk_of(rows, 2 * NSTATE, chunks),
            chunk_of(rows, LANES, chunks),
            lanes_of(rows, chunks),
            whole_of(*pack.shape),
            whole_of(2 * LANES, width),
        ],
        out_specs=[
            chunk_of(rows, width, chunks),
            chunk_of(rows, width, chunks),
            stack_of(NSTATE, width, chunks),
            stack_of(8, LANES, chunks),
            whole_of(NSTATE, width),
            whole_of(8, width),
        ],
        out_shape=[
            shape(length, width),
            shape(length, width, dtype=BF16),
            shape(chunks, NSTATE, width),
            shape(chunks, 8, LANES),
            shape(NSTATE, width),
            shape(8, width),
        ],
        scratch_shapes=[pltpu.VMEM((NSTATE, width), F32), pltpu.VMEM((8, LANES), F32)],
        compiler_params=params_of(),
        cost_estimate=cost(4 * length * NSTATE * width, 28 * length * width),
        name="gate_back",
    )(grad_scaled, comb, z, conv_s, cum, sums, pack, spread_matrix)


def mix_back_kernel(
    conv_x_ref,
    conv_s_ref,
    dmix_ref,
    step_ref,
    cum_ref,
    entry_ref,
    entry_rate_ref,
    entry_in_ref,
    adj_ref,
    spread_ref,
    gather_ref,
    ones_ref,
    grad_step_ref,
    grad_b_ref,
    grad_c_ref,
    decay_ref,
    skip_ref,
    flows,
):
    chunk = pl.program_id(0)
    rows, width = conv_x_ref.shape

    @pl.when(chunk == 0)
    def _():
        skip_ref[...] = jnp.zeros_like(skip_ref)

    spread_matrix = spread_ref[...]
    gather_matrix = gather_ref[...]
    conv = conv_x_ref[...]
    values = conv * logistic(conv)
    conv_s = conv_s_ref[...]
    bc = conv_s * logistic(conv_s)
    b_part, c_part = bc[:, :NSTATE], bc[:, NSTATE:]
    cum = cum_ref[...]
    dmix = dmix_ref[...]
    dmix_low = dmix.astype(BF16)
    last = cum[rows - 1 : rows, :]
    grown = spread(jnp.exp(cum), spread_matrix)
    left_wide = spread(jnp.exp(last - cum), spread_matrix)
    entry = entry_ref[0] + spread(entry_rate_ref[0], spread_matrix)[0:1, :] * entry_in_ref[...]
    adj = adj_ref[0]
    entry_low = entry.astype(BF16)
    adj_low = adj.astype(BF16)
    skip_ref[0:1, :] += jnp.sum(dmix * values, axis=0, keepdims=True)

    stepped = spread(step_ref[...], spread_matrix) * values
    stepped_low = stepped.astype(BF16)
    from_entry = grown * mm(both_halves(c_part), twice(entry_low))
    later = left_wide * mm(both_halves(b_part), twice(adj_low))
    grad_c = mm((grown * dmix).astype(BF16), entry_low, NT)
    grad_b = mm((left_wide * stepped).astype(BF16), adj_low, NT)

    t_after = lower_ones(rows).T
    scores = jnp.where(t_after, mm(*triple(b_part, c_part), NT), 0.0)
    cum_t = cum.T
    first, second = pair_masks()
    grad_scores = jnp.zeros((rows, rows), F32)
    for j in range(width // LANES):
        lanes = slice(j * LANES, (j + 1) * LANES)
        dmix_pair = dmix_low[:, lanes]
        stacked = jnp.concatenate([dmix_pair * first, dmix_pair * second], axis=0)
        grad_pair = mm(stepped_low[:, lanes], stacked, NT)
        parts = []
        for i in range(2):
            h = 2 * j + i
            gap = jnp.minimum(cum_t[h : h + 1, :] - cum[:, h : h + 1], 0.0)
            reach = jnp.exp(gap)
            mixing = scores * reach
            grad_mixing = grad_pair[:, i * rows : (i + 1) * rows]
            grad_scores = grad_scores + grad_mixing * reach
            flows[:, h * rows : (h + 1) * rows] = (grad_mixing * mixing).astype(BF16)
            parts.append(mixing.astype(BF16))
        grad_step_ref[:, lanes] = later[:, lanes] + mm(jnp.concatenate(parts, axis=1), stacked)
    grad_scores = jnp.where(t_after, grad_scores, 0.0)
    s_top, s_rest = halves(grad_scores)
    c_top, c_rest = halves(c_part)
    b_top, b_rest = halves(b_part)
    grad_b_ref[...] = grad_b + mm(
        jnp.concatenate([s_top, s_rest, s_top], axis=1),
        jnp.concatenate([c_top, c_top, c_rest], axis=0),
    )
    grad_c_ref[...] = grad_c + mm(
        jnp.concatenate([s_top, s_rest, s_top], axis=0),
        jnp.concatenate([b_top, b_top, b_rest], axis=0),
        TN,
    )

    out_flow = gather_heads(dmix * from_entry, gather_matrix)
    in_flow = gather_heads(later * stepped, gather_matrix)
    kept = jnp.sum(entry * adj, axis=0, keepdims=True) * grown[rows - 1 : rows, :]
    kept = gather_heads(jnp.broadcast_to(kept, (8, width)), gather_matrix)[0:1, :]
    flow = flows[...]
    source = mm(flow, ones_ref[...])
    target = mm(jnp.ones((8, rows), BF16), flow)
    heads = width // HEAD_DIM
    target = jnp.concatenate(
        [target[0:1, h * rows : (h + 1) * rows] for h in range(heads)]
        + [jnp.zeros((LANES - heads, rows), F32)],
        axis=0,
    ).T
    after = exact(t_after.astype(F32), target - source + out_flow)
    before = exact(lower_ones(rows).astype(F32), in_flow) - in_flow
    decay_ref[...] = kept + after + before


def mix_back_call(kept, dmix, adj, consts):
    conv_x, conv_s, step, cum, _, entry, rate, entry_in = kept
    length, width = conv_x.shape
    rows = min(SPAN, length)
    chunks = length // rows
    spread_matrix, gather_matrix, ones = consts
    head_count = width // HEAD_DIM
    return pl.pallas_call(
        mix_back_kernel,
        grid=(chunks,),
        in_specs=[
            chunk_of(rows, width),
            chunk_of(rows, 2 * NSTATE),
            chunk_of(rows, width),
            chunk_of(rows, LANES),
            chunk_of(rows, LANES),
            stack_of(NSTATE, width),
            stack_of(8, LANES),
            whole_of(NSTATE, width),
            stack_of(NSTATE, width),
            whole_of(2 * LANES, width),
            whole_of(2 * width, LANES),
            whole_of(head_count * rows, LANES),
        ],
        out_specs=[
            chunk_of(rows, width),
            chunk_of(rows, NSTATE),
            chunk_of(rows, NSTATE),
            chunk_of(rows, LANES),
            whole_of(8, width),
        ],
        out_shape=[
            shape(length, width),
            shape(length, NSTATE),
            shape(length, NSTATE),
            shape(length, LANES),
            shape(8, width),
        ],
        scratch_shapes=[pltpu.VMEM((rows, head_count * rows), BF16)],
        compiler_params=params_of(),
        cost_estimate=cost(40 * length * rows * width, 20 * length * width),
        name="mix_back",
    )(conv_x, conv_s, dmix, step, cum, entry, rate, entry_in, adj, spread_matrix, gather_matrix, ones)


def later_kernel(
    conv_x_ref,
    conv_s_ref,
    dmix_ref,
    step_ref,
    cum_ref,
    raw_ref,
    entry_ref,
    entry_rate_ref,
    entry_in_ref,
    adj_rate_ref,
    adj_in_ref,
    grad_step_ref,
    grad_b_ref,
    grad_c_ref,
    decay_ref,
    pack_ref,
    spread_ref,
    gather_ref,
    grad_ref,
    grad_raw_ref,
    small_ref,
):
    chunk = pl.program_id(0)
    rows, width = conv_x_ref.shape

    @pl.when(chunk == 0)
    def _():
        small_ref[...] = jnp.zeros_like(small_ref)

    spread_matrix = spread_ref[...]
    gather_matrix = gather_ref[...]
    conv = conv_x_ref[...]
    sig = logistic(conv)
    values = conv * sig
    conv_s = conv_s_ref[...]
    sig_s = logistic(conv_s)
    b_part = conv_s[:, :NSTATE] * sig_s[:, :NSTATE]
    step = step_ref[...]
    cum = cum_ref[...]
    last = cum[rows - 1 : rows, :]
    step_wide = spread(step, spread_matrix)
    left_wide = spread(jnp.exp(last - cum), spread_matrix)
    kept = spread(jnp.exp(cum[rows - 8 : rows, :]), spread_matrix)[7:8, :]
    entry = entry_ref[0] + spread(entry_rate_ref[0], spread_matrix)[0:1, :] * entry_in_ref[...]
    adj = spread(adj_rate_ref[0], spread_matrix)[0:1, :] * adj_in_ref[...]
    adj_low = adj.astype(BF16)
    stepped = step_wide * values
    later = left_wide * mm(both_halves(b_part), twice(adj_low))
    grad_b = grad_b_ref[...] + mm((left_wide * stepped).astype(BF16), adj_low, NT)
    in_flow = gather_heads(later * stepped, gather_matrix)
    kept = jnp.sum(entry * adj, axis=0, keepdims=True) * kept
    kept = gather_heads(jnp.broadcast_to(kept, (8, width)), gather_matrix)[0:1, :]
    before = exact(lower_ones(rows).astype(F32), in_flow) - in_flow
    grad_decay = decay_ref[...] + kept + before
    grad_stepped = grad_step_ref[...] + later
    grad_step = gather_heads(grad_stepped * values, gather_matrix)
    grad_values = step_wide * grad_stepped + pack_ref[SKIP : SKIP + 1, :width] * dmix_ref[...]
    grad_ref[:, :width] = grad_values * (sig * (1.0 + conv * (1.0 - sig)))
    slope = sig_s * (1.0 + conv_s * (1.0 - sig_s))
    grad_ref[:, width : width + NSTATE] = grad_b * slope[:, :NSTATE]
    grad_ref[:, width + NSTATE :] = grad_c_ref[...] * slope[:, NSTATE:]
    rate = -jnp.exp(pack_ref[DECAY : DECAY + 1, :LANES])
    grad_raw = (grad_step + rate * grad_decay) * logistic(raw_ref[...] + pack_ref[STEP : STEP + 1, :LANES])
    grad_raw_ref[...] = grad_raw.astype(BF16)
    small_ref[0:1, :] += jnp.sum(grad_raw, axis=0, keepdims=True)
    small_ref[1:2, :] += jnp.sum(grad_decay * (rate * step), axis=0, keepdims=True)


def later_call(kept, dmix, adj_rate, adj_in, parts, pack, consts):
    conv_x, conv_s, step, cum, raw, entry, rate, entry_in = kept
    length, width = conv_x.shape
    rows = min(SPAN, length)
    chunks = length // rows
    spread_matrix, gather_matrix, _ = consts
    return pl.pallas_call(
        later_kernel,
        grid=(chunks,),
        in_specs=[
            chunk_of(rows, width),
            chunk_of(rows, 2 * NSTATE),
            chunk_of(rows, width),
            chunk_of(rows, LANES),
            chunk_of(rows, LANES),
            chunk_of(rows, LANES),
            stack_of(NSTATE, width),
            stack_of(8, LANES),
            whole_of(NSTATE, width),
            stack_of(8, LANES),
            whole_of(NSTATE, width),
            chunk_of(rows, width),
            chunk_of(rows, NSTATE),
            chunk_of(rows, NSTATE),
            chunk_of(rows, LANES),
            whole_of(*pack.shape),
            whole_of(2 * LANES, width),
            whole_of(2 * width, LANES),
        ],
        out_specs=[chunk_of(rows, width + 2 * NSTATE), chunk_of(rows, LANES), whole_of(8, LANES)],
        out_shape=[
            shape(length, width + 2 * NSTATE),
            shape(length, LANES, dtype=BF16),
            shape(8, LANES),
        ],
        compiler_params=params_of(),
        cost_estimate=cost(8 * length * NSTATE * width, 24 * length * width),
        name="later",
    )(
        conv_x,
        conv_s,
        dmix,
        step,
        cum,
        raw,
        entry,
        rate,
        entry_in,
        adj_rate,
        adj_in,
        *parts,
        pack,
        spread_matrix,
        gather_matrix,
    )


def conv_back_kernel(
    chunks,
    where_ref,
    grad_ref,
    pre_ref,
    raw_ref,
    dz_ref,
    tok_ref,
    halo_ref,
    halo_tok_ref,
    pack_ref,
    x_ref,
    inv_ref,
    head_ref,
    skip_ref,
    gained_ref,
    gather_ref,
    f0,
    f1,
    f2,
    f3,
    f4,
    f5,
    z0,
    z1,
    z2,
    z3,
    keep_ref,
    send_ref,
    part_ref,
    small_ref,
    front,
    front_sems,
    gate,
    gate_sems,
    ext,
    ext_tok,
    grads,
):
    step = pl.program_id(0)
    rows, both = pre_ref.shape
    width = both - 2 * NSTATE
    half = width // 2
    tile = part_ref.shape[1]
    core = where_ref[2]
    held_front = front_refs((f0, f1, f2, f3, f4, f5))
    held_gate = gate_refs((z0, z1, z2, z3))

    @pl.when(step == 0)
    def _():
        start_weights(where_ref, held_front, front, front_sems)
        start_weights(where_ref, held_gate, gate, gate_sems)
        ext[rows : rows + 8, :] = halo_ref[...]
        ext_tok[rows : rows + 8, :] = halo_tok_ref[...]
        small_ref[...] = jnp.zeros_like(small_ref)

    @pl.when(jnp.logical_and(step > 0, step < chunks))
    def _():
        ext[rows : rows + 8, :] = ext[0:8, :]
        ext_tok[rows : rows + 8, :] = ext_tok[0:8, :]

    @pl.when(step < chunks)
    def _():
        grad = grad_ref[...]
        ext[0:rows, :] = grad
        ext_tok[0:rows, :] = tok_ref[...]
        pre = pre_ref[...]
        out = pack_ref[TAPS : TAPS + 1, :] * grad
        small_ref[TAPS : TAPS + 1, :] += jnp.sum(grad * pre, axis=0, keepdims=True)
        small_ref[BIAS : BIAS + 1, :] += jnp.sum(grad, axis=0, keepdims=True)
        for k in range(1, CONV):
            shifted = ext_tok[k : k + rows, k : k + 1] * ext[k : k + rows, :]
            out = out + pack_ref[TAPS + k : TAPS + k + 1, :] * shifted
            small_ref[TAPS + k : TAPS + k + 1, :] += jnp.sum(shifted * pre, axis=0, keepdims=True)
        out_x = out[:, :width].astype(BF16)
        s_top, s_rest = halves(out[:, width:])
        raw = raw_ref[...]
        dz = dz_ref[...]
        at = pl.ds(pl.multiple_of((chunks - 1 - step) * rows, rows), rows)
        grads[at, :] = jnp.concatenate([out_x, s_top, raw, dz, s_rest], axis=1)
        none = jnp.zeros((rows, LANES), BF16)
        for_lower = [dz[:, :half], out_x[:, :half], s_top, s_rest]
        for_upper = [dz[:, half:], out_x[:, half:], raw, none, none, none]

        @pl.when(core == 0)
        def _():
            keep_ref[...] = jnp.concatenate(for_lower, axis=1)
            send_ref[...] = jnp.concatenate(for_upper, axis=1)

        @pl.when(core == 1)
        def _():
            keep_ref[...] = jnp.concatenate(for_upper, axis=1)
            send_ref[...] = jnp.concatenate(for_lower, axis=1)

    @pl.when(step == chunks)
    def _():
        wait_weights(where_ref, held_front, front, front_sems)
        wait_weights(where_ref, held_gate, gate, gate_sems)
        skip = gather_heads(skip_ref[...], gather_ref[...])
        small_ref[SKIP : SKIP + 1, :LANES] = skip[0:1, :]
        small_ref[GATED : GATED + 1, :width] = gained_ref[0:1, :]
        small_ref[STEP : STEP + 2, :LANES] = head_ref[0:2, :]

    for n in range(2 * front.shape[0] // (2 * tile)):

        @pl.when(step == chunks + n)
        def _():
            at = slice(n * tile, (n + 1) * tile)
            part = (
                mm(grads[:, : both + LANES], front[at, :], NT)
                + mm(grads[:, both + LANES : both + LANES + width], gate[at, :], NT)
                + mm(grads[:, both + LANES + width :], front[at, width:both], NT)
            )
            part_ref[...] = part
            row = jnp.sum(part * (x_ref[...].astype(F32) * inv_ref[:, 0:1]), axis=0, keepdims=True)
            per_row = front.shape[0] // 2 // tile
            place = slice((n % per_row) * tile, (n % per_row + 1) * tile)
            small_ref[NORM + n // per_row : NORM + n // per_row + 1, place] = row


def conv_back_call(
    where, grad, pre, grad_raw, dz, tok, halo, halo_tok, pack, x, inv, head, skip, gained, gather_matrix, front, gate
):
    length, both = pre.shape
    width = both - 2 * NSTATE
    model = 4 * front[-1].shape[0]
    rows = min(SPAN, length)
    chunks = length // rows
    tile = model // 4
    out_width = width + 4 * NSTATE

    def chunk_spec(size):
        return pl.BlockSpec((rows, size), lambda c: (jnp.maximum(chunks - 1 - c, 0), 0))

    def tile_spec(rows_):
        return pl.BlockSpec((rows_, tile), lambda c: (0, jnp.maximum(c - chunks, 0)))

    return pl.pallas_call(
        functools.partial(conv_back_kernel, chunks),
        grid=(chunks + model // tile,),
        in_specs=[
            scalars_of(),
            chunk_spec(both),
            chunk_spec(both),
            chunk_spec(LANES),
            chunk_spec(width),
            chunk_spec(LANES),
            whole_of(8, both),
            whole_of(8, LANES),
            whole_of(*pack.shape),
            tile_spec(length),
            whole_of(length, LANES),
            whole_of(8, LANES),
            whole_of(8, width),
            whole_of(8, width),
            whole_of(2 * width, LANES),
        ]
        + anywhere(10),
        out_specs=[
            chunk_spec(out_width),
            chunk_spec(out_width),
            tile_spec(length),
            whole_of(*pack.shape),
        ],
        out_shape=[
            shape(length, out_width, dtype=BF16),
            shape(length, out_width, dtype=BF16),
            shape(length, model),
            shape(*pack.shape),
        ],
        scratch_shapes=weight_scratch(front)
        + weight_scratch(gate)
        + [
            pltpu.VMEM((rows + 8, both), F32),
            pltpu.VMEM((rows + 8, LANES), F32),
            pltpu.VMEM((length, both + LANES + width + 2 * NSTATE), BF16),
        ],
        compiler_params=params_of(),
        cost_estimate=cost(4 * length * model * both, 24 * length * width),
        name="conv_back",
    )(where, grad, pre, grad_raw, dz, tok, halo, halo_tok, pack, x, inv, head, skip, gained, gather_matrix, *front, *gate)


def swap(value, axis):
    return lax.ppermute(value, axis, [(0, 1), (1, 0)])


def shifted_along(value, axis, by):
    count = lax.axis_size(axis)
    return lax.ppermute(
        value, axis, [(i, i + by) for i in range(count) if 0 <= i + by < count]
    )


def sum_over(value, axis):
    if lax.axis_size(axis) == 2:
        return value + swap(value, axis)
    return lax.psum(value, axis)


def after(value, *earlier):
    return lax.optimization_barrier((value,) + earlier)[0]


def carried_state(state, rate_wide, axis, backward):
    count = lax.axis_size(axis)
    if count == 2:
        return shifted_along(state, axis, -1 if backward else 1)
    here = lax.axis_index(axis)
    states = lax.all_gather(state, axis)
    rates = lax.all_gather(rate_wide, axis)
    result = jnp.zeros_like(state)
    for k in range(count):
        at = count - 1 - k if backward else k
        reached = at > here if backward else at < here
        result = jnp.where(reached, rates[at] * result + states[at], result)
    return result


def small_sum(value):
    count = lax.axis_size("tensor")
    total = value
    for by in range(1, count):
        total = total + lax.ppermute(
            value, "tensor", [(i, (i + by) % count) for i in range(count)]
        )
    return total


def tensor_sum(value, kind, pieces):
    index = lax.axis_index("tensor")
    odd = index % 2
    pair = [(0, 1), (1, 0), (2, 3), (3, 2)]
    cross = [(0, 2), (2, 0), (1, 3), (3, 1)]
    rows = value.shape[0] // (2 * pieces)
    results = []
    for p in range(pieces):
        base = 2 * rows * p
        give = lax.dynamic_slice_in_dim(value, base + (1 - odd) * rows, rows, 0).astype(kind)
        keep = lax.dynamic_slice_in_dim(value, base + odd * rows, rows, 0)
        part = (keep + lax.ppermute(give, "tensor", pair).astype(F32)).astype(kind)
        total = part.astype(F32) + lax.ppermute(part, "tensor", cross).astype(F32)
        total = total.astype(kind)
        other = lax.ppermute(total, "tensor", pair)
        results.append(jnp.where(odd == 0, total, other))
        results.append(jnp.where(odd == 0, other, total))
    return jnp.concatenate(results, axis=0)


def scatter_sum(value, kind):
    return lax.psum_scatter(
        value.astype(kind), ("fsdp", "context"), scatter_dimension=0, tiled=False
    )


def shards(
    block_input,
    doc_start,
    cotangent,
    norm_gain,
    proj_main,
    proj_states,
    proj_step,
    conv_main,
    conv_main_bias,
    conv_states,
    conv_states_bias,
    step_bias,
    log_decay,
    skip_gain,
    gated_gain,
    proj_out,
):
    core = lax.axis_index("section")
    lower_core = core == 0
    length = block_input.shape[1]
    model = block_input.shape[2]
    heads = proj_step.shape[2]
    width = heads * HEAD_DIM
    half = width // 2
    both = width + 2 * NSTATE
    rows = min(SPAN, length)
    first = (1 - lax.axis_index("fsdp")).astype(jnp.int32)
    places = [
        jnp.stack([(core == layer).astype(jnp.int32), first, core.astype(jnp.int32)]) for layer in (0, 1)
    ]

    main_own = lax.optimization_barrier(proj_main[0].reshape(-1, 2 * width))
    rest_own = jnp.concatenate(
        [proj_states[0], jnp.pad(proj_step[0], ((0, 0), (0, LANES - heads)))], axis=1
    )
    out_own = proj_out[0]
    main_near = swap(main_own, "section")
    rest_near = swap(rest_own, "section")
    out_near = swap(out_own, "section")
    near_rows = main_own.shape[0]

    def half_of(layer, own, near):
        shard = jnp.where(core == layer, own, near)
        return lax.dynamic_slice_in_dim(shard, core * (near_rows // 2), near_rows // 2, 0)

    def across(piece):
        mine = swap(piece, "fsdp")
        return mine, swap(mine, "section")

    def front_piece(layer):
        return jnp.concatenate(
            [
                half_of(layer, main_own[:, width:], main_near[:, width:]),
                half_of(layer, rest_own, rest_near),
            ],
            axis=1,
        )

    def gate_piece(layer):
        return half_of(layer, main_own[:, :width], main_near[:, :width])

    def out_piece(layer):
        return half_of(layer, out_own, out_near)

    front_far0 = across(front_piece(0))
    gate_far0 = across(after(gate_piece(0), front_far0[0]))
    out_far0 = across(after(out_piece(0), gate_far0[0]))
    front_far1 = across(after(front_piece(1), out_far0[0]))
    out_far1 = across(after(out_piece(1), front_far1[0]))
    gate_far1 = across(after(gate_piece(1), out_far1[0]))
    mains = (main_own, main_near)
    fronts = [mains + (rest_own, rest_near) + far for far in (front_far0, front_far1)]
    gates = [mains + far for far in (gate_far0, gate_far1)]
    outs = [(out_own, out_near) + far for far in (out_far0, out_far1)]

    head_of = np.arange(width) // HEAD_DIM
    one_hot = (np.arange(LANES)[:, None] == head_of[None, :]).astype(np.float32)
    spread_matrix = jnp.asarray(np.concatenate([one_hot, one_hot], axis=0), BF16)
    gather_matrix = jnp.asarray(np.concatenate([one_hot.T, one_hot.T], axis=0), BF16)
    row_head = np.arange(heads * rows) // rows
    ones = jnp.asarray((row_head[:, None] == np.arange(LANES)[None, :]).astype(np.float32), BF16)
    consts = (spread_matrix, gather_matrix, ones)

    tokens = lax.dynamic_index_in_dim(block_input, core, 0, keepdims=False)
    cot = lax.dynamic_index_in_dim(cotangent, core, 0, keepdims=False)
    starts = lax.dynamic_index_in_dim(doc_start, core, 0, keepdims=False).astype(F32)
    earlier = shifted_along(starts[length - 8 :], "context", 1)
    later = shifted_along(starts[:8], "context", -1)
    line = jnp.concatenate([earlier, starts, later])
    keep = 1.0 - line
    one_back = keep[8:]
    two_back = one_back * keep[7:-1]
    three_back = two_back * keep[6:-2]
    tok_all = jnp.stack([line[8:], one_back, two_back, three_back], axis=1)
    tok_all = jnp.pad(tok_all, ((0, 0), (0, LANES - 4)))
    tok, tok_after = tok_all[:length], tok_all[length:]

    def head_lanes(row):
        return jnp.pad(row, ((0, 0), (0, LANES - heads)))

    pack_own = pl.pallas_call(pack_kernel, out_shape=shape(PACK, both), name="pack")(
        conv_main[0],
        conv_states[0],
        conv_main_bias,
        conv_states_bias,
        jnp.repeat(skip_gain, HEAD_DIM, axis=1),
        gated_gain,
        norm_gain,
        head_lanes(step_bias),
        head_lanes(log_decay),
    )
    pack_other = swap(pack_own, "section")
    packs = [jnp.where(core == layer, pack_own, pack_other) for layer in (0, 1)]

    def layer_forward(x, halo, layer, *grad_scaled):
        pack = packs[layer]
        place = places[layer]
        normed, inv, pre, conv_x, conv_s, raw, step, cum, entry, rate, end, end_rate = front_call(
            place, x, halo, tok, pack, spread_matrix, fronts[layer]
        )
        rate_wide = jnp.repeat(end_rate[0:1, :heads], HEAD_DIM, axis=1)
        entry_in = carried_state(end, rate_wide, "context", False)
        z = project_call(place, normed, gate_refs, gates[layer])
        y = mix_call(conv_x, conv_s, step, cum, entry, spread_matrix)
        comb, gated, sums = gate_call(
            y, z, conv_x, conv_s, cum, rate, entry_in, pack, spread_matrix, *grad_scaled
        )
        sums = small_sum(sums)
        low_keep, low_send, branch = out_call(place, gated, sums, pack, outs[layer])
        kept = (conv_x, conv_s, step, cum, raw, entry, rate, entry_in)
        return branch, (normed, inv, pre, z, kept, comb, (low_keep, low_send), sums, rate_wide)

    def layer_backward(grad_scaled, sums, x, forward, layer):
        normed, inv, pre, z, kept, comb, _, _, rate_wide = forward
        pack = packs[layer]
        dmix, dz, adj, adj_rate, begin, gained = gate_back_call(
            grad_scaled, comb, z, kept[1], kept[3], sums, pack, spread_matrix
        )
        adj_in = carried_state(begin, rate_wide, "context", True)
        *parts, skip = mix_back_call(kept, dmix, adj, consts)
        grad, grad_raw, head = later_call(kept, dmix, adj_rate, adj_in, parts, pack, consts)
        edge = shifted_along(grad[:8], "context", -1)
        return conv_back_call(
            places[layer],
            grad,
            pre,
            grad_raw,
            dz,
            tok,
            edge,
            tok_after,
            pack,
            x,
            inv,
            head,
            skip,
            gained,
            gather_matrix,
            fronts[layer],
            gates[layer],
        )

    blocks = lax.axis_size("fsdp") * lax.axis_size("context")
    share = model // blocks

    def matrix_grads(normed, g_low, low, keep, send):
        received = swap(send, "section")
        normed_other = swap(normed, "section")
        low_keep, low_send = low
        low_received = swap(low_send, "section")
        g_other = swap(g_low, "section")
        cols = mm(normed, keep[:, :width], TN) + mm(normed_other, received[:, :width], TN)
        top = slice(width, width + 2 * NSTATE)
        rest = slice(width + 2 * NSTATE, width + 4 * NSTATE)
        states = (
            mm(normed, keep[:, top], TN)
            + mm(normed, keep[:, rest], TN)
            + mm(normed_other, received[:, top], TN)
            + mm(normed_other, received[:, rest], TN)
        )
        outer = mm(g_low, low_keep, TN) + mm(g_other, low_received, TN)
        states = scatter_sum(states.reshape(blocks, share, -1), F32)
        states = jnp.where(lower_core, lax.psum(states, "tensor"), states)
        matrices = jnp.concatenate([cols.astype(BF16), outer.astype(BF16)], axis=1)
        return states, scatter_sum(matrices.reshape(blocks, share, -1), BF16)

    halo0 = shifted_along(tokens[length - 8 :], "context", 1)
    branch0, forward0 = layer_forward(tokens, halo0, 0)
    edge0 = tokens[length - 8 :].astype(F32) + small_sum(branch0[length - 8 :])
    halo1 = shifted_along(edge0, "context", 1)
    branch0 = tensor_sum(branch0, jnp.float16, 2).astype(F32)
    x1 = tokens.astype(F32) + branch0
    grad_scaled1 = project_call(places[1], cot, out_refs, outs[1])
    branch1, forward1 = layer_forward(x1, halo1, 1, grad_scaled1)
    x2 = x1 + lax.psum(branch1.astype(BF16), "tensor").astype(F32)

    keep1, send1, part1, small1 = layer_backward(grad_scaled1, forward1[7], x1, forward1, 1)
    normed_grad1 = tensor_sum(part1, BF16, 2)
    grad1, g_low0, grad_scaled0, sums0 = finish_call(
        places[0], normed_grad1, cot, x1, forward1[1], packs[1], branch0, forward0[7], *outs[0]
    )
    keep0, send0, part0, small0 = layer_backward(grad_scaled0, sums0, tokens, forward0, 0)
    normed_grad0 = tensor_sum(part0, BF16, 2)
    grad0 = finish_call(places[0], normed_grad0, grad1, tokens, forward0[1], packs[0])[0]

    mats1 = matrix_grads(forward1[0], cot, forward1[6], keep1, send1)
    mats0 = matrix_grads(forward0[0], g_low0, forward0[6], keep0, send0)

    def to_layer(first, second, kind):
        mine = jnp.where(lower_core, first, second).astype(kind)
        theirs = swap(jnp.where(lower_core, second, first).astype(kind), "section")
        return jnp.where(lower_core, mine, theirs).astype(F32), jnp.where(lower_core, theirs, mine).astype(F32)

    grad_states, step_wide = to_layer(mats0[0], mats1[0], F32)
    lower, upper = to_layer(mats0[1], mats1[1], BF16)
    grad_main = jnp.stack(
        [
            jnp.concatenate([lower[:, :half], upper[:, :half]], axis=1),
            jnp.concatenate([lower[:, half:width], upper[:, half:width]], axis=1),
        ],
        axis=1,
    )
    grad_out = jnp.concatenate([lower[:, width:], upper[:, width:]], axis=1)

    row = np.arange(PACK)[:, None]
    lane = np.arange(both)[None, :]
    shared = ((row < SKIP) & (lane >= width)) | (row == NORM) | (row == NORM + 1)

    def over_tensor(small):
        return jnp.where(shared, small_sum(small), small)

    vector = jnp.where(lower_core, small0, small1) + swap(
        jnp.where(lower_core, small1, small0), "section"
    )
    vector = over_tensor(sum_over(sum_over(vector, "fsdp"), "context"))

    def to_sections(first, second):
        mine = jnp.where(lower_core, first, second)
        theirs = swap(jnp.where(lower_core, second, first), "section")
        return jnp.stack([jnp.where(lower_core, mine, theirs), jnp.where(lower_core, theirs, mine)])

    layer_out = to_sections(x1, x2)
    layer_in_grad = to_sections(grad0, grad1)
    return (
        layer_out[None],
        layer_in_grad[None],
        vector[NORM : NORM + 2, : model // 2].reshape(1, model),
        grad_main[None],
        grad_states[None],
        step_wide[None, :, :heads],
        vector[None, TAPS : TAPS + CONV, :width],
        vector[BIAS : BIAS + 1, :width],
        vector[None, TAPS : TAPS + CONV, width:],
        vector[BIAS : BIAS + 1, width:],
        vector[STEP : STEP + 1, :heads],
        vector[DECAY : DECAY + 1, :heads],
        vector[SKIP : SKIP + 1, :heads],
        vector[GATED : GATED + 1, :width],
        grad_out[None],
    )


def solution(mesh):
    placed = (
        P("fsdp", "context", None),
        P("fsdp", "context"),
        P("fsdp", "context", None),
        P("section", None),
        P("section", "fsdp", None, "tensor"),
        P("section", "fsdp", None),
        P("section", "fsdp", "tensor"),
        P("section", None, "tensor"),
        P("section", "tensor"),
        P("section", None, None),
        P("section", None),
        P("section", "tensor"),
        P("section", "tensor"),
        P("section", "tensor"),
        P("section", "tensor"),
        P("section", "fsdp", "tensor"),
    )
    return jax.shard_map(
        shards,
        mesh=mesh,
        in_specs=placed,
        out_specs=(
            P("section", "fsdp", "context", None),
            P("section", "fsdp", "context", None),
            P("section", None),
            P("section", ("fsdp", "context"), None, "tensor"),
            P("section", ("fsdp", "context"), None),
            P("section", ("fsdp", "context"), "tensor"),
            P("section", None, "tensor"),
            P("section", "tensor"),
            P("section", None, None),
            P("section", None),
            P("section", "tensor"),
            P("section", "tensor"),
            P("section", "tensor"),
            P("section", "tensor"),
            P("section", ("fsdp", "context"), "tensor"),
        ),
        check_vma=False,
    )
```

time: 2830 us -> 647 us (0.23); the launches traced: 2780 us -> 636 us
  local copies, waits for them, and re-layouts: 1020 us -> 76.2 us
  waiting for transfers between devices: 685 us -> 261 us
  other arithmetic: 445 us -> 60.4 us
  matrix products: 383 us -> 25 us
  blocking collectives: 184 us -> 0 us
  Pallas kernels: 0 us -> 114 us
  starting transfers between devices: 25.3 us -> 82 us
    psum x8 -> x2, waiting for transfers between devices: 511 us -> 3.09 us  [the longest x1 3.09 us: shards(): x2 = x1 + lax.psum(branch1.astype(BF16), 'tensor').astype(F32)]
    dynamic_update_slice x162 -> x0, local copies, waits for them, and re-layouts: 475 us -> none  [the longest x126 465 us: scan_spans(): state_out, outputs = lax.scan(span_step, state_in, pieces)]
    dot_general x156 -> x16, matrix products: 383 us -> 25 us  [mm(): return lax.dot_general(a, b, dims, preferred_element_type=F32)]
    ppermute x10 -> x71, waiting for transfers between devices: 3.21 us -> 251 us  [the longest x6 81.5 us: tensor_sum(): total = part.astype(F32) + lax.ppermute(part, 'tensor', cross).astype(F32)]
    another operation x392 -> x5, local copies, waits for them, and re-layouts: 173 us -> 0.86 us  [shards(): tok_all = jnp.stack([line[8:], one_back, two_back, three_back], axis=1)]
    reduce_scatter x4 -> x0, waiting for transfers between devices: 144 us -> none  [the longest x1 60.8 us: shards(): lax.psum_scatter(matrix_totals[3], ('fsdp', 'context'), scatter_dimension...]
    pallas_call x0 -> x22, Pallas kernels: none -> 114 us  [the longest x2 20.8 us: conv_back_call(): pl.pallas_call(functools.partial(conv_back_kernel, chunks), grid=(chunks...]
    dynamic_slice x138 -> x0, local copies, waits for them, and re-layouts: 112 us -> none  [the longest x90 85.2 us: states_only(): state_out, rates = lax.scan(state_step, state_in, pieces)]
  transfers between devices with their start and end apart: 24 -> 77, of which waited for: 14 -> 38; matrix products, arithmetic and copies ran while one was open for 20% -> 16% of each run, Pallas kernels for 0% -> 14%
where the time goes in v1:
time: 647 us; the launch traced here: 636 us
  waiting for transfers between devices  261 us (40%)
  Pallas kernels  114 us (18%)
  starting transfers between devices  82 us (13%)
  local copies, waits for them, and re-layouts  76.2 us (12%)
  other arithmetic  60.4 us (9%)
  matrix products  25 us (4%)
  between operations  17.7 us (3%)
    ppermute x6, waiting for transfers between devices, tensor_sum(): total = part.astype(F32) + lax.ppermute(part, 'tensor', cross).astype(F32)  81.5 us
    ppermute x6, waiting for transfers between devices, tensor_sum(): part = (keep + lax.ppermute(give, 'tensor', pair).astype(F32)).astype(kind)  54.1 us
    ppermute x6, waiting for transfers between devices, tensor_sum(): other = lax.ppermute(total, 'tensor', pair)  53.4 us
    unnamed x278, local copies, waits for them, and re-layouts  47.7 us
    ppermute x31, waiting for transfers between devices, swap(): return lax.ppermute(value, axis, [(0, 1), (1, 0)])  34.4 us
    ppermute x10, starting transfers between devices, shifted_along(): lax.ppermute(value, axis, [(i, i + by) for i in range(count) if 0 <= i +...  26.4 us
    dot_general x16, matrix products, mm(): return lax.dot_general(a, b, dims, preferred_element_type=F32)  25 us
    pallas_call x2, Pallas kernels, conv_back_call(): pl.pallas_call(functools.partial(conv_back_kernel, chunks), grid=(chunks...  20.8 us
  transfers between devices with their start and end apart: 77, of which 38 were waited for; matrix products, arithmetic and copies ran while one was open for 16% of the time, Pallas kernels for 14%

profile of v1, /device:TPU:0, one launch (start us, length us, event | category | flops | bytes accessed | tf_op | source)
XLA Modules:
  0.0 636.2 jit_solution(5004111901547442394)
XLA Ops:
  8.1 3.7 copy.57
  28.5 4.5 collective-permute-start.2
  42.5 4.8 collective-permute-done.6.w4.f4
  47.4 4.3 collective-permute-start
  55.7 10.3 %collective-permute-done.8.w2.z2 = bf16[384,768]{1,0:T(8,128)(2,1)} collective-permute-done((bf16[384,768]{1,0:T(8,128)(2,1)S(1)}, bf16[384,768]{1,0:T(8,128)(2,1)}, u32[]{:S(2)}, u32[]{:S(2)}) %collective-permute-start.8) | collective-permute-done | bytes 589856 | tf_op jit(solution)/shard_map/ppermute | solution.py:1213
  73.1 10.0 %front.2 = (bf16[512,1536]{1,0:T(8,128)(2,1)S(1)}, f32[512,128]{1,0:T(8,128)S(1)}, f32[512,1024]{1,0:T(8,128)S(1)}, f32[512,768]{1,0:T(8,128)S(1)}, f32[512,256]...) custom-call(s32[3]{0:T(128)S(1)} %copy-done.88, ...), custom_call_target="tpu_custom_call" | custom-call | flops 1811939328 | bytes 9437184 | tf_op jit(solution)/shard_map/front/pallas_call | solution.py:336
  89.6 3.9 project.3.z_ref
  114.2 4.7 out.2
  136.1 4.6 collective-permute-start.26
  148.4 25.5 %collective-permute-done.18 = f16[128,1536]{1,0:T(8,128)(2,1)S(1)} collective-permute-done((f16[128,1536]{1,0:T(8,128)(2,1)S(1)}, f16[128,1536]{1,0:T(8,128)(2,1)S(1)}, u32[]{:S(2)}, u32[]{:S(2)}) %collective-permute-start.18) | collective-permute-done | bytes 393248 | tf_op jit(solution)/shard_map/ppermute | solution.py:1270
  175.7 6.6 %collective-permute-done.21 = f16[128,1536]{1,0:T(8,128)(2,1)S(1)} collective-permute-done((f16[128,1536]{1,0:T(8,128)(2,1)S(1)}, f16[128,1536]{1,0:T(8,128)(2,1)S(1)}, u32[]{:S(2)}, u32[]{:S(2)}) %collective-permute-start.21) | collective-permute-done | bytes 393248 | tf_op jit(solution)/shard_map/ppermute | solution.py:1270
  182.4 8.2 %collective-permute-done.19 = f16[128,1536]{1,0:T(8,128)(2,1)S(1)} collective-permute-done((f16[128,1536]{1,0:T(8,128)(2,1)S(1)}, f16[128,1536]{1,0:T(8,128)(2,1)S(1)}, u32[]{:S(2)}, u32[]{:S(2)}) %collective-permute-start.19) | collective-permute-done | bytes 393248 | tf_op jit(solution)/shard_map/ppermute | solution.py:1272
  190.9 10.7 %collective-permute-done.22 = f16[128,1536]{1,0:T(8,128)(2,1)S(1)} collective-permute-done((f16[128,1536]{1,0:T(8,128)(2,1)S(1)}, f16[128,1536]{1,0:T(8,128)(2,1)S(1)}, u32[]{:S(2)}, u32[]{:S(2)}) %collective-permute-start.22) | collective-permute-done | bytes 393248 | tf_op jit(solution)/shard_map/ppermute | solution.py:1272
  203.0 8.9 %front.3 = (bf16[512,1536]{1,0:T(8,128)(2,1)S(1)}, f32[512,128]{1,0:T(8,128)S(1)}, f32[512,1024]{1,0:T(8,128)S(1)}, f32[512,768]{1,0:T(8,128)S(1)}, f32[512,256]...) custom-call(s32[3]{0:T(128)S(1)} %add_add_fusion.4.where_ref, ...), custom_call_target="tpu_custom_call" | custom-call | flops 1811939328 | bytes 9437184 | tf_op jit(solution)/shard_map/front/pallas_call | solution.py:336
  211.9 4.7 collective-permute-start.32
  216.8 3.8 project.5.refs_0_.scaled_ref
  223.2 3.7 project.4.z_ref
  241.5 8.8 %mix_back.2 = (f32[512,768]{1,0:T(8,128)S(1)}, f32[512,128]{1,0:T(8,128)S(1)}, f32[512,128]{1,0:T(8,128)S(1)}, f32[512,128]{1,0:T(8,128)S(1)}, f32[8,768]{1,0:T(8,128)S(1)}) custom-call(f32[512,768]{1,0:T(8,128)S(1)} %get-tuple-element.108.conv_x_ref, f32[512,256]{1,0:T(8,128)S(1)} %get-tuple-element.109.conv_s_ref, ...), custom_call_target="tpu_custom_call" | custom-call | flops 2013265920 | bytes 7864320 | tf_op jit(solution)/shard_map/mix_back/pallas_call | solution.py:865
  250.3 5.4 later.2
  257.5 4.1 collective-permute-done.39.halo_ref
  261.6 10.6 %conv_back.2 = (bf16[512,1280]{1,0:T(8,128)(2,1)S(1)}, bf16[512,1280]{1,0:T(8,128)(2,1)S(1)}, f32[512,1536]{1,0:T(8,128)S(1)}, f32[16,1024]{1,0:T(8,128)S(1)}) custom-call(s32[3]{0:T(128)S(1)} %add_add_fusion.4.where_ref, f32[512,1024]{1,0:T(8,128)S(1)} %get-tuple-element.131.grad_ref, f32[512,1024]{1,0:T(8,128)S(1)} %get-tuple-element.132.pre_ref, ...), custom_call_target="tpu_custom_call" | custom-call | flops 3221225472 | bytes 9437184 | tf_op jit(solution)/shard_map/conv_back/pallas_call | solution.py:1166
  274.4 8.3 %collective-permute-done.40 = bf16[128,1536]{1,0:T(8,128)(2,1)S(1)} collective-permute-done((bf16[128,1536]{1,0:T(8,128)(2,1)S(1)}, bf16[128,1536]{1,0:T(8,128)(2,1)S(1)}, u32[]{:S(2)}, u32[]{:S(2)}) %collective-permute-start.40) | collective-permute-done | bytes 393248 | tf_op jit(solution)/shard_map/ppermute | solution.py:1269
  282.8 7.1 %collective-permute-done.43 = bf16[128,1536]{1,0:T(8,128)(2,1)S(1)} collective-permute-done((bf16[128,1536]{1,0:T(8,128)(2,1)S(1)}, bf16[128,1536]{1,0:T(8,128)(2,1)S(1)}, u32[]{:S(2)}, u32[]{:S(2)}) %collective-permute-start.43) | collective-permute-done | bytes 393248 | tf_op jit(solution)/shard_map/ppermute | solution.py:1269
  294.8 20.7 %collective-permute-done.41 = bf16[128,1536]{1,0:T(8,128)(2,1)S(1)} collective-permute-done((bf16[128,1536]{1,0:T(8,128)(2,1)S(1)}, bf16[128,1536]{1,0:T(8,128)(2,1)S(1)}, u32[]{:S(2)}, u32[]{:S(2)}) %collective-permute-start.41) | collective-permute-done | bytes 393248 | tf_op jit(solution)/shard_map/ppermute | solution.py:1270
  315.7 4.2 collective-permute-done.44
  320.2 8.1 %collective-permute-done.42 = bf16[128,1536]{1,0:T(8,128)(2,1)S(1)} collective-permute-done((bf16[128,1536]{1,0:T(8,128)(2,1)S(1)}, bf16[128,1536]{1,0:T(8,128)(2,1)S(1)}, u32[]{:S(2)}, u32[]{:S(2)}) %collective-permute-start.42) | collective-permute-done | bytes 393248 | tf_op jit(solution)/shard_map/ppermute | solution.py:1272
  328.4 4.2 collective-permute-done.45
  333.3 5.2 finish.2
  356.7 8.8 %mix_back.3 = (f32[512,768]{1,0:T(8,128)S(1)}, f32[512,128]{1,0:T(8,128)S(1)}, f32[512,128]{1,0:T(8,128)S(1)}, f32[512,128]{1,0:T(8,128)S(1)}, f32[8,768]{1,0:T(8,128)S(1)}) custom-call(f32[512,768]{1,0:T(8,128)S(1)} %copy-done.15, f32[512,256]{1,0:T(8,128)S(1)} %copy-done.28, f32[512,768]{1,0:T(8,128)S(1)} %get-tuple-element.143.dmix_ref, ...), custom_call_target="tpu_custom_call" | custom-call | flops 2013265920 | bytes 7864320 | tf_op jit(solution)/shard_map/mix_back/pallas_call | solution.py:865
  365.5 8.1 %collective-permute-done.46.adj_in_ref = f32[128,768]{1,0:T(8,128)S(1)} collective-permute-done((f32[128,768]{1,0:T(8,128)S(1)}, f32[128,768]{1,0:T(8,128)S(1)}, u32[]{:S(2)}, u32[]{:S(2)}) %collective-permute-start.46) | collective-permute-done | bytes 393248 | tf_op jit(solution)/shard_map/ppermute | solution.py:1218
  373.7 5.4 later.3
  380.5 4.4 collective-permute-done.47.halo_ref
  385.0 10.2 %conv_back.3 = (bf16[512,1280]{1,0:T(8,128)(2,1)S(1)}, bf16[512,1280]{1,0:T(8,128)(2,1)S(1)}, f32[512,1536]{1,0:T(8,128)S(1)}, f32[16,1024]{1,0:T(8,128)S(1)}) custom-call(s32[3]{0:T(128)S(1)} %copy-done.92, f32[512,1024]{1,0:T(8,128)S(1)} %get-tuple-element.152.grad_ref, f32[512,1024]{1,0:T(8,128)S(1)} %copy-done.54, ...), custom_call_target="tpu_custom_call" | custom-call | flops 3221225472 | bytes 9437184 | tf_op jit(solution)/shard_map/conv_back/pallas_call | solution.py:1166
  409.9 4.4 out.3
  426.8 6.1 reduce-scatter.17.cloned.1.call-done
  433.0 4.1 add_convert_fusion
  439.2 5.8 copy.56
  449.6 9.5 %collective-permute-done.48 = bf16[128,1536]{1,0:T(8,128)(2,1)S(1)} collective-permute-done((bf16[128,1536]{1,0:T(8,128)(2,1)S(1)}, bf16[128,1536]{1,0:T(8,128)(2,1)S(1)}, u32[]{:S(2)}, u32[]{:S(2)}) %collective-permute-start.48) | collective-permute-done | bytes 393248 | tf_op jit(solution)/shard_map/ppermute | solution.py:1269
  459.1 26.6 %collective-permute-done.51 = bf16[128,1536]{1,0:T(8,128)(2,1)S(1)} collective-permute-done((bf16[128,1536]{1,0:T(8,128)(2,1)S(1)}, bf16[128,1536]{1,0:T(8,128)(2,1)S(1)}, u32[]{:S(2)}, u32[]{:S(2)}) %collective-permute-start.51) | collective-permute-done | bytes 393248 | tf_op jit(solution)/shard_map/ppermute | solution.py:1269
  494.2 4.7 add_select_fusion
  501.8 24.5 %collective-permute-done.49 = bf16[128,1536]{1,0:T(8,128)(2,1)} collective-permute-done((bf16[128,1536]{1,0:T(8,128)(2,1)}, bf16[128,1536]{1,0:T(8,128)(2,1)}, u32[]{:S(2)}, u32[]{:S(2)}) %collective-permute-start.49) | collective-permute-done | bytes 393248 | tf_op jit(solution)/shard_map/ppermute | solution.py:1270
  536.3 3.7 copy.55
  542.6 3.7 collective-permute-done.50
  547.6 18.5 %collective-permute-done.53 = bf16[128,1536]{1,0:T(8,128)(2,1)S(1)} collective-permute-done((bf16[128,1536]{1,0:T(8,128)(2,1)S(1)}, bf16[128,1536]{1,0:T(8,128)(2,1)S(1)}, u32[]{:S(2)}, u32[]{:S(2)}) %collective-permute-start.53) | collective-permute-done | bytes 393248 | tf_op jit(solution)/shard_map/ppermute | solution.py:1272
  571.9 5.2 collective-permute-done.55
  578.6 4.6 collective-permute-done.56
  605.5 3.8 select_bitcast_fusion.1
  614.2 5.1 maximum_bitcast_fusion.1
  (520 shorter events, 241.6 us)
Async XLA Ops:
  8.0 418.8 %reduce-scatter.19.cloned.1.call-start = ((), (), s32[]{:S(2)}) async-start(), calls=%async_computation.8 | async-start | bytes 1966080
  24.2 23.1 %collective-permute-start.6 = (bf16[384,1152]{1,0:T(8,128)(2,1)}, bf16[384,1152]{1,0:T(8,128)(2,1)}, u32[]{:S(2)}, u32[]{:S(2)}) collective-permute-start(bf16[384,1152]{1,0:T(8,128)(2,1)} %pad_maximum_fusion.4), channel_id=1, source_target_pairs={{0,8},{8,0},{1,9},{9,1},{2,10},{10,2},{3,11},{11,3},{4,12},{12,4},... | collective-permute-start | bytes 2654216 | tf_op jit(solution)/shard_map/ppermute | solution.py:1213
  27.2 24.5 %collective-permute-start.1 = (f32[8]{0:T(128)S(1)}, f32[8]{0:T(128)S(1)}, u32[]{:S(2)}, u32[]{:S(2)}) collective-permute-start(f32[8]{0:T(128)S(1)} %get-tuple-element.264), channel_id=1, source_target_pairs={{4,0},{5,1},{6,2},{7,3},{12,8},{13,9},{14,10},{15,11},{20,16},{21,... | collective-permute-start | bytes 104 | tf_op jit(solution)/shard_map/ppermute | solution.py:1218
  28.5 24.7 %collective-permute-start.2 = (f32[8]{0:T(128)S(1)}, f32[8]{0:T(128)S(1)}, u32[]{:S(2)}, u32[]{:S(2)}) collective-permute-start(f32[8]{0:T(128)S(1)} %get-tuple-element.263), channel_id=1, source_target_pairs={{0,4},{1,5},{2,6},{3,7},{8,12},{9,13},{10,14},{11,15},{16,20},{17,... | collective-permute-start | bytes 104 | tf_op jit(solution)/shard_map/ppermute | solution.py:1218
  36.2 33.2 %collective-permute-start.3 = (f32[16,1024]{1,0:T(8,128)}, f32[16,1024]{1,0:T(8,128)}, u32[]{:S(2)}, u32[]{:S(2)}) collective-permute-start(f32[16,1024]{1,0:T(8,128)} %pack.1), channel_id=1, source_target_pairs={{0,16},{16,0},{1,17},{17,1},{2,18},{18,2},{3,19},{19,3},{4,20},{20... | collective-permute-start | bytes 196616 | tf_op jit(solution)/shard_map/ppermute | solution.py:1213
  36.2 17.1 %collective-permute-start.14 = (bf16[768,768]{1,0:T(8,128)(2,1)}, bf16[768,768]{1,0:T(8,128)(2,1)}, u32[]{:S(2)}, u32[]{:S(2)}) collective-permute-start(bf16[768,768]{1,0:T(8,128)(2,1)} %bitcast.106), channel_id=1, source_target_pairs={{0,16},{16,0},{1,17},{17,1},{2,18},{18,2},{3,19},{19,3},{4,20},{20... | collective-permute-start | bytes 3538952 | tf_op jit(solution)/shard_map/ppermute | solution.py:1213
  47.4 23.6 %collective-permute-start = (bf16[8,1536]{1,0:T(8,128)(2,1)}, bf16[8,1536]{1,0:T(8,128)(2,1)}, u32[]{:S(2)}, u32[]{:S(2)}) collective-permute-start(bf16[8,1536]{1,0:T(8,128)(2,1)} %dynamic-slice_bitcast_fusion.2), channel_id=1, source_target_pairs={{0,4},{1,5},{2,6},{3,7},{8,12},{9,13},{10,14},{11,15},{16,20},{17,... | collective-permute-start | bytes 73736 | tf_op jit(solution)/shard_map/ppermute | solution.py:1218
  51.6 14.4 %collective-permute-start.8 = (bf16[384,768]{1,0:T(8,128)(2,1)S(1)}, bf16[384,768]{1,0:T(8,128)(2,1)}, u32[]{:S(2)}, u32[]{:S(2)}) collective-permute-start(bf16[384,768]{1,0:T(8,128)(2,1)S(1)} %get-tuple-element.100), channel_id=1, source_target_pairs={{0,8},{8,0},{1,9},{9,1},{2,10},{10,2},{3,11},{11,3},{4,12},{12,4},... | collective-permute-start | bytes 1769480 | tf_op jit(solution)/shard_map/ppermute | solution.py:1213
  53.2 17.7 %collective-permute-start.7 = (bf16[384,1152]{1,0:T(8,128)(2,1)}, bf16[384,1152]{1,0:T(8,128)(2,1)}, u32[]{:S(2)}, u32[]{:S(2)}) collective-permute-start(bf16[384,1152]{1,0:T(8,128)(2,1)} %collective-permute-done.6.w4.f4), channel_id=1, source_target_pairs={{0,16},{16,0},{1,17},{17,1},{2,18},{18,2},{3,19},{19,3},{4,20},{20... | collective-permute-start | bytes 2654216 | tf_op jit(solution)/shard_map/ppermute | solution.py:1213
  66.0 20.4 %collective-permute-start.15 = (bf16[384,768]{1,0:T(8,128)(2,1)}, bf16[384,768]{1,0:T(8,128)(2,1)}, u32[]{:S(2)}, u32[]{:S(2)}) collective-permute-start(bf16[384,768]{1,0:T(8,128)(2,1)} %get-tuple-element.105), channel_id=1, source_target_pairs={{0,8},{8,0},{1,9},{9,1},{2,10},{10,2},{3,11},{11,3},{4,12},{12,4},... | collective-permute-start | bytes 1769480 | tf_op jit(solution)/shard_map/ppermute | solution.py:1213
  69.4 20.2 %collective-permute-start.9 = (bf16[384,768]{1,0:T(8,128)(2,1)}, bf16[384,768]{1,0:T(8,128)(2,1)S(1)}, u32[]{:S(2)}, u32[]{:S(2)}) collective-permute-start(bf16[384,768]{1,0:T(8,128)(2,1)} %collective-permute-done.8.w2.z2), channel_id=1, source_target_pairs={{0,16},{16,0},{1,17},{17,1},{2,18},{18,2},{3,19},{19,3},{4,20},{20... | collective-permute-start | bytes 1769480 | tf_op jit(solution)/shard_map/ppermute | solution.py:1213
  86.4 23.6 %collective-permute-start.16 = (bf16[384,768]{1,0:T(8,128)(2,1)}, bf16[384,768]{1,0:T(8,128)(2,1)}, u32[]{:S(2)}, u32[]{:S(2)}) collective-permute-start(bf16[384,768]{1,0:T(8,128)(2,1)} %collective-permute-done.15.w2.refs_4_), channel_id=1, source_target_pairs={{0,16},{16,0},{1,17},{17,1},{2,18},{18,2},{3,19},{19,3},{4,20},{20... | collective-permute-start | bytes 1769480 | tf_op jit(solution)/shard_map/ppermute | solution.py:1213
  123.2 20.0 %collective-permute-start.27 = (bf16[384,1152]{1,0:T(8,128)(2,1)S(1)}, bf16[384,1152]{1,0:T(8,128)(2,1)S(1)}, u32[]{:S(2)}, u32[]{:S(2)}) collective-permute-start(bf16[384,1152]{1,0:T(8,128)(2,1)S(1)} %pad_maximum_fusion.5), channel_id=1, source_target_pairs={{0,8},{8,0},{1,9},{9,1},{2,10},{10,2},{3,11},{11,3},{4,12},{12,4},... | collective-permute-start | bytes 2654216 | tf_op jit(solution)/shard_map/ppermute | solution.py:1213
  136.1 66.3 %collective-permute-start.26 = (f32[8,1536]{1,0:T(8,128)S(1)}, f32[8,1536]{1,0:T(8,128)S(1)}, u32[]{:S(2)}, u32[]{:S(2)}) collective-permute-start(f32[8,1536]{1,0:T(8,128)S(1)} %add_add_fusion), channel_id=1, source_target_pairs={{0,4},{1,5},{2,6},{3,7},{8,12},{9,13},{10,14},{11,15},{16,20},{17,... | collective-permute-start | bytes 147464 | tf_op jit(solution)/shard_map/ppermute | solution.py:1218
  143.1 30.9 %collective-permute-start.29 = (bf16[384,768]{1,0:T(8,128)(2,1)S(1)}, bf16[384,768]{1,0:T(8,128)(2,1)S(1)}, u32[]{:S(2)}, u32[]{:S(2)}) collective-permute-start(bf16[384,768]{1,0:T(8,128)(2,1)S(1)} %copy-done.129), channel_id=1, source_target_pairs={{0,8},{8,0},{1,9},{9,1},{2,10},{10,2},{3,11},{11,3},{4,12},{12,4},... | collective-permute-start | bytes 1769480 | tf_op jit(solution)/shard_map/ppermute | solution.py:1213
  143.7 58.7 %collective-permute-start.28 = (bf16[384,1152]{1,0:T(8,128)(2,1)S(1)}, bf16[384,1152]{1,0:T(8,128)(2,1)S(1)}, u32[]{:S(2)}, u32[]{:S(2)}) collective-permute-start(bf16[384,1152]{1,0:T(8,128)(2,1)S(1)} %collective-permute-done.27.w4.f4), channel_id=1, source_target_pairs={{0,16},{16,0},{1,17},{17,1},{2,18},{18,2},{3,19},{19,3},{4,20},{20... | collective-permute-start | bytes 2654216 | tf_op jit(solution)/shard_map/ppermute | solution.py:1213
  143.7 30.2 %collective-permute-start.18 = (f16[128,1536]{1,0:T(8,128)(2,1)S(1)}, f16[128,1536]{1,0:T(8,128)(2,1)S(1)}, u32[]{:S(2)}, u32[]{:S(2)}) collective-permute-start(f16[128,1536]{1,0:T(8,128)(2,1)S(1)} %get-tuple-element.221), channel_id=1, source_target_pairs={{0,2},{2,0},{1,3},{3,1},{4,6},{6,4},{5,7},{7,5},{8,10},{10,8},{9,1... | collective-permute-start | bytes 1179656 | tf_op jit(solution)/shard_map/ppermute | solution.py:1270
  148.3 33.9 %collective-permute-start.21 = (f16[128,1536]{1,0:T(8,128)(2,1)S(1)}, f16[128,1536]{1,0:T(8,128)(2,1)S(1)}, u32[]{:S(2)}, u32[]{:S(2)}) collective-permute-start(f16[128,1536]{1,0:T(8,128)(2,1)S(1)} %add_convert_fusion.11), channel_id=1, source_target_pairs={{0,2},{2,0},{1,3},{3,1},{4,6},{6,4},{5,7},{7,5},{8,10},{10,8},{9,1... | collective-permute-start | bytes 1179656 | tf_op jit(solution)/shard_map/ppermute | solution.py:1270
  174.0 16.5 %collective-permute-start.19 = (f16[128,1536]{1,0:T(8,128)(2,1)S(1)}, f16[128,1536]{1,0:T(8,128)(2,1)S(1)}, u32[]{:S(2)}, u32[]{:S(2)}) collective-permute-start(f16[128,1536]{1,0:T(8,128)(2,1)S(1)} %add_convert_fusion.12), channel_id=1, source_target_pairs={{0,1},{1,0},{2,3},{3,2},{4,5},{5,4},{6,7},{7,6},{8,9},{9,8},{10,11... | collective-permute-start | bytes 1179656 | tf_op jit(solution)/shard_map/ppermute | solution.py:1272
  174.1 16.7 %collective-permute-start.30 = (bf16[384,768]{1,0:T(8,128)(2,1)S(1)}, bf16[384,768]{1,0:T(8,128)(2,1)S(1)}, u32[]{:S(2)}, u32[]{:S(2)}) collective-permute-start(bf16[384,768]{1,0:T(8,128)(2,1)S(1)} %copy-done.128), channel_id=1, source_target_pairs={{0,8},{8,0},{1,9},{9,1},{2,10},{10,2},{3,11},{11,3},{4,12},{12,4},... | collective-permute-start | bytes 1769480 | tf_op jit(solution)/shard_map/ppermute | solution.py:1213
  182.2 34.5 %collective-permute-start.33 = (bf16[384,768]{1,0:T(8,128)(2,1)S(1)}, bf16[384,768]{1,0:T(8,128)(2,1)S(1)}, u32[]{:S(2)}, u32[]{:S(2)}) collective-permute-start(bf16[384,768]{1,0:T(8,128)(2,1)S(1)} %collective-permute-done.29.w2), channel_id=1, source_target_pairs={{0,16},{16,0},{1,17},{17,1},{2,18},{18,2},{3,19},{19,3},{4,20},{20... | collective-permute-start | bytes 1769480 | tf_op jit(solution)/shard_map/ppermute | solution.py:1213
  190.8 32.4 %collective-permute-start.31 = (bf16[384,768]{1,0:T(8,128)(2,1)S(1)}, bf16[384,768]{1,0:T(8,128)(2,1)S(1)}, u32[]{:S(2)}, u32[]{:S(2)}) collective-permute-start(bf16[384,768]{1,0:T(8,128)(2,1)S(1)} %collective-permute-done.30.w2.z2), channel_id=1, source_target_pairs={{0,16},{16,0},{1,17},{17,1},{2,18},{18,2},{3,19},{19,3},{4,20},{20... | collective-permute-start | bytes 1769480 | tf_op jit(solution)/shard_map/ppermute | solution.py:1213
  211.9 15.0 %collective-permute-start.32 = (f32[128,768]{1,0:T(8,128)S(1)}, f32[128,768]{1,0:T(8,128)S(1)}, u32[]{:S(2)}, u32[]{:S(2)}) collective-permute-start(f32[128,768]{1,0:T(8,128)S(1)} %get-tuple-element.117), channel_id=1, source_target_pairs={{0,4},{1,5},{2,6},{3,7},{8,12},{9,13},{10,14},{11,15},{16,20},{17,... | collective-permute-start | bytes 1179656 | tf_op jit(solution)/shard_map/ppermute | solution.py:1218
  274.1 15.8 %collective-permute-start.43 = (bf16[128,1536]{1,0:T(8,128)(2,1)S(1)}, bf16[128,1536]{1,0:T(8,128)(2,1)S(1)}, u32[]{:S(2)}, u32[]{:S(2)}) collective-permute-start(bf16[128,1536]{1,0:T(8,128)(2,1)S(1)} %get-tuple-element.220), channel_id=1, source_target_pairs={{0,1},{1,0},{2,3},{3,2},{4,5},{5,4},{6,7},{7,6},{8,9},{9,8},{10,11... | collective-permute-start | bytes 1179656 | tf_op jit(solution)/shard_map/ppermute | solution.py:1269
  290.1 25.5 %collective-permute-start.41 = (bf16[128,1536]{1,0:T(8,128)(2,1)S(1)}, bf16[128,1536]{1,0:T(8,128)(2,1)S(1)}, u32[]{:S(2)}, u32[]{:S(2)}) collective-permute-start(bf16[128,1536]{1,0:T(8,128)(2,1)S(1)} %get-tuple-element.217), channel_id=1, source_target_pairs={{0,2},{2,0},{1,3},{3,1},{4,6},{6,4},{5,7},{7,5},{8,10},{10,8},{9,1... | collective-permute-start | bytes 1179656 | tf_op jit(solution)/shard_map/ppermute | solution.py:1270
  292.3 48.5 %collective-permute-start.65 = (bf16[512,1536]{1,0:T(8,128)(2,1)S(1)}, bf16[512,1536]{1,0:T(8,128)(2,1)S(1)}, u32[]{:S(2)}, u32[]{:S(2)}) collective-permute-start(bf16[512,1536]{1,0:T(8,128)(2,1)S(1)} %get-tuple-element.113.a_ref), channel_id=1, source_target_pairs={{0,16},{16,0},{1,17},{17,1},{2,18},{18,2},{3,19},{19,3},{4,20},{20... | collective-permute-start | bytes 4718600 | tf_op jit(solution)/shard_map/ppermute | solution.py:1213
  292.4 48.5 %collective-permute-start.66 = (bf16[512,1280]{1,0:T(8,128)(2,1)S(1)}, bf16[512,1280]{1,0:T(8,128)(2,1)S(1)}, u32[]{:S(2)}, u32[]{:S(2)}) collective-permute-start(bf16[512,1280]{1,0:T(8,128)(2,1)S(1)} %get-tuple-element.170), channel_id=1, source_target_pairs={{0,16},{16,0},{1,17},{17,1},{2,18},{18,2},{3,19},{19,3},{4,20},{20... | collective-permute-start | bytes 3932168 | tf_op jit(solution)/shard_map/ppermute | solution.py:1213
  293.5 26.5 %collective-permute-start.44 = (bf16[128,1536]{1,0:T(8,128)(2,1)S(1)}, bf16[128,1536]{1,0:T(8,128)(2,1)S(1)}, u32[]{:S(2)}, u32[]{:S(2)}) collective-permute-start(bf16[128,1536]{1,0:T(8,128)(2,1)S(1)} %get-tuple-element.218), channel_id=1, source_target_pairs={{0,2},{2,0},{1,3},{3,1},{4,6},{6,4},{5,7},{7,5},{8,10},{10,8},{9,1... | collective-permute-start | bytes 1179656 | tf_op jit(solution)/shard_map/ppermute | solution.py:1270
  315.7 12.6 %collective-permute-start.42 = (bf16[128,1536]{1,0:T(8,128)(2,1)S(1)}, bf16[128,1536]{1,0:T(8,128)(2,1)S(1)}, u32[]{:S(2)}, u32[]{:S(2)}) collective-permute-start(bf16[128,1536]{1,0:T(8,128)(2,1)S(1)} %add_convert_fusion.8), channel_id=1, source_target_pairs={{0,1},{1,0},{2,3},{3,2},{4,5},{5,4},{6,7},{7,6},{8,9},{9,8},{10,11... | collective-permute-start | bytes 1179656 | tf_op jit(solution)/shard_map/ppermute | solution.py:1272
  320.1 12.4 %collective-permute-start.45 = (bf16[128,1536]{1,0:T(8,128)(2,1)S(1)}, bf16[128,1536]{1,0:T(8,128)(2,1)S(1)}, u32[]{:S(2)}, u32[]{:S(2)}) collective-permute-start(bf16[128,1536]{1,0:T(8,128)(2,1)S(1)} %add_convert_fusion.6), channel_id=1, source_target_pairs={{0,1},{1,0},{2,3},{3,2},{4,5},{5,4},{6,7},{7,6},{8,9},{9,8},{10,11... | collective-permute-start | bytes 1179656 | tf_op jit(solution)/shard_map/ppermute | solution.py:1272
  345.0 87.9 %reduce-scatter.17.cloned.1.call-start = ((), (), s32[]{:S(2)}) async-start(), calls=%async_computation.7 | async-start | bytes 1966080
  355.1 18.5 %collective-permute-start.46 = (f32[128,768]{1,0:T(8,128)S(1)}, f32[128,768]{1,0:T(8,128)S(1)}, u32[]{:S(2)}, u32[]{:S(2)}) collective-permute-start(f32[128,768]{1,0:T(8,128)S(1)} %get-tuple-element.146), channel_id=1, source_target_pairs={{4,0},{5,1},{6,2},{7,3},{12,8},{13,9},{14,10},{15,11},{20,16},{21,... | collective-permute-start | bytes 1179656 | tf_op jit(solution)/shard_map/ppermute | solution.py:1218
  380.4 17.0 %collective-permute-start.61 = (bf16[512,1536]{1,0:T(8,128)(2,1)S(1)}, bf16[512,1536]{1,0:T(8,128)(2,1)S(1)}, u32[]{:S(2)}, u32[]{:S(2)}) collective-permute-start(bf16[512,1536]{1,0:T(8,128)(2,1)S(1)} %copy-done.4), channel_id=1, source_target_pairs={{0,16},{16,0},{1,17},{17,1},{2,18},{18,2},{3,19},{19,3},{4,20},{20... | collective-permute-start | bytes 4718600 | tf_op jit(solution)/shard_map/ppermute | solution.py:1213
  401.9 92.4 %all-reduce.12.cloned.1.call-start = ((), (), s32[]{:S(2)}) async-start(), calls=%async_computation.4 | async-start | bytes 3145728 | tf_op jit(solution)/shard_map/psum | solution.py:1479
  403.2 13.3 %collective-permute-start.67 = (bf16[512,1536]{1,0:T(8,128)(2,1)S(1)}, bf16[512,1536]{1,0:T(8,128)(2,1)}, u32[]{:S(2)}, u32[]{:S(2)}) collective-permute-start(bf16[512,1536]{1,0:T(8,128)(2,1)S(1)} %copy-done.13), channel_id=1, source_target_pairs={{0,16},{16,0},{1,17},{17,1},{2,18},{18,2},{3,19},{19,3},{4,20},{20... | collective-permute-start | bytes 4718600 | tf_op jit(solution)/shard_map/ppermute | solution.py:1213
  416.4 192.8 %all-reduce.14.cloned.1.call-start = ((), (), s32[]{:S(2)}) async-start(), calls=%async_computation.9 | async-start | bytes 1572864 | tf_op jit(solution)/shard_map/psum | solution.py:1467
  433.0 178.5 %reduce-scatter.15.cloned.1.call-start = ((), (), s32[]{:S(2)}) async-start(), calls=%async_computation.6 | async-start | bytes 4423680
  445.0 166.5 %reduce-scatter.13.cloned.1.call-start = ((), (), s32[]{:S(2)}) async-start(), calls=%async_computation.5 | async-start | bytes 4423680
  446.9 12.1 %collective-permute-start.48 = (bf16[128,1536]{1,0:T(8,128)(2,1)S(1)}, bf16[128,1536]{1,0:T(8,128)(2,1)S(1)}, u32[]{:S(2)}, u32[]{:S(2)}) collective-permute-start(bf16[128,1536]{1,0:T(8,128)(2,1)S(1)} %get-tuple-element.215), channel_id=1, source_target_pairs={{0,1},{1,0},{2,3},{3,2},{4,5},{5,4},{6,7},{7,6},{8,9},{9,8},{10,11... | collective-permute-start | bytes 1179656 | tf_op jit(solution)/shard_map/ppermute | solution.py:1269
  448.5 37.1 %collective-permute-start.51 = (bf16[128,1536]{1,0:T(8,128)(2,1)S(1)}, bf16[128,1536]{1,0:T(8,128)(2,1)S(1)}, u32[]{:S(2)}, u32[]{:S(2)}) collective-permute-start(bf16[128,1536]{1,0:T(8,128)(2,1)S(1)} %get-tuple-element.216), channel_id=1, source_target_pairs={{0,1},{1,0},{2,3},{3,2},{4,5},{5,4},{6,7},{7,6},{8,9},{9,8},{10,11... | collective-permute-start | bytes 1179656 | tf_op jit(solution)/shard_map/ppermute | solution.py:1269
  449.0 80.0 %collective-permute-start.64 = (bf16[512,384]{1,0:T(8,128)(2,1)}, bf16[512,384]{1,0:T(8,128)(2,1)}, u32[]{:S(2)}, u32[]{:S(2)}) collective-permute-start(bf16[512,384]{1,0:T(8,128)(2,1)} %get-tuple-element.168), channel_id=1, source_target_pairs={{0,16},{16,0},{1,17},{17,1},{2,18},{18,2},{3,19},{19,3},{4,20},{20... | collective-permute-start | bytes 1179656 | tf_op jit(solution)/shard_map/ppermute | solution.py:1213
  449.0 80.0 %collective-permute-start.63 = (bf16[512,1536]{1,0:T(8,128)(2,1)S(1)}, bf16[512,1536]{1,0:T(8,128)(2,1)}, u32[]{:S(2)}, u32[]{:S(2)}) collective-permute-start(bf16[512,1536]{1,0:T(8,128)(2,1)S(1)} %copy-done.63), channel_id=1, source_target_pairs={{0,16},{16,0},{1,17},{17,1},{2,18},{18,2},{3,19},{19,3},{4,20},{20... | collective-permute-start | bytes 4718600 | tf_op jit(solution)/shard_map/ppermute | solution.py:1213
  488.1 38.2 %collective-permute-start.49 = (bf16[128,1536]{1,0:T(8,128)(2,1)}, bf16[128,1536]{1,0:T(8,128)(2,1)}, u32[]{:S(2)}, u32[]{:S(2)}) collective-permute-start(bf16[128,1536]{1,0:T(8,128)(2,1)} %get-tuple-element.213), channel_id=1, source_target_pairs={{0,2},{2,0},{1,3},{3,1},{4,6},{6,4},{5,7},{7,5},{8,10},{10,8},{9,1... | collective-permute-start | bytes 1179656 | tf_op jit(solution)/shard_map/ppermute | solution.py:1270
  499.0 100.7 %collective-permute-start.37 = (f32[512,1536]{1,0:T(8,128)}, f32[512,1536]{1,0:T(8,128)}, u32[]{:S(2)}, u32[]{:S(2)}) collective-permute-start(f32[512,1536]{1,0:T(8,128)} %add_select_fusion), channel_id=1, source_target_pairs={{0,16},{16,0},{1,17},{17,1},{2,18},{18,2},{3,19},{19,3},{4,20},{20... | collective-permute-start | bytes 9437192 | tf_op jit(solution)/shard_map/ppermute | solution.py:1213
  499.0 40.9 %collective-permute-start.52 = (bf16[128,1536]{1,0:T(8,128)(2,1)}, bf16[128,1536]{1,0:T(8,128)(2,1)}, u32[]{:S(2)}, u32[]{:S(2)}) collective-permute-start(bf16[128,1536]{1,0:T(8,128)(2,1)} %get-tuple-element.214), channel_id=1, source_target_pairs={{0,2},{2,0},{1,3},{3,1},{4,6},{6,4},{5,7},{7,5},{8,10},{10,8},{9,1... | collective-permute-start | bytes 1179656 | tf_op jit(solution)/shard_map/ppermute | solution.py:1270
  528.2 18.1 %collective-permute-start.50 = (bf16[128,1536]{1,0:T(8,128)(2,1)}, bf16[128,1536]{1,0:T(8,128)(2,1)}, u32[]{:S(2)}, u32[]{:S(2)}) collective-permute-start(bf16[128,1536]{1,0:T(8,128)(2,1)} %add_convert_fusion.4), channel_id=1, source_target_pairs={{0,1},{1,0},{2,3},{3,2},{4,5},{5,4},{6,7},{7,6},{8,9},{9,8},{10,11... | collective-permute-start | bytes 1179656 | tf_op jit(solution)/shard_map/ppermute | solution.py:1272
  541.3 24.7 %collective-permute-start.53 = (bf16[128,1536]{1,0:T(8,128)(2,1)S(1)}, bf16[128,1536]{1,0:T(8,128)(2,1)S(1)}, u32[]{:S(2)}, u32[]{:S(2)}) collective-permute-start(bf16[128,1536]{1,0:T(8,128)(2,1)S(1)} %add_convert_fusion.2), channel_id=1, source_target_pairs={{0,1},{1,0},{2,3},{3,2},{4,5},{5,4},{6,7},{7,6},{8,9},{9,8},{10,11... | collective-permute-start | bytes 1179656 | tf_op jit(solution)/shard_map/ppermute | solution.py:1272
  571.3 34.2 %collective-permute-start.54 = (f32[512,1536]{1,0:T(8,128)S(1)}, f32[512,1536]{1,0:T(8,128)S(1)}, u32[]{:S(2)}, u32[]{:S(2)}) collective-permute-start(f32[512,1536]{1,0:T(8,128)S(1)} %broadcast_select_fusion), channel_id=1, source_target_pairs={{0,16},{16,0},{1,17},{17,1},{2,18},{18,2},{3,19},{19,3},{4,20},{20... | collective-permute-start | bytes 9437192 | tf_op jit(solution)/shard_map/ppermute | solution.py:1213
  (165 other events, 2217.3 us)
Sparse Core Ops, SparseCore 0:
  345.1 38.4 reduce-scatter.18
  402.0 30.9 reduce-scatter.16
  445.1 47.2 reduce-scatter.14
  540.1 49.2 reduce-scatter.12
Sparse Core Ops, SparseCore 1:
  416.5 77.7 all-reduce.11
  496.5 68.9 all-reduce.13

commit v2 on v1

--- a/solution.py
+++ b/solution.py
@@ -19,7 +19,6 @@
 HIGH = lax.Precision.HIGHEST
 F32 = jnp.float32
 BF16 = jnp.bfloat16
-VMEM_BYTES = 24 * 1024 * 1024
 
 NT = (((1,), (1,)), ((), ()))
 TN = (((0,), (0,)), ((), ()))
@@ -115,91 +114,226 @@
 
 
 def anywhere(count):
-    return [pl.BlockSpec(memory_space=pl.ANY)] * count
-
-
-def params_of():
-    return pltpu.CompilerParams(dimension_semantics=("arbitrary",), vmem_limit_bytes=VMEM_BYTES)
+    return [pl.BlockSpec(memory_space=pltpu.HBM)] * count
+
+
+def params_of(mebibytes):
+    return pltpu.CompilerParams(
+        dimension_semantics=("arbitrary",), vmem_limit_bytes=mebibytes * 1024 * 1024
+    )
 
 
 def shape(*dims, dtype=F32):
     return jax.ShapeDtypeStruct(dims, dtype)
 
 
+CORE, FIRST, ODD, RIGHT, ALONG_X, ALONG_Y = range(6)
+
+
+def ordered_call(kernel, ahead, in_specs, **options):
+    count, extra = len(in_specs), len(ahead)
+
+    def body(*refs):
+        kernel(*refs[:count], *refs[count + extra :])
+
+    call = pl.pallas_call(
+        body, in_specs=list(in_specs) + [pl.BlockSpec(memory_space=pl.ANY)] * extra, **options
+    )
+    return lambda *operands: call(*operands, *ahead)
+
+
 def cost(flops, moved):
-    return pl.CostEstimate(flops=int(flops), bytes_accessed=int(moved), transcendentals=0)
-
-
-def weight_copies(where_ref, refs, buffer, sems):
-    first, core = where_ref[1], where_ref[2]
+    return pl.CostEstimate(flops=1, bytes_accessed=1, transcendentals=0)
+
+
+def weight_copies(spec, where_ref, refs, buffer, sems, held):
+    first, core = where_ref[FIRST], where_ref[CORE]
+    _, near, (far_start, far_size) = spec
     rows = buffer.shape[0] // 2
-    width = buffer.shape[1]
     near_at = pl.ds(pl.multiple_of((1 - first) * rows, rows), rows)
     far = first * rows
     step = rows // 2
-    *near, far_mine, far_other = refs
-    pairs = []
+    copies = []
     column = 0
-    for (start, size), held, other in near:
-        part = buffer.at[near_at, column : column + size]
-        sem = sems.at[len(pairs)]
-        pairs.append(
-            (
-                pltpu.make_async_copy(held.at[:, start : start + size], part, sem),
-                pltpu.make_async_copy(other.at[:, start : start + size], part, sem),
+    for n, (start, size) in enumerate(near):
+        copies.append(
+            pltpu.make_async_copy(
+                refs[2 * n if held else 2 * n + 1].at[:, start : start + size],
+                buffer.at[near_at, column : column + size],
+                sems.at[len(copies)],
             )
         )
         column += size
-    for ref, which in ((far_mine, core), (far_other, 1 - core)):
+    for ref, which in ((refs[-2], core), (refs[-1], 1 - core)):
         part = buffer.at[pl.ds(pl.multiple_of(far + which * step, step), step)]
-        copy = pltpu.make_async_copy(ref, part, sems.at[len(pairs)])
-        pairs.append((copy, copy))
-    return pairs
-
-
-def start_weights(where_ref, refs, buffer, sems):
-    pairs = weight_copies(where_ref, refs, buffer, sems)
-
-    @pl.when(where_ref[0] == 1)
-    def _():
-        for held, _ in pairs:
-            held.start()
-
-    @pl.when(where_ref[0] == 0)
-    def _():
-        for _, other in pairs:
-            other.start()
-
-
-def wait_weights(where_ref, refs, buffer, sems):
-    for held, _ in weight_copies(where_ref, refs, buffer, sems):
-        held.wait()
-
-
-def load_weights(where_ref, refs, buffer, sems):
-    start_weights(where_ref, refs, buffer, sems)
-    wait_weights(where_ref, refs, buffer, sems)
-
-
-def front_refs(refs):
-    main, main_other, rest, rest_other, mine, other = refs
-    width = main.shape[1] // 2
-    return ((width, width), main, main_other), ((0, rest.shape[1]), rest, rest_other), mine, other
-
-
-def gate_refs(refs):
-    main, main_other, mine, other = refs
-    return ((0, main.shape[1] // 2), main, main_other), mine, other
-
-
-def out_refs(refs):
-    held, held_other, mine, other = refs
-    return ((0, held.shape[1]), held, held_other), mine, other
+        source = ref.at[:, far_start : far_start + far_size]
+        copies.append(pltpu.make_async_copy(source, part, sems.at[len(copies)]))
+    return copies
+
+
+def start_weights(spec, where_ref, refs, buffer, sems):
+    for held in (True, False):
+
+        @pl.when((where_ref[CORE] == spec[0]) == held)
+        def _():
+            for copy in weight_copies(spec, where_ref, refs, buffer, sems, held):
+                copy.start()
+
+
+def wait_weights(spec, where_ref, refs, buffer, sems):
+    for copy in weight_copies(spec, where_ref, refs, buffer, sems, True):
+        copy.wait()
+
+
+def load_weights(spec, where_ref, refs, buffer, sems):
+    start_weights(spec, where_ref, refs, buffer, sems)
+    wait_weights(spec, where_ref, refs, buffer, sems)
 
 
 def weight_scratch(weights):
-    rows, width = weights[-1].shape
-    return [pltpu.VMEM((4 * rows, width), BF16), pltpu.SemaphoreType.DMA((4,))]
+    (_, _, (_, width)), arrays = weights
+    return [pltpu.VMEM((2 * arrays[0].shape[0], width), BF16), pltpu.SemaphoreType.DMA((4,))]
+
+
+def pieces_kernel(layer, parts, where_ref, *refs):
+    out_ref, sems = refs[-2:]
+    rows = out_ref.shape[0]
+    mine = pl.ds(pl.multiple_of(where_ref[CORE] * rows, rows), rows)
+
+    def copies(held):
+        column = 0
+        for n, (array, start, size) in enumerate(parts):
+            source = refs[2 * array if held else 2 * array + 1]
+            yield pltpu.make_async_copy(
+                source.at[mine, start : start + size], out_ref.at[:, column : column + size], sems.at[n]
+            )
+            column += size
+
+    for held in (True, False):
+
+        @pl.when((where_ref[CORE] == layer) == held)
+        def _():
+            for copy in copies(held):
+                copy.start()
+
+    for copy in copies(True):
+        copy.wait()
+
+
+def pieces_call(where, layer, parts, arrays, *ahead):
+    rows = arrays[0].shape[0] // 2
+    total = sum(size for _, _, size in parts)
+    return ordered_call(
+        functools.partial(pieces_kernel, layer, parts),
+        ahead,
+        in_specs=[scalars_of()] + anywhere(len(arrays)),
+        out_specs=pl.BlockSpec(memory_space=pltpu.VMEM),
+        out_shape=shape(rows, total, dtype=BF16),
+        scratch_shapes=[pltpu.SemaphoreType.DMA((len(parts),))],
+        compiler_params=pltpu.CompilerParams(vmem_limit_bytes=8 * 1024 * 1024),
+        cost_estimate=cost(0, 4 * rows * total),
+        name="pieces",
+    )(where, *arrays)
+
+
+def joined(where_ref, refs, at, digits=(ODD, RIGHT)):
+    quarter = refs[0].shape[0]
+    rows = []
+    for n in range(at.start // quarter, at.stop // quarter):
+        half, place = divmod(n, 2)
+        own, other = refs[2 * half][...].astype(F32), refs[2 * half + 1][...].astype(F32)
+        rows.append(jnp.where(where_ref[digits[half]] == place, own, other))
+    return rows[0] if len(rows) == 1 else jnp.concatenate(rows, axis=0)
+
+
+def put_quarters(where_ref, value, refs, digits=(ODD, RIGHT)):
+    quarter = value.shape[0] // 4
+    for half in range(2):
+        digit = where_ref[digits[half]]
+        first = value[2 * half * quarter : (2 * half + 1) * quarter]
+        second = value[(2 * half + 1) * quarter : (2 * half + 2) * quarter]
+        refs[2 * half][...] = jnp.where(digit == 1, first, second).astype(refs[2 * half].dtype)
+        refs[2 * half + 1][...] = jnp.where(digit == 1, second, first).astype(refs[2 * half + 1].dtype)
+
+
+def quarter_shapes(length, model, kind):
+    return [shape(length // 4, model, dtype=kind), shape(length // 4, model)] * 2
+
+
+def merge_kernel(*refs):
+    count = len(refs) // 3
+    for a_ref, b_ref, out_ref in zip(refs[:count], refs[count : 2 * count], refs[2 * count :]):
+        out_ref[...] = (a_ref[...].astype(F32) + b_ref[...].astype(F32)).astype(out_ref.dtype)
+
+
+def merge_call(firsts, seconds, kind, *ahead):
+    return ordered_call(
+        merge_kernel,
+        ahead,
+        in_specs=[pl.BlockSpec(memory_space=pltpu.VMEM)] * (2 * len(firsts)),
+        out_specs=[pl.BlockSpec(memory_space=pltpu.VMEM)] * len(firsts),
+        out_shape=[shape(*a.shape, dtype=kind) for a in firsts],
+        compiler_params=pltpu.CompilerParams(vmem_limit_bytes=10 * 1024 * 1024),
+        cost_estimate=cost(0, 0),
+        name="merge",
+    )(*firsts, *seconds)
+
+
+def hold_kernel(*refs):
+    count = len(refs) // 2
+    for in_ref, out_ref in zip(refs[:count], refs[count:]):
+        out_ref[...] = in_ref[...]
+
+
+def hold_call(arrays, *ahead):
+    return ordered_call(
+        hold_kernel,
+        ahead,
+        in_specs=[pl.BlockSpec(memory_space=pltpu.VMEM)] * len(arrays),
+        out_specs=[pl.BlockSpec(memory_space=pltpu.VMEM)] * len(arrays),
+        out_shape=[shape(*v.shape, dtype=v.dtype) for v in arrays],
+        compiler_params=pltpu.CompilerParams(vmem_limit_bytes=12 * 1024 * 1024),
+        cost_estimate=cost(0, 0),
+        name="hold",
+    )(*arrays)
+
+
+def vector_kernel(mask_ref, a_ref, b_ref, c_ref, d_ref, out_ref):
+    total = a_ref[...] + b_ref[...] + c_ref[...] + d_ref[...]
+    out_ref[...] = jnp.where(mask_ref[...] > 0.0, total, a_ref[...])
+
+
+def vector_call(mask, values):
+    return pl.pallas_call(
+        vector_kernel,
+        in_specs=[pl.BlockSpec(memory_space=pltpu.VMEM)] * 5,
+        out_specs=pl.BlockSpec(memory_space=pltpu.VMEM),
+        out_shape=shape(*mask.shape),
+        compiler_params=pltpu.CompilerParams(vmem_limit_bytes=4 * 1024 * 1024),
+        cost_estimate=cost(0, 0),
+        name="vector",
+    )(mask, *values)
+
+
+def join_kernel(where_ref, x_ref, t0, o0, t1, o1, out_ref):
+    length = x_ref.shape[0]
+    rows = min(SPAN, length)
+    for r in range(length // rows):
+        at = slice(r * rows, (r + 1) * rows)
+        out_ref[at, :] = x_ref[at, :] + joined(where_ref, (t0, o0, t1, o1), at, (ODD, ODD))
+
+
+def join_call(where, x, quarters, *ahead):
+    return ordered_call(
+        join_kernel,
+        ahead,
+        in_specs=[scalars_of()] + [pl.BlockSpec(memory_space=pltpu.VMEM)] * 5,
+        out_specs=pl.BlockSpec(memory_space=pltpu.VMEM),
+        out_shape=shape(*x.shape),
+        compiler_params=pltpu.CompilerParams(vmem_limit_bytes=16 * 1024 * 1024),
+        cost_estimate=cost(0, 0),
+        name="join",
+    )(where, x, *quarters)
 
 
 TAPS, BIAS, SKIP, GATED, NORM, STEP, DECAY, PACK = 0, 4, 8, 9, 10, 12, 13, 16
@@ -226,6 +360,7 @@
 
 
 def front_kernel(
+    spec,
     where_ref,
     x_ref,
     halo_ref,
@@ -238,6 +373,26 @@
     w3,
     w4,
     w5,
+    *refs,
+):
+    if spec[0] == 1:
+        quarters, refs = refs[:4], refs[4:]
+    else:
+        quarters = None
+    front_body(spec, where_ref, x_ref, halo_ref, tok_ref, pack_ref, spread_ref, (w0, w1, w2, w3, w4, w5), quarters, *refs)
+
+
+def front_body(
+    spec,
+    where_ref,
+    x_ref,
+    halo_ref,
+    tok_ref,
+    pack_ref,
+    spread_ref,
+    held,
+    quarters,
+    sum_ref,
     normed_ref,
     inv_ref,
     pre_ref,
@@ -261,11 +416,10 @@
     length, model = x_ref.shape
     both = width + 2 * NSTATE
     chunk = pl.program_id(0)
-    held = front_refs((w0, w1, w2, w3, w4, w5))
 
     @pl.when(chunk == 0)
     def _():
-        start_weights(where_ref, held, weights, sems)
+        start_weights(spec, where_ref, held, weights, sems)
         gain = norm_row(pack_ref, model // 2)
 
         def normalize(v):
@@ -274,11 +428,15 @@
 
         for r in range(length // rows):
             at = slice(r * rows, (r + 1) * rows)
-            normed, inv = normalize(x_ref[at, :].astype(F32))
+            x = x_ref[at, :].astype(F32)
+            if quarters is not None:
+                x = x + joined(where_ref, quarters, at)
+                sum_ref[at, :] = x
+            normed, inv = normalize(x)
             normed_ref[at, :] = normed
             inv_ref[at, :] = jnp.broadcast_to(inv, (rows, LANES))
         halo, _ = normalize(halo_ref[...].astype(F32))
-        wait_weights(where_ref, held, weights, sems)
+        wait_weights(spec, where_ref, held, weights, sems)
         ext[0:8, :] = mm(halo, weights[:, :both])
         cols[...] = mm(normed_ref[...], weights[...])
         state[...] = jnp.zeros_like(state)
@@ -326,15 +484,16 @@
     end_rate_ref[...] = new_total
 
 
-def front_call(where, x, halo, tok, pack, spread_matrix, weights):
+def front_call(where, x, halo, tok, pack, spread_matrix, weights, quarters, *ahead):
     length, model = x.shape
-    all_width = weights[-1].shape[1]
+    all_width = weights[0][2][1]
     both = all_width - LANES
     width = both - 2 * NSTATE
     rows = min(SPAN, length)
     chunks = length // rows
-    return pl.pallas_call(
-        front_kernel,
+    return ordered_call(
+        functools.partial(front_kernel, weights[0]),
+        ahead,
         grid=(chunks,),
         in_specs=[
             scalars_of(),
@@ -344,8 +503,10 @@
             whole_of(PACK, both),
             whole_of(2 * LANES, width),
         ]
-        + anywhere(6),
+        + anywhere(6)
+        + [whole_of(length // 4, model)] * len(quarters),
         out_specs=[
+            whole_of(length, model) if quarters else whole_of(8, model),
             whole_of(length, model),
             whole_of(length, LANES),
             chunk_of(rows, both),
@@ -360,6 +521,7 @@
             whole_of(8, LANES),
         ],
         out_shape=[
+            shape(length, model) if quarters else shape(8, model),
             shape(length, model, dtype=BF16),
             shape(length, LANES),
             shape(length, both),
@@ -380,38 +542,39 @@
             pltpu.VMEM((NSTATE, width), F32),
             pltpu.VMEM((8, LANES), F32),
         ],
-        compiler_params=params_of(),
+        compiler_params=params_of(32),
         cost_estimate=cost(2 * length * model * all_width, 24 * length * width),
         name="front",
-    )(where, x, halo, tok, pack, spread_matrix, *weights)
-
-
-def project_kernel(kind, where_ref, a_ref, w0, w1, w2, w3, out_ref, weights, sems):
+    )(where, x, halo, tok, pack, spread_matrix, *weights[1], *quarters)
+
+
+def project_kernel(spec, where_ref, a_ref, w0, w1, w2, w3, out_ref, weights, sems):
     tile = out_ref.shape[1]
 
     @pl.when(pl.program_id(0) == 0)
     def _():
-        load_weights(where_ref, kind((w0, w1, w2, w3)), weights, sems)
+        load_weights(spec, where_ref, (w0, w1, w2, w3), weights, sems)
 
     at = pl.ds(pl.multiple_of(pl.program_id(0) * tile, tile), tile)
     out_ref[...] = mm(a_ref[...], weights[:, at])
 
 
-def project_call(where, a, kind, weights):
+def project_call(where, a, weights, *ahead):
     length, model = a.shape
-    width = weights[-1].shape[1]
+    width = weights[0][2][1]
     tile = 2 * LANES
-    return pl.pallas_call(
-        functools.partial(project_kernel, kind),
+    return ordered_call(
+        functools.partial(project_kernel, weights[0]),
+        ahead,
         grid=(width // tile,),
         in_specs=[scalars_of(), whole_of(length, model)] + anywhere(4),
         out_specs=pl.BlockSpec((length, tile), lambda n: (0, n)),
         out_shape=shape(length, width),
         scratch_shapes=weight_scratch(weights),
-        compiler_params=params_of(),
+        compiler_params=params_of(12),
         cost_estimate=cost(2 * length * model * width, 4 * length * width),
         name="project",
-    )(where, a, *weights)
+    )(where, a, *weights[1])
 
 
 def mix_kernel(conv_x_ref, conv_s_ref, step_ref, cum_ref, entry_ref, spread_ref, y_ref):
@@ -440,11 +603,12 @@
         )
 
 
-def mix_call(conv_x, conv_s, step, cum, entry, spread_matrix):
+def mix_call(conv_x, conv_s, step, cum, entry, spread_matrix, *ahead):
     length, width = conv_x.shape
     rows = min(SPAN, length)
-    return pl.pallas_call(
+    return ordered_call(
         mix_kernel,
+        ahead,
         grid=(length // rows,),
         in_specs=[
             chunk_of(rows, width),
@@ -456,7 +620,7 @@
         ],
         out_specs=chunk_of(rows, width),
         out_shape=shape(length, width),
-        compiler_params=params_of(),
+        compiler_params=params_of(12),
         cost_estimate=cost(16 * length * rows * width, 12 * length * width),
         name="mix",
     )(conv_x, conv_s, step, cum, entry, spread_matrix)
@@ -522,7 +686,7 @@
         + [chunk_of(rows, width)] * len(grad_scaled),
         out_specs=[chunk_of(rows, width), chunk_of(rows, width), lanes_of(rows)],
         out_shape=[shape(length, width), shape(length, width), shape(8, length)],
-        compiler_params=params_of(),
+        compiler_params=params_of(12),
         cost_estimate=cost(4 * length * NSTATE * width, 28 * length * width),
         name="gate",
     )(y, z, conv_x, conv_s, cum, rate, entry, pack, spread_matrix, *grad_scaled)
@@ -534,79 +698,91 @@
 
 
 def out_kernel(
-    where_ref, gated_ref, sums_ref, pack_ref, w0, w1, w2, w3, low_ref, other_ref, branch_ref, weights, sems, full
+    spec, where_ref, gated_ref, sums_ref, pack_ref, w0, w1, w2, w3, low_ref, g0, k0, g1, k1, edge_ref, weights, sems
 ):
-    tile = branch_ref.shape[1]
+    tile = edge_ref.shape[1]
     length, width = gated_ref.shape
-    half = width // 2
 
     @pl.when(pl.program_id(0) == 0)
     def _():
-        start_weights(where_ref, out_refs((w0, w1, w2, w3)), weights, sems)
+        start_weights(spec, where_ref, (w0, w1, w2, w3), weights, sems)
         gain = pack_ref[GATED : GATED + 1, :width]
         rows = min(SPAN, length)
         for r in range(length // rows):
             at = slice(r * rows, (r + 1) * rows)
             inv = lax.rsqrt(columns(sums_ref[:, at])[:, 0:1] * (1.0 / INNER) + EPS)
-            full[at, :] = (gated_ref[at, :] * inv * gain).astype(BF16)
-        low_ref[...] = full[:, pl.ds(pl.multiple_of(where_ref[2] * half, LANES), half)]
-        other_ref[...] = full[:, pl.ds(pl.multiple_of((1 - where_ref[2]) * half, LANES), half)]
-        wait_weights(where_ref, out_refs((w0, w1, w2, w3)), weights, sems)
+            low_ref[at, :] = (gated_ref[at, :] * inv * gain).astype(BF16)
+        wait_weights(spec, where_ref, (w0, w1, w2, w3), weights, sems)
 
     at = pl.ds(pl.multiple_of(pl.program_id(0) * tile, tile), tile)
-    branch_ref[...] = mm(full[...], weights[at, :], NT)
-
-
-def out_call(where, gated, sums, pack, weights):
+    branch = mm(low_ref[...], weights[at, :], NT)
+    put_quarters(where_ref, branch, (g0, k0, g1, k1), (ODD, (RIGHT, ODD)[spec[0]]))
+    edge_ref[...] = branch[length - 8 :]
+
+
+def out_call(where, gated, sums, pack, weights, kind, *ahead):
     length, width = gated.shape
-    model = 4 * weights[-1].shape[0]
+    model = 2 * weights[1][0].shape[0]
     tile = model // 4
-    half = width // 2
-    return pl.pallas_call(
-        out_kernel,
+    return ordered_call(
+        functools.partial(out_kernel, weights[0]),
+        ahead,
         grid=(model // tile,),
         in_specs=[scalars_of(), whole_of(length, width), whole_of(8, length), whole_of(*pack.shape)]
         + anywhere(4),
         out_specs=[
-            whole_of(length, half),
-            whole_of(length, half),
-            pl.BlockSpec((length, tile), lambda n: (0, n)),
-        ],
+            whole_of(length, width),
+        ]
+        + [pl.BlockSpec((length // 4, tile), lambda n: (0, n))] * 4
+        + [pl.BlockSpec((8, tile), lambda n: (0, n))],
         out_shape=[
-            shape(length, half, dtype=BF16),
-            shape(length, half, dtype=BF16),
-            shape(length, model),
-        ],
-        scratch_shapes=weight_scratch(weights) + [pltpu.VMEM((length, width), BF16)],
-        compiler_params=params_of(),
+            shape(length, width, dtype=BF16),
+        ]
+        + quarter_shapes(length, model, kind)
+        + [shape(8, model)],
+        scratch_shapes=weight_scratch(weights),
+        compiler_params=params_of(14),
         cost_estimate=cost(2 * length * model * width, 8 * length * width),
         name="out",
-    )(where, gated, sums, pack, *weights)
-
-
-def finish_kernel(last, where_ref, grad_ref, g_ref, x_ref, inv_ref, pack_ref, *refs):
-    rows, model = grad_ref.shape
+    )(where, gated, sums, pack, *weights[1])
+
+
+def finish_kernel(spec, where_ref, g_ref, x_ref, inv_ref, pack_ref, t0, o0, t1, o1, *refs):
+    rows, model = g_ref.shape
     chunk = pl.program_id(0)
+    *refs, grad = refs
+
+    @pl.when(chunk == 0)
+    def _():
+        for r in range(grad.shape[0] // rows):
+            at = slice(r * rows, (r + 1) * rows)
+            grad[at, :] = joined(where_ref, (t0, o0, t1, o1), at).astype(BF16)
+
     gain = norm_row(pack_ref, model // 2)
     x = x_ref[...].astype(F32)
     inv = inv_ref[:, 0:1]
-    weighted = grad_ref[...].astype(F32) * gain
+    weighted = grad[pl.ds(pl.multiple_of(chunk * rows, rows), rows), :].astype(F32) * gain
     mean = jnp.mean(weighted * x, axis=-1, keepdims=True)
     result = g_ref[...].astype(F32) + inv * weighted - x * (inv * inv * inv * mean)
-    if last:
+    if spec is None:
         refs[0][...] = result
         return
-    branch_ref, sums_ref, w0, w1, w2, w3, out_ref, low_ref, scaled_ref, new_sums_ref, weights, sems = refs
-    candidates = out_refs((w0, w1, w2, w3))
+    b0, b1, b2, b3, sums_ref, w0, w1, w2, w3, out_ref, low_ref, scaled_ref, new_sums_ref, weights, sems, branch = refs
+    length = branch.shape[0]
+    candidates = (w0, w1, w2, w3)
 
     @pl.when(chunk == 0)
     def _():
-        start_weights(where_ref, candidates, weights, sems)
+        start_weights(spec, where_ref, candidates, weights, sems)
+        for r in range(length // rows):
+            at = slice(r * rows, (r + 1) * rows)
+            branch[at, :] = joined(where_ref, (b0, b1, b2, b3), at)
 
     out_ref[...] = result
     low = result.astype(BF16)
     low_ref[pl.ds(pl.multiple_of(chunk * rows, rows), rows), :] = low
-    dot = jnp.sum(low.astype(F32) * branch_ref[...], axis=1, keepdims=True)
+    here = branch[pl.ds(pl.multiple_of(chunk * rows, rows), rows), :]
+    dot = jnp.sum(low.astype(F32) * here, axis=1, keepdims=True)
     square = columns(sums_ref[...])[:, 0:1]
     dot = dot / lax.rsqrt(square * (1.0 / INNER) + EPS)
     lane = lax.broadcasted_iota(jnp.int32, (rows, LANES), 1)
@@ -615,43 +791,43 @@
 
     @pl.when(chunk == pl.num_programs(0) - 1)
     def _():
-        wait_weights(where_ref, candidates, weights, sems)
+        wait_weights(spec, where_ref, candidates, weights, sems)
         scaled_ref[...] = mm(low_ref[...], weights[...])
 
 
-def finish_call(where, grad, g, x, inv, pack, *more):
-    length, model = grad.shape
+def finish_call(where, quarters, g, x, inv, pack, ahead, branch=None, sums=None, weights=None):
+    length, model = g.shape
     rows = min(SPAN, length)
-    last = not more
     in_specs = [
         scalars_of(),
         chunk_of(rows, model),
         chunk_of(rows, model),
-        chunk_of(rows, model),
         chunk_of(rows, LANES),
         whole_of(*pack.shape),
-    ]
+    ] + [whole_of(length // 4, model)] * 4
     out_specs = [chunk_of(rows, model)]
     out_shape = [shape(length, model)]
-    scratch = []
-    if more:
-        branch, sums, *weights = more
-        width = weights[-1].shape[1]
-        in_specs += [chunk_of(rows, model), lanes_of(rows)] + anywhere(4)
+    scratch = [pltpu.VMEM((length, model), BF16)]
+    more = ()
+    if weights is not None:
+        width = weights[0][2][1]
+        in_specs += [whole_of(length // 4, model)] * 4 + [lanes_of(rows)] + anywhere(4)
         out_specs += [whole_of(length, model), whole_of(length, width), lanes_of(rows)]
         out_shape += [shape(length, model, dtype=BF16), shape(length, width), shape(8, length)]
-        scratch = weight_scratch(weights)
-    return pl.pallas_call(
-        functools.partial(finish_kernel, last),
+        scratch = weight_scratch(weights) + [pltpu.VMEM((length, model), F32)] + scratch
+        more = tuple(branch) + (sums,) + tuple(weights[1])
+    return ordered_call(
+        functools.partial(finish_kernel, None if weights is None else weights[0]),
+        ahead,
         grid=(length // rows,),
         in_specs=in_specs,
         out_specs=out_specs,
         out_shape=out_shape,
         scratch_shapes=scratch,
-        compiler_params=params_of(),
+        compiler_params=params_of(28),
         cost_estimate=cost(length * model * 800, 16 * length * model),
         name="finish",
-    )(where, grad, g, x, inv, pack, *more)
+    )(where, g, x, inv, pack, *quarters, *more)
 
 
 def gate_back_kernel(
@@ -743,7 +919,7 @@
             shape(8, width),
         ],
         scratch_shapes=[pltpu.VMEM((NSTATE, width), F32), pltpu.VMEM((8, LANES), F32)],
-        compiler_params=params_of(),
+        compiler_params=params_of(12),
         cost_estimate=cost(4 * length * NSTATE * width, 28 * length * width),
         name="gate_back",
     )(grad_scaled, comb, z, conv_s, cum, sums, pack, spread_matrix)
@@ -855,15 +1031,16 @@
     decay_ref[...] = kept + after + before
 
 
-def mix_back_call(kept, dmix, adj, consts):
+def mix_back_call(kept, dmix, adj, consts, *ahead):
     conv_x, conv_s, step, cum, _, entry, rate, entry_in = kept
     length, width = conv_x.shape
     rows = min(SPAN, length)
     chunks = length // rows
     spread_matrix, gather_matrix, ones = consts
     head_count = width // HEAD_DIM
-    return pl.pallas_call(
+    return ordered_call(
         mix_back_kernel,
+        ahead,
         grid=(chunks,),
         in_specs=[
             chunk_of(rows, width),
@@ -894,7 +1071,7 @@
             shape(8, width),
         ],
         scratch_shapes=[pltpu.VMEM((rows, head_count * rows), BF16)],
-        compiler_params=params_of(),
+        compiler_params=params_of(14),
         cost_estimate=cost(40 * length * rows * width, 20 * length * width),
         name="mix_back",
     )(conv_x, conv_s, dmix, step, cum, entry, rate, entry_in, adj, spread_matrix, gather_matrix, ones)
@@ -969,14 +1146,15 @@
     small_ref[1:2, :] += jnp.sum(grad_decay * (rate * step), axis=0, keepdims=True)
 
 
-def later_call(kept, dmix, adj_rate, adj_in, parts, pack, consts):
+def later_call(kept, dmix, adj_rate, adj_in, parts, pack, consts, *ahead):
     conv_x, conv_s, step, cum, raw, entry, rate, entry_in = kept
     length, width = conv_x.shape
     rows = min(SPAN, length)
     chunks = length // rows
     spread_matrix, gather_matrix, _ = consts
-    return pl.pallas_call(
+    return ordered_call(
         later_kernel,
+        ahead,
         grid=(chunks,),
         in_specs=[
             chunk_of(rows, width),
@@ -1004,7 +1182,7 @@
             shape(length, LANES, dtype=BF16),
             shape(8, LANES),
         ],
-        compiler_params=params_of(),
+        compiler_params=params_of(14),
         cost_estimate=cost(8 * length * NSTATE * width, 24 * length * width),
         name="later",
     )(
@@ -1028,11 +1206,14 @@
 
 def conv_back_kernel(
     chunks,
+    front_spec,
+    gate_spec,
     where_ref,
     grad_ref,
     pre_ref,
     raw_ref,
     dz_ref,
+    low_ref,
     tok_ref,
     halo_ref,
     halo_tok_ref,
@@ -1053,9 +1234,42 @@
     z1,
     z2,
     z3,
+    *refs,
+):
+    if front_spec[0] == 0:
+        above, refs = refs[0], refs[1:]
+    else:
+        above = None
+    conv_back_body(
+        chunks,
+        front_spec,
+        gate_spec,
+        (where_ref, grad_ref, pre_ref, raw_ref, dz_ref, low_ref, tok_ref, halo_ref, halo_tok_ref, pack_ref, x_ref, inv_ref),
+        (head_ref, skip_ref, gained_ref, gather_ref),
+        (f0, f1, f2, f3, f4, f5),
+        (z0, z1, z2, z3),
+        above,
+        *refs,
+    )
+
+
+def conv_back_body(
+    chunks,
+    front_spec,
+    gate_spec,
+    inputs,
+    vectors,
+    held_front,
+    held_gate,
+    above,
     keep_ref,
     send_ref,
-    part_ref,
+    g0,
+    k0,
+    g1,
+    k1,
+    vector_ref,
+    vector_send_ref,
     small_ref,
     front,
     front_sems,
@@ -1065,19 +1279,18 @@
     ext_tok,
     grads,
 ):
+    where_ref, grad_ref, pre_ref, raw_ref, dz_ref, low_ref, tok_ref, halo_ref, halo_tok_ref, pack_ref, x_ref, inv_ref = inputs
+    head_ref, skip_ref, gained_ref, gather_ref = vectors
     step = pl.program_id(0)
     rows, both = pre_ref.shape
     width = both - 2 * NSTATE
-    half = width // 2
-    tile = part_ref.shape[1]
-    core = where_ref[2]
-    held_front = front_refs((f0, f1, f2, f3, f4, f5))
-    held_gate = gate_refs((z0, z1, z2, z3))
+    tile = g0.shape[1]
+    core = where_ref[CORE]
 
     @pl.when(step == 0)
     def _():
-        start_weights(where_ref, held_front, front, front_sems)
-        start_weights(where_ref, held_gate, gate, gate_sems)
+        start_weights(front_spec, where_ref, held_front, front, front_sems)
+        start_weights(gate_spec, where_ref, held_gate, gate, gate_sems)
         ext[rows : rows + 8, :] = halo_ref[...]
         ext_tok[rows : rows + 8, :] = halo_tok_ref[...]
         small_ref[...] = jnp.zeros_like(small_ref)
@@ -1106,9 +1319,11 @@
         dz = dz_ref[...]
         at = pl.ds(pl.multiple_of((chunks - 1 - step) * rows, rows), rows)
         grads[at, :] = jnp.concatenate([out_x, s_top, raw, dz, s_rest], axis=1)
+        low = low_ref[...]
         none = jnp.zeros((rows, LANES), BF16)
-        for_lower = [dz[:, :half], out_x[:, :half], s_top, s_rest]
-        for_upper = [dz[:, half:], out_x[:, half:], raw, none, none, none]
+        halves_of = [dz, out_x, low, s_top, s_rest]
+        for_lower = [v[:, : v.shape[1] // 2] for v in halves_of] + [raw]
+        for_upper = [v[:, v.shape[1] // 2 :] for v in halves_of] + [none]
 
         @pl.when(core == 0)
         def _():
@@ -1122,8 +1337,8 @@
 
     @pl.when(step == chunks)
     def _():
-        wait_weights(where_ref, held_front, front, front_sems)
-        wait_weights(where_ref, held_gate, gate, gate_sems)
+        wait_weights(front_spec, where_ref, held_front, front, front_sems)
+        wait_weights(gate_spec, where_ref, held_gate, gate, gate_sems)
         skip = gather_heads(skip_ref[...], gather_ref[...])
         small_ref[SKIP : SKIP + 1, :LANES] = skip[0:1, :]
         small_ref[GATED : GATED + 1, :width] = gained_ref[0:1, :]
@@ -1139,23 +1354,33 @@
                 + mm(grads[:, both + LANES : both + LANES + width], gate[at, :], NT)
                 + mm(grads[:, both + LANES + width :], front[at, width:both], NT)
             )
-            part_ref[...] = part
+            put_quarters(where_ref, part, (g0, k0, g1, k1))
             row = jnp.sum(part * (x_ref[...].astype(F32) * inv_ref[:, 0:1]), axis=0, keepdims=True)
             per_row = front.shape[0] // 2 // tile
             place = slice((n % per_row) * tile, (n % per_row + 1) * tile)
             small_ref[NORM + n // per_row : NORM + n // per_row + 1, place] = row
 
+    @pl.when(step == pl.num_programs(0) - 1)
+    def _():
+        if above is None:
+            vector_ref[...] = small_ref[...]
+            vector_send_ref[...] = jnp.zeros_like(vector_send_ref)
+            return
+        small, other = small_ref[...], above[...]
+        vector_ref[...] = jnp.where(core == 0, small, other)
+        vector_send_ref[...] = jnp.where(core == 0, other, small)
+
 
 def conv_back_call(
-    where, grad, pre, grad_raw, dz, tok, halo, halo_tok, pack, x, inv, head, skip, gained, gather_matrix, front, gate
+    where, grad, pre, grad_raw, dz, low, tok, halo, halo_tok, pack, x, inv, head, skip, gained, gather_matrix, front, gate, above, *ahead
 ):
     length, both = pre.shape
     width = both - 2 * NSTATE
-    model = 4 * front[-1].shape[0]
+    model = 2 * front[1][0].shape[0]
     rows = min(SPAN, length)
     chunks = length // rows
     tile = model // 4
-    out_width = width + 4 * NSTATE
+    out_width = 3 * (width // 2) + 2 * NSTATE + LANES
 
     def chunk_spec(size):
         return pl.BlockSpec((rows, size), lambda c: (jnp.maximum(chunks - 1 - c, 0), 0))
@@ -1163,14 +1388,16 @@
     def tile_spec(rows_):
         return pl.BlockSpec((rows_, tile), lambda c: (0, jnp.maximum(c - chunks, 0)))
 
-    return pl.pallas_call(
-        functools.partial(conv_back_kernel, chunks),
+    return ordered_call(
+        functools.partial(conv_back_kernel, chunks, front[0], gate[0]),
+        ahead,
         grid=(chunks + model // tile,),
         in_specs=[
             scalars_of(),
             chunk_spec(both),
             chunk_spec(both),
             chunk_spec(LANES),
+            chunk_spec(width),
             chunk_spec(width),
             chunk_spec(LANES),
             whole_of(8, both),
@@ -1183,30 +1410,221 @@
             whole_of(8, width),
             whole_of(2 * width, LANES),
         ]
-        + anywhere(10),
+        + anywhere(10)
+        + [whole_of(*pack.shape)] * len(above),
         out_specs=[
             chunk_spec(out_width),
             chunk_spec(out_width),
-            tile_spec(length),
-            whole_of(*pack.shape),
-        ],
+        ]
+        + [tile_spec(length // 4)] * 4
+        + [whole_of(*pack.shape)] * 2,
         out_shape=[
             shape(length, out_width, dtype=BF16),
             shape(length, out_width, dtype=BF16),
-            shape(length, model),
-            shape(*pack.shape),
-        ],
-        scratch_shapes=weight_scratch(front)
+        ]
+        + quarter_shapes(length, model, BF16)
+        + [shape(*pack.shape)] * 2,
+        scratch_shapes=[pltpu.VMEM(pack.shape, F32)]
+        + weight_scratch(front)
         + weight_scratch(gate)
         + [
             pltpu.VMEM((rows + 8, both), F32),
             pltpu.VMEM((rows + 8, LANES), F32),
             pltpu.VMEM((length, both + LANES + width + 2 * NSTATE), BF16),
         ],
-        compiler_params=params_of(),
+        compiler_params=params_of(24),
         cost_estimate=cost(4 * length * model * both, 24 * length * width),
         name="conv_back",
-    )(where, grad, pre, grad_raw, dz, tok, halo, halo_tok, pack, x, inv, head, skip, gained, gather_matrix, *front, *gate)
+    )(where, grad, pre, grad_raw, dz, low, tok, halo, halo_tok, pack, x, inv, head, skip, gained, gather_matrix, *front[1], *gate[1], *above)
+
+
+def split_states(total, width):
+    top, rest = halves(total[:, width : width + NSTATE])
+    return jnp.concatenate(
+        [total[:, :width].astype(BF16), top, rest, total[:, width + NSTATE :].astype(BF16)], axis=1
+    )
+
+
+def whole_states(value, width):
+    value = value.astype(F32)
+    states = value[:, width : width + NSTATE] + value[:, width + NSTATE : width + 2 * NSTATE]
+    return jnp.concatenate([value[:, :width], states, value[:, width + 2 * NSTATE :]], axis=1)
+
+
+def block_grads(n0, n1, g0, g1, keep_ref, got_ref):
+    width = keep_ref.shape[1] - 2 * NSTATE - LANES
+    inner = 2 * width // 3
+    mine, theirs = n0[...], n1[...]
+    main = mm(mine, keep_ref[:, :inner], TN) + mm(theirs, got_ref[:, :inner], TN)
+    outer = mm(g0[...].astype(BF16), keep_ref[:, inner:width], TN) + mm(
+        g1[...].astype(BF16), got_ref[:, inner:width], TN
+    )
+    rest = mm(mine, keep_ref[:, width:], TN) + mm(theirs, got_ref[:, width:], TN)
+    states = rest[:, :NSTATE] + rest[:, NSTATE : 2 * NSTATE]
+    return split_states(jnp.concatenate([main, outer, states, rest[:, 2 * NSTATE :]], axis=1), width)
+
+
+def wgrad_plain_kernel(*refs):
+    refs[-1][0] = block_grads(*refs[:-1])
+
+
+def wgrad_relative_kernel(extra, where_ref, *refs):
+    value = block_grads(*refs[:6])
+    first_give, first_keep, second_give, second_keep = refs[6 + extra :]
+    half = value.shape[0] // 2
+    step = pl.program_id(0)
+
+    @pl.when(step < 2)
+    def _():
+        first_give[0] = value[:half]
+
+    @pl.when(step >= 2)
+    def _():
+        first_keep[0] = value[:half]
+
+    @pl.when(step % 2 == 1)
+    def _():
+        second_give[0] = value[half:]
+
+    @pl.when(step % 2 == 0)
+    def _():
+        second_keep[0] = value[half:]
+
+
+def wgrad_call(where, spans, normed, normed_other, g_low, g_other, keep, got, *ahead):
+    length, model = normed.shape
+    size = keep.shape[1]
+    blocks = spans[0] * spans[1]
+    rows = model // blocks
+    operands = (normed, normed_other, g_low, g_other, keep, got)
+    if spans != (2, 2):
+        grid_rows = max(rows, LANES)
+        steps = model // grid_rows
+        return pl.pallas_call(
+            wgrad_plain_kernel,
+            grid=(steps,),
+            in_specs=[pl.BlockSpec((length, grid_rows), lambda b: (0, b))] * 4
+            + [whole_of(*v.shape) for v in operands[4:]],
+            out_specs=pl.BlockSpec((1, grid_rows, size), lambda b: (b, 0, 0)),
+            out_shape=shape(steps, grid_rows, size, dtype=BF16),
+            compiler_params=params_of(20),
+            cost_estimate=cost(0, 0),
+            name="wgrad",
+        )(*operands).reshape(blocks, rows, size)
+
+    def block_index(b, where_ref):
+        x = jnp.where(b < 2, 1 - where_ref[ALONG_X], where_ref[ALONG_X])
+        y = jnp.where(b % 2 == 1, 1 - where_ref[ALONG_Y], where_ref[ALONG_Y])
+        return (0, 2 * x + y)
+
+    def whole(v):
+        return pl.BlockSpec(v.shape, lambda b, where_ref: (0,) * v.ndim)
+
+    maps = [
+        lambda b, where_ref: (jnp.minimum(b, 1), 0, 0),
+        lambda b, where_ref: (jnp.maximum(b - 2, 0), 0, 0),
+        lambda b, where_ref: (1 - b // 2, 0, 0),
+        lambda b, where_ref: (1 - b // 2, 0, 0),
+    ]
+    return pl.pallas_call(
+        functools.partial(wgrad_relative_kernel, len(ahead)),
+        grid_spec=pltpu.PrefetchScalarGridSpec(
+            num_scalar_prefetch=1,
+            grid=(4,),
+            in_specs=[pl.BlockSpec((length, rows), block_index)] * 4
+            + [whole(v) for v in operands[4:]]
+            + [pl.BlockSpec(memory_space=pl.ANY)] * len(ahead),
+            out_specs=[pl.BlockSpec((1, rows // 2, size), m) for m in maps],
+        ),
+        out_shape=[shape(2, rows // 2, size, dtype=BF16)] * 4,
+        compiler_params=params_of(20),
+        cost_estimate=cost(0, 0),
+        name="wgrad",
+    )(where, *operands, *ahead)
+
+
+def turn_kernel(*refs):
+    for n in range(2):
+        keep_ref, got_ref, give_ref, kept_ref = refs[n::2]
+        width = keep_ref.shape[2] - 2 * NSTATE - LANES
+        sums = [whole_states(keep_ref[m], width) + whole_states(got_ref[m], width) for m in range(2)]
+        kept_ref[...] = sums[0]
+        give_ref[...] = split_states(sums[1], width)
+
+
+def turn_call(keeps, gots, *ahead):
+    _, rows, size = keeps[0].shape
+    outputs = ordered_call(
+        turn_kernel,
+        ahead,
+        in_specs=[pl.BlockSpec(memory_space=pltpu.VMEM)] * 4,
+        out_specs=[pl.BlockSpec(memory_space=pltpu.VMEM)] * 4,
+        out_shape=[shape(rows, size, dtype=BF16)] * 2 + [shape(rows, size - NSTATE)] * 2,
+        compiler_params=pltpu.CompilerParams(vmem_limit_bytes=16 * 1024 * 1024),
+        cost_estimate=cost(0, 0),
+        name="turn",
+    )(*keeps, *gots)
+    return outputs[:2], outputs[2:]
+
+
+def summed_kernel(where_ref, first_keep, first_got, second_keep, second_got, *refs):
+    rows = first_keep.shape[0]
+    above, (matrices_ref, steps_ref, *states_refs) = (None, refs) if len(refs) == 3 else (refs[0], refs[1:])
+    width = matrices_ref.shape[1]
+    states = []
+    for at, keep, got in ((slice(0, rows), first_keep, first_got), (slice(rows, 2 * rows), second_keep, second_got)):
+        total = keep[...] + whole_states(got[...], width)
+        matrices_ref[at, :] = total[:, :width].astype(BF16)
+        states.append(total[:, width : width + NSTATE])
+        steps_ref[at, :] = total[:, width + NSTATE :]
+    states = jnp.concatenate(states, axis=0)
+    if above is None:
+        states_refs[0][...] = states
+    else:
+        put_quarters(where_ref, jnp.concatenate([states, above[...]], axis=1), states_refs)
+
+
+def summed_call(where, operands, above, *ahead):
+    rows, size = operands[1].shape
+    width = size - 2 * NSTATE - LANES
+    states = quarter_shapes(2 * rows, 2 * NSTATE, F32) if above else [shape(2 * rows, NSTATE)]
+    return ordered_call(
+        summed_kernel,
+        ahead,
+        in_specs=[scalars_of()] + [pl.BlockSpec(memory_space=pltpu.VMEM)] * (4 + len(above)),
+        out_specs=[pl.BlockSpec(memory_space=pltpu.VMEM)] * (2 + len(states)),
+        out_shape=[
+            shape(2 * rows, width, dtype=BF16),
+            shape(2 * rows, LANES),
+        ]
+        + states,
+        compiler_params=pltpu.CompilerParams(vmem_limit_bytes=16 * 1024 * 1024),
+        cost_estimate=cost(0, 0),
+        name="summed",
+    )(where, *operands, *above)
+
+
+def renorm_kernel(x_ref, pack_ref, out_ref):
+    gain = norm_row(pack_ref, x_ref.shape[1] // 2)
+    x = x_ref[...].astype(F32)
+    inv = lax.rsqrt(jnp.mean(x * x, axis=-1, keepdims=True) + EPS)
+    out_ref[...] = (x * inv * gain).astype(BF16)
+
+
+def renorm_call(x, pack, *ahead):
+    length, model = x.shape
+    rows = min(SPAN, length)
+    return ordered_call(
+        renorm_kernel,
+        ahead,
+        grid=(length // rows,),
+        in_specs=[chunk_of(rows, model), whole_of(*pack.shape)],
+        out_specs=chunk_of(rows, model),
+        out_shape=shape(length, model, dtype=BF16),
+        compiler_params=params_of(10),
+        cost_estimate=cost(0, 0),
+        name="renorm",
+    )(x, pack)
 
 
 def swap(value, axis):
@@ -1226,8 +1644,17 @@
     return lax.psum(value, axis)
 
 
+def sum_given(value, axis):
+    if lax.axis_size(axis) == 2:
+        return swap(value, axis)
+    return lax.psum(value, axis) - value
+
+
 def after(value, *earlier):
-    return lax.optimization_barrier((value,) + earlier)[0]
+    for event in earlier:
+        first = lax.slice(event, (0,) * event.ndim, (1,) * event.ndim).reshape(())
+        value = value + (first.astype(F32) * 0.0).astype(value.dtype)
+    return value
 
 
 def carried_state(state, rate_wide, axis, backward):
@@ -1255,30 +1682,207 @@
     return total
 
 
-def tensor_sum(value, kind, pieces):
-    index = lax.axis_index("tensor")
-    odd = index % 2
-    pair = [(0, 1), (1, 0), (2, 3), (3, 2)]
-    cross = [(0, 2), (2, 0), (1, 3), (3, 1)]
-    rows = value.shape[0] // (2 * pieces)
-    results = []
-    for p in range(pieces):
-        base = 2 * rows * p
-        give = lax.dynamic_slice_in_dim(value, base + (1 - odd) * rows, rows, 0).astype(kind)
-        keep = lax.dynamic_slice_in_dim(value, base + odd * rows, rows, 0)
-        part = (keep + lax.ppermute(give, "tensor", pair).astype(F32)).astype(kind)
-        total = part.astype(F32) + lax.ppermute(part, "tensor", cross).astype(F32)
-        total = total.astype(kind)
-        other = lax.ppermute(total, "tensor", pair)
-        results.append(jnp.where(odd == 0, total, other))
-        results.append(jnp.where(odd == 0, other, total))
-    return jnp.concatenate(results, axis=0)
-
-
-def scatter_sum(value, kind):
-    return lax.psum_scatter(
-        value.astype(kind), ("fsdp", "context"), scatter_dimension=0, tiled=False
-    )
+class TensorSum:
+    NEAR = [(0, 1), (1, 0), (2, 3), (3, 2)]
+    FAR = [(0, 2), (2, 0), (1, 3), (3, 1)]
+    STEPS = ((NEAR, FAR, NEAR), (FAR, NEAR, FAR))
+
+    def __init__(self, pieces):
+        self.pieces = pieces
+        self.given = self._send([give for _, give, _ in pieces], 0)
+        self.kind = pieces[0][1].dtype
+
+    def _send(self, arrays, step):
+        return [
+            lax.ppermute(v, "tensor", self.STEPS[half][step])
+            for (half, _, _), v in zip(self.pieces, arrays)
+        ]
+
+    def _merge(self, firsts, seconds, ahead):
+        if self.kind == jnp.float16:
+            return [(a.astype(F32) + b.astype(F32)).astype(self.kind) for a, b in zip(firsts, seconds)]
+        return merge_call(firsts, seconds, self.kind, *ahead)
+
+    def add(self, *ahead):
+        self.parts = self._merge([keep for _, _, keep in self.pieces], self.given, ahead)
+        return self.parts[-1]
+
+    def hold(self, *ahead):
+        held = hold_call(self.parts, *ahead)
+        self.given = self._send(held, 1)
+        return held[-1]
+
+    def across(self, *ahead):
+        self.add(*ahead)
+        self.given = self._send(self.parts, 1)
+        return self.parts[-1]
+
+    def total(self, *ahead):
+        self.totals = self._merge(self.parts, self.given, ahead)
+        return self.totals[-1]
+
+    def spread(self, *ahead):
+        held = hold_call(self.totals, *ahead)
+        self.others = self._send(held, 2)
+        return held[-1]
+
+    def back(self, *ahead):
+        self.total(*ahead)
+        self.others = self._send(self.totals, 2)
+        return self.totals[-1]
+
+    def quarters(self):
+        return [v for pair in zip(self.totals, self.others) for v in pair]
+
+
+class ScatterSum:
+    def __init__(self, value):
+        self.whole = None
+        if not isinstance(value, (list, tuple)):
+            self.whole = lax.psum_scatter(value, ("fsdp", "context"), scatter_dimension=0, tiled=False)
+            return
+        self.keeps = [value[1], value[3]]
+        self.given = [swap(value[0], "fsdp"), swap(value[2], "context")]
+
+    def turn(self, *ahead):
+        if self.whole is not None:
+            return self.whole
+        gives, self.keeps = turn_call(self.keeps, self.given, *ahead)
+        self.given = [swap(gives[0], "context"), swap(gives[1], "fsdp")]
+        return gives[0]
+
+    def result(self, where, above, *ahead):
+        if self.whole is not None:
+            half = self.whole.shape[0] // 2
+            none = jnp.zeros((half, self.whole.shape[1] - NSTATE), F32)
+            operands = none, self.whole[:half], none, self.whole[half:]
+        else:
+            operands = self.keeps[0], self.given[0], self.keeps[1], self.given[1]
+        return summed_call(where, operands, above, *ahead)
+
+
+def rest_kernel(where_ref, t0, o0, t1, o1, steps0, steps1, out_ref):
+    rows = steps0.shape[0]
+    states = joined(where_ref, (t0, o0, t1, o1), slice(0, rows))
+    out_ref[...] = jnp.concatenate(
+        [states[:, :NSTATE], steps0[...], states[:, NSTATE:], steps1[...]], axis=1
+    )
+
+
+def rest_call(where, quarters, steps0, steps1, *ahead):
+    return ordered_call(
+        rest_kernel,
+        ahead,
+        in_specs=[scalars_of()] + [pl.BlockSpec(memory_space=pltpu.VMEM)] * 6,
+        out_specs=pl.BlockSpec(memory_space=pltpu.VMEM),
+        out_shape=shape(steps0.shape[0], 2 * (NSTATE + LANES)),
+        compiler_params=pltpu.CompilerParams(vmem_limit_bytes=8 * 1024 * 1024),
+        cost_estimate=cost(0, 0),
+        name="rest",
+    )(where, *quarters, steps0, steps1)
+
+
+def matrices_kernel(where_ref, m0, r0, m1, r1, rest, rest_got, main_ref, states_ref, step_ref, out_ref):
+    def put(lower, upper, lower_rest, upper_rest, column):
+        half = main_ref.shape[3] // 2
+        a, b = lower[...].astype(F32), upper[...].astype(F32)
+        main_ref[0, :, 0, :] = jnp.concatenate([a[:, :half], b[:, :half]], axis=1)
+        main_ref[0, :, 1, :] = jnp.concatenate([a[:, half : 2 * half], b[:, half : 2 * half]], axis=1)
+        out_ref[0] = jnp.concatenate([a[:, 2 * half :], b[:, 2 * half :]], axis=1)
+        states = slice(column, column + NSTATE)
+        states_ref[0] = jnp.concatenate([lower_rest[:, states], upper_rest[:, states]], axis=1)
+        step_ref[0] = lower_rest[:, column + NSTATE : column + NSTATE + step_ref.shape[2]]
+
+    @pl.when(where_ref[CORE] == 0)
+    def _():
+        put(m0, r0, rest, rest_got, 0)
+
+    @pl.when(where_ref[CORE] == 1)
+    def _():
+        put(r1, m1, rest_got, rest, NSTATE + LANES)
+
+
+def matrices_call(where, heads, *arrays):
+    rows, columns_ = arrays[0].shape
+    half = columns_ // 3
+    block = rows // 2
+
+    def out_spec(*dims):
+        return pl.BlockSpec((1, block) + dims, lambda r: (0, r) + (0,) * len(dims))
+
+    return pl.pallas_call(
+        matrices_kernel,
+        grid=(2,),
+        in_specs=[scalars_of()] + [pl.BlockSpec((block, v.shape[1]), lambda r: (r, 0)) for v in arrays],
+        out_specs=[out_spec(2, 2 * half), out_spec(2 * NSTATE), out_spec(heads), out_spec(2 * half)],
+        out_shape=[
+            shape(1, rows, 2, 2 * half),
+            shape(1, rows, 2 * NSTATE),
+            shape(1, rows, heads),
+            shape(1, rows, 2 * half),
+        ],
+        compiler_params=params_of(20),
+        cost_estimate=cost(0, 0),
+        name="matrices",
+    )(where, *arrays)
+
+
+def tokens_kernel(where_ref, own0, got0, own1, got1, *refs):
+    out_ref, tick_ref = refs[-2:]
+    tick_ref[...] = jnp.zeros_like(tick_ref)
+    which = pl.program_id(0)
+    core = where_ref[CORE]
+
+    @pl.when(core == 0)
+    def _():
+        @pl.when(which == 0)
+        def _():
+            out_ref[0, 0] = own0[...]
+
+        @pl.when(which == 1)
+        def _():
+            out_ref[0, 0] = got0[...].astype(F32)
+
+    @pl.when(core == 1)
+    def _():
+        @pl.when(which == 0)
+        def _():
+            out_ref[0, 0] = got1[...].astype(F32)
+
+        @pl.when(which == 1)
+        def _():
+            out_ref[0, 0] = own1[...]
+
+
+def tokens_call(where, own0, got0, own1, got1, *ahead):
+    length, model = own0.shape
+    block = length // 2
+
+    def spec(core, which):
+        def index(s, r, where_ref):
+            return (jnp.where((where_ref[CORE] == core) & (s == which), r, 0), 0)
+
+        return pl.BlockSpec((block, model), index)
+
+    return pl.pallas_call(
+        tokens_kernel,
+        grid_spec=pltpu.PrefetchScalarGridSpec(
+            num_scalar_prefetch=1,
+            grid=(2, length // block),
+            in_specs=[spec(0, 0), spec(0, 1), spec(1, 1), spec(1, 0)]
+            + [pl.BlockSpec(memory_space=pl.ANY)] * len(ahead),
+            out_specs=[
+                pl.BlockSpec((1, 1, block, model), lambda s, r, where_ref: (0, s, r, 0)),
+                pl.BlockSpec((8, LANES), lambda s, r, where_ref: (0, 0)),
+            ],
+        ),
+        out_shape=[shape(1, 2, length, model), shape(8, LANES)],
+        compiler_params=pltpu.CompilerParams(
+            dimension_semantics=("arbitrary", "arbitrary"), vmem_limit_bytes=20 * 1024 * 1024
+        ),
+        cost_estimate=cost(0, 16 * length * model),
+        name="tokens",
+    )(where, own0, got0, own1, got1, *ahead)
 
 
 def shards(
@@ -1308,10 +1912,10 @@
     half = width // 2
     both = width + 2 * NSTATE
     rows = min(SPAN, length)
-    first = (1 - lax.axis_index("fsdp")).astype(jnp.int32)
-    places = [
-        jnp.stack([(core == layer).astype(jnp.int32), first, core.astype(jnp.int32)]) for layer in (0, 1)
-    ]
+    spans = lax.axis_size("fsdp"), lax.axis_size("context")
+    x_index, y_index = lax.axis_index("fsdp"), lax.axis_index("context")
+    z_index = lax.axis_index("tensor")
+    place = jnp.stack([core, 1 - x_index, z_index % 2, z_index // 2, x_index, y_index]).astype(jnp.int32)
 
     main_own = lax.optimization_barrier(proj_main[0].reshape(-1, 2 * width))
     rest_own = jnp.concatenate(
@@ -1321,41 +1925,24 @@
     main_near = swap(main_own, "section")
     rest_near = swap(rest_own, "section")
     out_near = swap(out_own, "section")
-    near_rows = main_own.shape[0]
-
-    def half_of(layer, own, near):
-        shard = jnp.where(core == layer, own, near)
-        return lax.dynamic_slice_in_dim(shard, core * (near_rows // 2), near_rows // 2, 0)
-
-    def across(piece):
-        mine = swap(piece, "fsdp")
-        return mine, swap(mine, "section")
-
-    def front_piece(layer):
-        return jnp.concatenate(
-            [
-                half_of(layer, main_own[:, width:], main_near[:, width:]),
-                half_of(layer, rest_own, rest_near),
-            ],
-            axis=1,
+    rest_width = rest_own.shape[1]
+    front_width = width + rest_width
+    held = (main_own, main_near, rest_own, rest_near, out_own, out_near)
+    front_part, gate_part, out_part = [(0, width, width), (1, 0, rest_width)], [(0, 0, width)], [(2, 0, width)]
+    mains = (main_own, main_near)
+    def weights_of(layer, far_arrays, front_at, gate_at, out_at):
+        front = (layer, [(width, width), (0, rest_width)], (front_at, front_width))
+        gate = (layer, [(0, width)], (gate_at, width))
+        out = (layer, [(0, width)], (out_at, width))
+        return (
+            (front, mains + (rest_own, rest_near) + far_arrays),
+            (gate, mains + far_arrays),
+            (out, (out_own, out_near) + far_arrays),
         )
 
-    def gate_piece(layer):
-        return half_of(layer, main_own[:, :width], main_near[:, :width])
-
-    def out_piece(layer):
-        return half_of(layer, out_own, out_near)
-
-    front_far0 = across(front_piece(0))
-    gate_far0 = across(after(gate_piece(0), front_far0[0]))
-    out_far0 = across(after(out_piece(0), gate_far0[0]))
-    front_far1 = across(after(front_piece(1), out_far0[0]))
-    out_far1 = across(after(out_piece(1), front_far1[0]))
-    gate_far1 = across(after(gate_piece(1), out_far1[0]))
-    mains = (main_own, main_near)
-    fronts = [mains + (rest_own, rest_near) + far for far in (front_far0, front_far1)]
-    gates = [mains + far for far in (gate_far0, gate_far1)]
-    outs = [(out_own, out_near) + far for far in (out_far0, out_far1)]
+    def both_halves_of(far, *ahead):
+        far = after(far, *ahead)
+        return far, swap(far, "section")
 
     head_of = np.arange(width) // HEAD_DIM
     one_hot = (np.arange(LANES)[:, None] == head_of[None, :]).astype(np.float32)
@@ -1365,11 +1952,17 @@
     ones = jnp.asarray((row_head[:, None] == np.arange(LANES)[None, :]).astype(np.float32), BF16)
     consts = (spread_matrix, gather_matrix, ones)
 
-    tokens = lax.dynamic_index_in_dim(block_input, core, 0, keepdims=False)
-    cot = lax.dynamic_index_in_dim(cotangent, core, 0, keepdims=False)
-    starts = lax.dynamic_index_in_dim(doc_start, core, 0, keepdims=False).astype(F32)
-    earlier = shifted_along(starts[length - 8 :], "context", 1)
-    later = shifted_along(starts[:8], "context", -1)
+    tokens = lax.dynamic_index_in_dim(block_input, core, 0, keepdims=False, allow_negative_indices=False)
+    first_piece = pieces_call(place, 0, front_part, held[:4])
+    cot = lax.dynamic_index_in_dim(cotangent, core, 0, keepdims=False, allow_negative_indices=False)
+    tokens_other = lax.dynamic_index_in_dim(block_input, 1 - core, 0, keepdims=False, allow_negative_indices=False)
+    cot_other = lax.dynamic_index_in_dim(cotangent, 1 - core, 0, keepdims=False, allow_negative_indices=False)
+    starts = lax.dynamic_index_in_dim(doc_start, core, 0, keepdims=False, allow_negative_indices=False).astype(F32)
+    front_far0 = swap(first_piece, "fsdp")
+    gate_far0 = swap(after(pieces_call(place, 0, gate_part, held[:2]), front_far0), "fsdp")
+    out_piece0 = pieces_call(place, 0, [(0, 0, width)], held[4:])
+    earlier = shifted_along(after(starts[length - 8 :], first_piece), "context", 1)
+    later = shifted_along(after(starts[:8], first_piece), "context", -1)
     line = jnp.concatenate([earlier, starts, later])
     keep = 1.0 - line
     one_back = keep[8:]
@@ -1382,7 +1975,12 @@
     def head_lanes(row):
         return jnp.pad(row, ((0, 0), (0, LANES - heads)))
 
-    pack_own = pl.pallas_call(pack_kernel, out_shape=shape(PACK, both), name="pack")(
+    pack_own = pl.pallas_call(
+        pack_kernel,
+        out_shape=shape(PACK, both),
+        compiler_params=pltpu.CompilerParams(vmem_limit_bytes=4 * 1024 * 1024),
+        name="pack",
+    )(
         conv_main[0],
         conv_states[0],
         conv_main_bias,
@@ -1396,142 +1994,224 @@
     pack_other = swap(pack_own, "section")
     packs = [jnp.where(core == layer, pack_own, pack_other) for layer in (0, 1)]
 
-    def layer_forward(x, halo, layer, *grad_scaled):
-        pack = packs[layer]
-        place = places[layer]
-        normed, inv, pre, conv_x, conv_s, raw, step, cum, entry, rate, end, end_rate = front_call(
-            place, x, halo, tok, pack, spread_matrix, fronts[layer]
+    def layer_front(x, halo, layer, weights, quarters, *ahead):
+        front = front_call(
+            place, x, halo, tok, packs[layer], spread_matrix, weights, quarters, *ahead
         )
+        end, end_rate = front[-2:]
         rate_wide = jnp.repeat(end_rate[0:1, :heads], HEAD_DIM, axis=1)
-        entry_in = carried_state(end, rate_wide, "context", False)
-        z = project_call(place, normed, gate_refs, gates[layer])
-        y = mix_call(conv_x, conv_s, step, cum, entry, spread_matrix)
+        return front, rate_wide, carried_state(end, rate_wide, "context", False)
+
+    def layer_rest(front, entry_in, y, z, layer, *grad_scaled):
+        _, _, _, _, conv_x, conv_s, _, _, cum, _, rate, _, _ = front
         comb, gated, sums = gate_call(
-            y, z, conv_x, conv_s, cum, rate, entry_in, pack, spread_matrix, *grad_scaled
+            y, z, conv_x, conv_s, cum, rate, entry_in, packs[layer], spread_matrix, *grad_scaled
         )
-        sums = small_sum(sums)
-        low_keep, low_send, branch = out_call(place, gated, sums, pack, outs[layer])
-        kept = (conv_x, conv_s, step, cum, raw, entry, rate, entry_in)
-        return branch, (normed, inv, pre, z, kept, comb, (low_keep, low_send), sums, rate_wide)
-
-    def layer_backward(grad_scaled, sums, x, forward, layer):
-        normed, inv, pre, z, kept, comb, _, _, rate_wide = forward
-        pack = packs[layer]
+        return comb, gated, small_sum(sums)
+
+    def layer_gate_back(grad_scaled, sums, comb, z, front, rate_wide, layer):
+        _, _, _, _, _, conv_s, _, _, cum, _, _, _, _ = front
         dmix, dz, adj, adj_rate, begin, gained = gate_back_call(
-            grad_scaled, comb, z, kept[1], kept[3], sums, pack, spread_matrix
+            grad_scaled, comb, z, conv_s, cum, sums, packs[layer], spread_matrix
         )
         adj_in = carried_state(begin, rate_wide, "context", True)
-        *parts, skip = mix_back_call(kept, dmix, adj, consts)
-        grad, grad_raw, head = later_call(kept, dmix, adj_rate, adj_in, parts, pack, consts)
+        return dmix, dz, adj, adj_rate, adj_in, gained
+
+    def layer_mix_back(gate_back, front, entry_in, layer, ahead, before_later):
+        _, _, _, _, conv_x, conv_s, raw, step, cum, entry, rate, _, _ = front
+        kept = (conv_x, conv_s, step, cum, raw, entry, rate, entry_in)
+        dmix, dz, adj, adj_rate, adj_in, gained = gate_back
+        *parts, skip = mix_back_call(kept, dmix, adj, consts, *ahead)
+        grad, grad_raw, head = later_call(
+            kept, dmix, adj_rate, adj_in, parts, packs[layer], consts, *before_later(skip)
+        )
         edge = shifted_along(grad[:8], "context", -1)
-        return conv_back_call(
-            places[layer],
+        return grad, grad_raw, dz, head, skip, gained, edge
+
+    def layer_down(back, low, x, front, layer, front_weights, gate_weights, above, *ahead):
+        grad, grad_raw, dz, head, skip, gained, edge = back
+        keep, send, g0, k0, g1, k1, vector, vector_send = conv_back_call(
+            place,
             grad,
-            pre,
+            front[3],
             grad_raw,
             dz,
+            low,
             tok,
             edge,
             tok_after,
-            pack,
+            packs[layer],
             x,
-            inv,
+            front[2],
             head,
             skip,
             gained,
             gather_matrix,
-            fronts[layer],
-            gates[layer],
+            front_weights,
+            gate_weights,
+            above,
+            *ahead,
         )
-
-    blocks = lax.axis_size("fsdp") * lax.axis_size("context")
-    share = model // blocks
-
-    def matrix_grads(normed, g_low, low, keep, send):
-        received = swap(send, "section")
-        normed_other = swap(normed, "section")
-        low_keep, low_send = low
-        low_received = swap(low_send, "section")
-        g_other = swap(g_low, "section")
-        cols = mm(normed, keep[:, :width], TN) + mm(normed_other, received[:, :width], TN)
-        top = slice(width, width + 2 * NSTATE)
-        rest = slice(width + 2 * NSTATE, width + 4 * NSTATE)
-        states = (
-            mm(normed, keep[:, top], TN)
-            + mm(normed, keep[:, rest], TN)
-            + mm(normed_other, received[:, top], TN)
-            + mm(normed_other, received[:, rest], TN)
-        )
-        outer = mm(g_low, low_keep, TN) + mm(g_other, low_received, TN)
-        states = scatter_sum(states.reshape(blocks, share, -1), F32)
-        states = jnp.where(lower_core, lax.psum(states, "tensor"), states)
-        matrices = jnp.concatenate([cols.astype(BF16), outer.astype(BF16)], axis=1)
-        return states, scatter_sum(matrices.reshape(blocks, share, -1), BF16)
-
-    halo0 = shifted_along(tokens[length - 8 :], "context", 1)
-    branch0, forward0 = layer_forward(tokens, halo0, 0)
-    edge0 = tokens[length - 8 :].astype(F32) + small_sum(branch0[length - 8 :])
-    halo1 = shifted_along(edge0, "context", 1)
-    branch0 = tensor_sum(branch0, jnp.float16, 2).astype(F32)
-    x1 = tokens.astype(F32) + branch0
-    grad_scaled1 = project_call(places[1], cot, out_refs, outs[1])
-    branch1, forward1 = layer_forward(x1, halo1, 1, grad_scaled1)
-    x2 = x1 + lax.psum(branch1.astype(BF16), "tensor").astype(F32)
-
-    keep1, send1, part1, small1 = layer_backward(grad_scaled1, forward1[7], x1, forward1, 1)
-    normed_grad1 = tensor_sum(part1, BF16, 2)
-    grad1, g_low0, grad_scaled0, sums0 = finish_call(
-        places[0], normed_grad1, cot, x1, forward1[1], packs[1], branch0, forward0[7], *outs[0]
-    )
-    keep0, send0, part0, small0 = layer_backward(grad_scaled0, sums0, tokens, forward0, 0)
-    normed_grad0 = tensor_sum(part0, BF16, 2)
-    grad0 = finish_call(places[0], normed_grad0, grad1, tokens, forward0[1], packs[0])[0]
-
-    mats1 = matrix_grads(forward1[0], cot, forward1[6], keep1, send1)
-    mats0 = matrix_grads(forward0[0], g_low0, forward0[6], keep0, send0)
-
-    def to_layer(first, second, kind):
-        mine = jnp.where(lower_core, first, second).astype(kind)
-        theirs = swap(jnp.where(lower_core, second, first).astype(kind), "section")
-        return jnp.where(lower_core, mine, theirs).astype(F32), jnp.where(lower_core, theirs, mine).astype(F32)
-
-    grad_states, step_wide = to_layer(mats0[0], mats1[0], F32)
-    lower, upper = to_layer(mats0[1], mats1[1], BF16)
-    grad_main = jnp.stack(
-        [
-            jnp.concatenate([lower[:, :half], upper[:, :half]], axis=1),
-            jnp.concatenate([lower[:, half:width], upper[:, half:width]], axis=1),
-        ],
-        axis=1,
-    )
-    grad_out = jnp.concatenate([lower[:, width:], upper[:, width:]], axis=1)
-
+        return keep, send, [(0, g0, k0), (1, g1, k1)], vector, vector_send
+
+    fronts0 = weights_of(0, both_halves_of(front_far0), 0, 0, 0)[0]
+    halo0 = shifted_along(after(tokens[length - 8 :], first_piece), "context", 1)
+    front0, rate_wide0, entry0 = layer_front(
+        tokens, halo0, 0, fronts0, (), packs[1]
+    )
+    normed0 = front0[1]
+    gate_far0 = after(gate_far0, front0[-1])
+    gates0 = weights_of(0, (gate_far0, swap(gate_far0, "section")), 0, 0, 0)[1]
+    out_far0 = swap(after(out_piece0, gate_far0), "fsdp")
+    y0 = mix_call(front0[4], front0[5], front0[7], front0[8], front0[9], spread_matrix)
+    z0 = project_call(place, normed0, gates0)
+    comb0, gated0, sums0 = layer_rest(front0, entry0, y0, z0, 0)
+    out_far0 = after(out_far0, comb0)
+    outs0 = weights_of(0, (out_far0, swap(out_far0, "section")), 0, 0, 0)[2]
+    pieces1 = pieces_call(place, 1, front_part + gate_part + out_part, held, out_far0)
+    far1 = swap(pieces1, "fsdp")
+    low0, g0, k0, g1, k1, edge0 = out_call(place, gated0, sums0, packs[0], outs0, F32, pieces1)
+
+    half16 = jnp.float16
+    total0 = TensorSum([(0, g0.astype(half16), k0), (1, g1.astype(half16), k1)])
+    halo1 = shifted_along(tokens[length - 8 :].astype(F32) + small_sum(edge0), "context", 1)
+    total0.across()
+    event = total0.back()
+    fronts1, gates1, outs1 = weights_of(
+        1, both_halves_of(far1, event), 0, front_width, front_width + width
+    )
+    grad_scaled1 = project_call(place, cot, outs1)
+    normed_other0 = renorm_call(tokens_other, packs[0], edge0)
+    branch0 = [v.astype(F32) for v in total0.quarters()]
+
+    front1, rate_wide1, entry1 = layer_front(
+        tokens, halo1, 1, fronts1, branch0
+    )
+    x1, normed1 = front1[:2]
+    y1 = mix_call(front1[4], front1[5], front1[7], front1[8], front1[9], spread_matrix)
+    z1 = project_call(place, normed1, gates1)
+    comb1, gated1, sums1 = layer_rest(front1, entry1, y1, z1, 1, grad_scaled1)
+
+    gate_back1 = layer_gate_back(grad_scaled1, sums1, comb1, z1, front1, rate_wide1, 1)
+    low1, g0, k0, g1, k1, edge1 = out_call(place, gated1, sums1, packs[1], outs1, BF16)
+    half_a = TensorSum([(0, g0, k0)])
+    half_b = TensorSum([(0, g1, k1)])
+    back1 = layer_mix_back(gate_back1, front1, entry1, 1, (edge1,), lambda tick: ())
+    keep1, send1, pieces, small1, _ = layer_down(
+        back1,
+        low1,
+        x1,
+        front1,
+        1,
+        fronts1,
+        gates1,
+        (),
+        half_a.across(back1[3]),
+        half_b.add(back1[3]),
+    )
+    *gives, send1 = hold_call([give for _, give, _ in pieces] + [send1], half_a.total(keep1))
+    total1 = TensorSum([(half, give, keep) for (half, _, keep), give in zip(pieces, gives)])
+    received1 = swap(send1, "section")
+    x1_other = swap(x1, "section")
+    normed_other1 = renorm_call(x1_other, packs[1], keep1)
+    matrices1 = wgrad_call(place, spans, normed1, normed_other1, cot, cot_other, keep1, received1)
+    scatter1 = ScatterSum(matrices1)
+    total1.across(jax.tree.leaves(matrices1)[0])
+    event = scatter1.turn(total1.back())
+    matrices1, steps1, states1 = scatter1.result(place, (), event)
+    grad1, g_low0, grad_scaled0, sums0_back = finish_call(
+        place, total1.quarters(), cot, x1, front1[2], packs[1], (steps1,), branch0, sums0, outs0
+    )
+
+    gate_back0 = layer_gate_back(grad_scaled0, sums0_back, comb0, z0, front0, rate_wide0, 0)
+    ahead = half_b.hold(sums0_back), half_a.spread(sums0_back)
+    back0 = layer_mix_back(
+        gate_back0, front0, entry0, 0, ahead, lambda tick: ()
+    )
+    tick = back0[3]
+    grad_got1 = swap(grad1, "section")
+    keep0, send0, pieces, vector, vector_send = layer_down(
+        back0,
+        low0,
+        tokens,
+        front0,
+        0,
+        fronts0,
+        gates0,
+        (small1,),
+        half_b.back(tick),
+        half_a.others[0],
+        grad_got1,
+    )
+    x2 = join_call(place, x1, half_a.quarters() + half_b.quarters(), keep0)
+    *gives, send0 = hold_call([give for _, give, _ in pieces] + [send0], x2)
+    total0 = TensorSum([(half, give, keep) for (half, _, keep), give in zip(pieces, gives)])
+    received0 = swap(send0, "section")
+    (vector,) = merge_call([vector], [swap(vector_send, "section")], F32)
+    (vector,) = merge_call([vector], [sum_given(vector, "fsdp")], F32)
+    (vector,) = merge_call([vector], [sum_given(vector, "context")], F32)
+    matrices0 = wgrad_call(
+        place,
+        spans,
+        normed0,
+        normed_other0,
+        g_low0,
+        grad_got1,
+        keep0,
+        received0,
+        vector,
+    )
+    scatter0 = ScatterSum(matrices0)
+    event = total0.across(jax.tree.leaves(matrices0)[0])
+    x2_other = swap(x2, "section")
+    event = scatter0.turn(event)
+    event = total0.back(event)
+    layer_out, event = tokens_call(place, x1, x1_other, x2, x2_other, event)
+    (vector,) = hold_call([vector], event)
+    count = lax.axis_size("tensor")
+    vectors = [vector] + [
+        lax.ppermute(vector, "tensor", [(i, (i + by) % count) for i in range(count)])
+        for by in range(1, count)
+    ]
     row = np.arange(PACK)[:, None]
     lane = np.arange(both)[None, :]
     shared = ((row < SKIP) & (lane >= width)) | (row == NORM) | (row == NORM + 1)
-
-    def over_tensor(small):
-        return jnp.where(shared, small_sum(small), small)
-
-    vector = jnp.where(lower_core, small0, small1) + swap(
-        jnp.where(lower_core, small1, small0), "section"
-    )
-    vector = over_tensor(sum_over(sum_over(vector, "fsdp"), "context"))
-
-    def to_sections(first, second):
-        mine = jnp.where(lower_core, first, second)
-        theirs = swap(jnp.where(lower_core, second, first), "section")
-        return jnp.stack([jnp.where(lower_core, mine, theirs), jnp.where(lower_core, theirs, mine)])
-
-    layer_out = to_sections(x1, x2)
-    layer_in_grad = to_sections(grad0, grad1)
+    shared = jnp.asarray(shared.astype(np.float32))
+    vector = vector_call(shared, vectors)
+    matrices0, steps0, *states = scatter0.result(place, (states1,), event)
+    states = TensorSum([(0, *states[:2]), (1, *states[2:])])
+    matrices_got1 = swap(matrices1, "section")
+    matrices_got0 = swap(matrices0, "section")
+    grad0 = finish_call(
+        place,
+        total0.quarters(),
+        grad1,
+        tokens,
+        front0[2],
+        packs[0],
+        (states.across(vector),),
+    )[0]
+    grad_got0 = swap(grad0.astype(BF16), "section")
+    event = states.back(grad0)
+    layer_in_grad, event = tokens_call(place, grad0, grad_got0, grad1, grad_got1, event)
+    rest = rest_call(place, states.quarters(), steps0, steps1, event)
+    grad_main, grad_states, grad_step, grad_out = matrices_call(
+        place,
+        heads,
+        matrices0,
+        matrices_got0,
+        matrices1,
+        matrices_got1,
+        rest,
+        swap(rest, "section"),
+    )
     return (
-        layer_out[None],
-        layer_in_grad[None],
+        layer_out,
+        layer_in_grad,
         vector[NORM : NORM + 2, : model // 2].reshape(1, model),
-        grad_main[None],
-        grad_states[None],
-        step_wide[None, :, :heads],
+        grad_main,
+        grad_states,
+        grad_step,
         vector[None, TAPS : TAPS + CONV, :width],
         vector[BIAS : BIAS + 1, :width],
         vector[None, TAPS : TAPS + CONV, width:],
@@ -1540,7 +2220,7 @@
         vector[DECAY : DECAY + 1, :heads],
         vector[SKIP : SKIP + 1, :heads],
         vector[GATED : GATED + 1, :width],
-        grad_out[None],
+        grad_out,
     )
 
 

time: 647 us -> 522 us (0.81)
  waiting for transfers between devices: 261 us -> 208 us
  other arithmetic: 60.4 us -> 8.44 us
  Pallas kernels: 114 us -> 158 us
  local copies, waits for them, and re-layouts: 76.2 us -> 33.2 us
  matrix products: 25 us -> 0 us
  starting transfers between devices: 82 us -> 97.8 us
  between operations: 17.7 us -> 7.27 us
    pallas_call x18 -> x54, Pallas kernels: 102 us -> 147 us  [the longest x47 119 us: ordered_call(): return lambda *operands: call(*operands, *ahead)]
    ppermute x18 -> x33, waiting for transfers between devices: 189 us -> 155 us  [the longest x30 141 us: _send(): lax.ppermute(v, 'tensor', self.STEPS[half][step])]
    unnamed x278 -> x185, local copies, waits for them, and re-layouts: 47.7 us -> 18.5 us
    dot_general x16 -> x0, matrix products: 25 us -> none  [mm(): return lax.dot_general(a, b, dims, preferred_element_type=F32)]
    ppermute x18 -> x33, starting transfers between devices: 19.1 us -> 39.5 us  [the longest x30 36.6 us: _send(): lax.ppermute(v, 'tensor', self.STEPS[half][step])]
    select_n x16 -> x0, other arithmetic: 17.8 us -> none  [the longest x4 6.28 us: half_of(): shard = jnp.where(core == layer, own, near)]
    convert_element_type x15 -> x10, other arithmetic: 13.4 us -> 0.9 us  [the longest x4 0.4 us: shards(): branch0 = [v.astype(F32) for v in total0.quarters()]]
    broadcast_in_dim x6 -> x0, other arithmetic: 11.4 us -> none  [the longest x1 5.13 us: shards(): layer_in_grad[None]]
  transfers between devices with their start and end apart: 77 -> 84, of which waited for: 38 -> 40; matrix products, arithmetic and copies ran while one was open for 16% -> 5% of each run, Pallas kernels for 14% -> 25%
where the time goes in v2:
time: 522 us; the launch traced here: 513 us
  waiting for transfers between devices  208 us (40%)
  Pallas kernels  158 us (30%)
  starting transfers between devices  97.8 us (19%)
  local copies, waits for them, and re-layouts  33.2 us (6%)
  other arithmetic  8.44 us (2%)
  between operations  7.27 us (1%)
    ppermute x30, waiting for transfers between devices, _send(): lax.ppermute(v, 'tensor', self.STEPS[half][step])  141 us
    pallas_call x47, Pallas kernels, ordered_call(): return lambda *operands: call(*operands, *ahead)  119 us
    ppermute x30, starting transfers between devices, _send(): lax.ppermute(v, 'tensor', self.STEPS[half][step])  36.6 us
    ppermute x32, waiting for transfers between devices, swap(): return lax.ppermute(value, axis, [(0, 1), (1, 0)])  30.1 us
    ppermute x10, starting transfers between devices, shifted_along(): lax.ppermute(value, axis, [(i, i + by) for i in range(count) if 0 <= i +...  27.2 us
    ppermute x32, starting transfers between devices, swap(): return lax.ppermute(value, axis, [(0, 1), (1, 0)])  19.5 us
    unnamed x185, local copies, waits for them, and re-layouts  18.5 us
    pallas_call x2, Pallas kernels, wgrad_call(): pl.pallas_call(functools.partial(wgrad_relative_kernel, len(ahead)), grid...  17.2 us
  transfers between devices with their start and end apart: 84, of which 40 were waited for; matrix products, arithmetic and copies ran while one was open for 5% of the time, Pallas kernels for 25%

profile of v2, /device:TPU:0, one launch (start us, length us, event | category | flops | bytes accessed | tf_op | source)
XLA Modules:
  0.0 512.5 jit_solution(12500865439835968181)
XLA Ops:
  29.5 3.4 collective-permute-start.4
  34.9 4.5 collective-permute-start.2
  49.4 8.9 %front.2 = (f32[8,1536]{1,0:T(8,128)}, bf16[512,1536]{1,0:T(8,128)(2,1)S(1)}, f32[512,128]{1,0:T(8,128)S(1)}, f32[512,1024]{1,0:T(8,128)S(1)}, f32[512,768]{1,0:...) custom-call(s32[6]{0:T(128)S(1)} %stack.42.refs_0_.where_ref, ...), custom_call_target="tpu_custom_call" | custom-call | flops 1 | bytes 1 | tf_op jit(solution)/shard_map/front/pallas_call | solution.py:142
  65.9 3.4 collective-permute-start.10
  74.8 3.2 collective-permute-done.10.entry_ref.refs_7_.refs_8_
  85.1 3.6 collective-permute-start.13
  90.2 3.2 collective-permute-done.12
  94.3 4.1 out.2
  99.7 16.7 %collective-permute-done.22 = f16[128,1536]{1,0:T(8,128)(2,1)S(1)} collective-permute-done((f16[128,1536]{1,0:T(8,128)(2,1)S(1)}, f16[128,1536]{1,0:T(8,128)(2,1)S(1)}, u32[]{:S(2)}, u32[]{:S(2)}) %collective-permute-start.22) | collective-permute-done | bytes 393248 | tf_op jit(solution)/shard_map/ppermute | solution.py:1697
  118.7 9.8 %collective-permute-done.23 = f16[128,1536]{1,0:T(8,128)(2,1)S(1)} collective-permute-done((f16[128,1536]{1,0:T(8,128)(2,1)S(1)}, f16[128,1536]{1,0:T(8,128)(2,1)S(1)}, u32[]{:S(2)}, u32[]{:S(2)}) %collective-permute-start.23) | collective-permute-done | bytes 393248 | tf_op jit(solution)/shard_map/ppermute | solution.py:1697
  131.6 4.4 collective-permute-done.25
  141.2 16.8 %collective-permute-done.26 = f16[128,1536]{1,0:T(8,128)(2,1)S(1)} collective-permute-done((f16[128,1536]{1,0:T(8,128)(2,1)S(1)}, f16[128,1536]{1,0:T(8,128)(2,1)S(1)}, u32[]{:S(2)}, u32[]{:S(2)}) %collective-permute-start.26) | collective-permute-done | bytes 393248 | tf_op jit(solution)/shard_map/ppermute | solution.py:1697
  158.1 8.1 %collective-permute-start.27 = (f16[128,1536]{1,0:T(8,128)(2,1)S(1)}, f16[128,1536]{1,0:T(8,128)(2,1)S(1)}, u32[]{:S(2)}, u32[]{:S(2)}) collective-permute-start(f16[128,1536]{1,0:T(8,128)(2,1)S(1)} %get-tuple-element.343), channel_id=1, source_target_pairs={{0,1},{1,0},{2,3},{3,2},{4,5},{5,4},{6,7},{7,6},{8,9},{9,8},{10,11... | collective-permute-start | bytes 1179656 | tf_op jit(solution)/shard_map/ppermute | solution.py:1697
  168.6 4.6 collective-permute-start.20
  173.1 10.8 %collective-permute-done.27 = f16[128,1536]{1,0:T(8,128)(2,1)S(1)} collective-permute-done((f16[128,1536]{1,0:T(8,128)(2,1)S(1)}, f16[128,1536]{1,0:T(8,128)(2,1)S(1)}, u32[]{:S(2)}, u32[]{:S(2)}) %collective-permute-start.27) | collective-permute-done | bytes 393248 | tf_op jit(solution)/shard_map/ppermute | solution.py:1697
  184.2 10.4 %front.3 = (f32[512,1536]{1,0:T(8,128)}, bf16[512,1536]{1,0:T(8,128)(2,1)S(1)}, f32[512,128]{1,0:T(8,128)S(1)}, f32[512,1024]{1,0:T(8,128)S(1)}, f32[512,768]{1,...) custom-call(s32[6]{0:T(128)S(1)} %stack.42.refs_0_.where_ref, ...), custom_call_target="tpu_custom_call" | custom-call | flops 1 | bytes 1 | tf_op jit(solution)/shard_map/front/pallas_call | solution.py:142
  194.7 4.4 collective-permute-start.30
  203.2 3.7 project.5.refs_0_.scaled_ref
  206.9 3.7 project.4.z_ref
  220.0 3.1 gate_back.2
  224.4 4.6 out.3
  231.1 9.1 %mix_back.2 = (f32[512,768]{1,0:T(8,128)S(1)}, f32[512,128]{1,0:T(8,128)S(1)}, f32[512,128]{1,0:T(8,128)S(1)}, f32[512,128]{1,0:T(8,128)S(1)}, f32[8,768]{1,0:T(8,128)S(1)}) custom-call(f32[512,768]{1,0:T(8,128)S(1)} %get-tuple-element.173.refs_0_.conv_x_ref, f32[512,256]{1,0:T(8,128)S(1)} %get-tuple-element.174.refs_1_.conv_s_ref, ...), custom_call_target="tpu_custom_call" | custom-call | flops 1 | bytes 1 | tf_op jit(solution)/shard_map/mix_back/pallas_call | solution.py:142
  240.2 5.8 %later.2 = (f32[512,1024]{1,0:T(8,128)S(1)}, bf16[512,128]{1,0:T(8,128)(2,1)S(1)}, f32[8,128]{1,0:T(8,128)S(1)}) custom-call(f32[512,768]{1,0:T(8,128)S(1)} %get-tuple-element.173.refs_0_.conv_x_ref, f32[512,256]{1,0:T(8,128)S(1)} %get-tuple-element.174.refs_1_.conv_s_ref, f32[512,768]{1,0:T(8,128)S(1)} %get-tuple-element.186.refs_2_, ...), custom_call_target="tpu_custom_call" | custom-call | flops 1 | bytes 1 | tf_op jit(solution)/shard_map/later/pallas_call | solution.py:142
  248.2 4.5 collective-permute-done.37.refs_7_
  254.3 11.8 %conv_back.2 = (bf16[512,1536]{1,0:T(8,128)(2,1)S(1)}, bf16[512,1536]{1,0:T(8,128)(2,1)S(1)}, bf16[128,1536]{1,0:T(8,128)(2,1)S(1)}, f32[128,1536]{1,0:T(8,128)S...) custom-call(s32[6]{0:T(128)S(1)} %stack.42.refs_0_.where_ref, ...), custom_call_target="tpu_custom_call" | custom-call | flops 1 | bytes 1 | tf_op jit(solution)/shard_map/conv_back/pallas_call | solution.py:142
  269.9 8.6 %wgrad.2 = (bf16[2,192,1536]{2,1,0:T(8,128)(2,1)S(1)}, bf16[2,192,1536]{2,1,0:T(8,128)(2,1)S(1)}, bf16[2,192,1536]{2,1,0:T(8,128)(2,1)S(1)}, bf16[2,192,1536]{2,1,0:T(8,128)(2,1)S(1)}) custom-call(s32[6]{0:T(128)S(1)} %stack.42.refs_0_.where_ref, bf16[512,1536]{1,0:T(8,128)(2,1)S(1)} %copy-done.29, bf16[512,1536]{1,0:T(8,128)(2,1)S(1)} %renorm.2.refs_1_, ...), custom_call_target="tpu_custom_call" | custom-call | flops 1 | bytes 1 | tf_op jit(solution)/shard_map/wgrad/pallas_call | solution.py:1529
  284.0 16.3 %collective-permute-done.39.refs_2_ = bf16[128,1536]{1,0:T(8,128)(2,1)S(1)} collective-permute-done((bf16[128,1536]{1,0:T(8,128)(2,1)S(1)}, bf16[128,1536]{1,0:T(8,128)(2,1)S(1)}, u32[]{:S(2)}, u32[]{:S(2)}) %collective-permute-start.39) | collective-permute-done | bytes 393248 | tf_op jit(solution)/shard_map/ppermute | solution.py:1697
  305.9 14.2 %collective-permute-done.42.refs_2_ = bf16[128,1536]{1,0:T(8,128)(2,1)S(1)} collective-permute-done((bf16[128,1536]{1,0:T(8,128)(2,1)S(1)}, bf16[128,1536]{1,0:T(8,128)(2,1)S(1)}, u32[]{:S(2)}, u32[]{:S(2)}) %collective-permute-start.42) | collective-permute-done | bytes 393248 | tf_op jit(solution)/shard_map/ppermute | solution.py:1697
  325.7 8.4 %collective-permute-done.49.refs_4_ = bf16[192,1536]{1,0:T(8,128)(2,1)S(1)} collective-permute-done((bf16[192,1536]{1,0:T(8,128)(2,1)S(1)}, bf16[192,1536]{1,0:T(8,128)(2,1)S(1)}, u32[]{:S(2)}, u32[]{:S(2)}) %collective-permute-start.49) | collective-permute-done | bytes 589856 | tf_op jit(solution)/shard_map/ppermute | solution.py:1631
  342.3 6.3 %finish.2 = (f32[512,1536]{1,0:T(8,128)S(1)}, bf16[512,1536]{1,0:T(8,128)(2,1)S(1)}, f32[512,768]{1,0:T(8,128)S(1)}, f32[8,512]{1,0:T(8,128)S(1)}) custom-call(s32[6]{0:T(128)S(1)} %stack.42.refs_0_.where_ref, bf16[512,1536]{1,0:T(8,128)(2,1)S(1)} %get-tuple-element.349.refs_1_.refs_2_, f32[512,1536]{1,0:T(8,128)S(1)} %copy-done.1, ...), custom_call_target="tpu_custom_call" | custom-call | flops 1 | bytes 1 | tf_op jit(solution)/shard_map/finish/pallas_call | solution.py:142
  349.9 3.3 gate_back.3
  357.6 9.2 %mix_back.3 = (f32[512,768]{1,0:T(8,128)S(1)}, f32[512,128]{1,0:T(8,128)S(1)}, f32[512,128]{1,0:T(8,128)S(1)}, f32[512,128]{1,0:T(8,128)S(1)}, f32[8,768]{1,0:T(8,128)S(1)}) custom-call(f32[512,768]{1,0:T(8,128)S(1)} %get-tuple-element.155.refs_0_.conv_x_ref, f32[512,256]{1,0:T(8,128)S(1)} %get-tuple-element.156.refs_1_.conv_s_ref, ...), custom_call_target="tpu_custom_call" | custom-call | flops 1 | bytes 1 | tf_op jit(solution)/shard_map/mix_back/pallas_call | solution.py:142
  366.9 5.8 %later.3 = (f32[512,1024]{1,0:T(8,128)S(1)}, bf16[512,128]{1,0:T(8,128)(2,1)S(1)}, f32[8,128]{1,0:T(8,128)S(1)}) custom-call(f32[512,768]{1,0:T(8,128)S(1)} %get-tuple-element.155.refs_0_.conv_x_ref, f32[512,256]{1,0:T(8,128)S(1)} %get-tuple-element.156.refs_1_.conv_s_ref, f32[512,768]{1,0:T(8,128)S(1)} %get-tuple-element.231.refs_2_, ...), custom_call_target="tpu_custom_call" | custom-call | flops 1 | bytes 1 | tf_op jit(solution)/shard_map/later/pallas_call | solution.py:142
  376.8 4.5 collective-permute-done.54.refs_7_
  381.4 11.0 %conv_back.3 = (bf16[512,1536]{1,0:T(8,128)(2,1)S(1)}, bf16[512,1536]{1,0:T(8,128)(2,1)S(1)}, bf16[128,1536]{1,0:T(8,128)(2,1)S(1)}, f32[128,1536]{1,0:T(8,128)S...) custom-call(s32[6]{0:T(128)S(1)} %stack.42.refs_0_.where_ref, ...), custom_call_target="tpu_custom_call" | custom-call | flops 1 | bytes 1 | tf_op jit(solution)/shard_map/conv_back/pallas_call | solution.py:142
  394.3 7.4 %collective-permute-done.60.refs_1_ = f32[16,1024]{1,0:T(8,128)S(1)} collective-permute-done((f32[16,1024]{1,0:T(8,128)S(1)}, f32[16,1024]{1,0:T(8,128)S(1)}, u32[]{:S(2)}, u32[]{:S(2)}) %collective-permute-start.60) | collective-permute-done | bytes 65568 | tf_op jit(solution)/shard_map/ppermute | solution.py:1631
  402.9 3.2 collective-permute-done.61.refs_1_
  407.0 3.4 collective-permute-done.62.refs_1_
  410.4 8.6 %wgrad.3 = (bf16[2,192,1536]{2,1,0:T(8,128)(2,1)S(1)}, bf16[2,192,1536]{2,1,0:T(8,128)(2,1)S(1)}, bf16[2,192,1536]{2,1,0:T(8,128)(2,1)S(1)}, bf16[2,192,1536]{2,1,0:T(8,128)(2,1)S(1)}) custom-call(s32[6]{0:T(128)S(1)} %stack.42.refs_0_.where_ref, bf16[512,1536]{1,0:T(8,128)(2,1)S(1)} %copy-done.33, bf16[512,1536]{1,0:T(8,128)(2,1)S(1)} %renorm.3.refs_1_, ...), custom_call_target="tpu_custom_call" | custom-call | flops 1 | bytes 1 | tf_op jit(solution)/shard_map/wgrad/pallas_call | solution.py:1529
  422.4 14.2 %collective-permute-done.57.refs_2_ = bf16[128,1536]{1,0:T(8,128)(2,1)S(1)} collective-permute-done((bf16[128,1536]{1,0:T(8,128)(2,1)S(1)}, bf16[128,1536]{1,0:T(8,128)(2,1)S(1)}, u32[]{:S(2)}, u32[]{:S(2)}) %collective-permute-start.57) | collective-permute-done | bytes 393248 | tf_op jit(solution)/shard_map/ppermute | solution.py:1697
  436.6 8.7 %collective-permute-done.58.refs_3_ = bf16[128,1536]{1,0:T(8,128)(2,1)S(1)} collective-permute-done((bf16[128,1536]{1,0:T(8,128)(2,1)S(1)}, bf16[128,1536]{1,0:T(8,128)(2,1)S(1)}, u32[]{:S(2)}, u32[]{:S(2)}) %collective-permute-start.58) | collective-permute-done | bytes 393248 | tf_op jit(solution)/shard_map/ppermute | solution.py:1697
  450.0 7.1 %collective-permute-done.63.refs_2_ = bf16[128,1536]{1,0:T(8,128)(2,1)S(1)} collective-permute-done((bf16[128,1536]{1,0:T(8,128)(2,1)S(1)}, bf16[128,1536]{1,0:T(8,128)(2,1)S(1)}, u32[]{:S(2)}, u32[]{:S(2)}) %collective-permute-start.63) | collective-permute-done | bytes 393248 | tf_op jit(solution)/shard_map/ppermute | solution.py:1697
  457.1 5.5 %collective-permute-done.64.refs_3_ = bf16[128,1536]{1,0:T(8,128)(2,1)S(1)} collective-permute-done((bf16[128,1536]{1,0:T(8,128)(2,1)S(1)}, bf16[128,1536]{1,0:T(8,128)(2,1)S(1)}, u32[]{:S(2)}, u32[]{:S(2)}) %collective-permute-start.64) | collective-permute-done | bytes 393248 | tf_op jit(solution)/shard_map/ppermute | solution.py:1697
  465.0 3.6 tokens.2
  472.4 7.0 %collective-permute-done.75.d_ref = f32[16,1024]{1,0:T(8,128)S(1)} collective-permute-done((f32[16,1024]{1,0:T(8,128)S(1)}, f32[16,1024]{1,0:T(8,128)S(1)}, u32[]{:S(2)}, u32[]{:S(2)}) %collective-permute-start.75) | collective-permute-done | bytes 65568 | tf_op jit(solution)/shard_map/ppermute | solution.py:2173
  481.9 5.4 %collective-permute-done.73.b_ref = f32[16,1024]{1,0:T(8,128)S(1)} collective-permute-done((f32[16,1024]{1,0:T(8,128)S(1)}, f32[16,1024]{1,0:T(8,128)S(1)}, u32[]{:S(2)}, u32[]{:S(2)}) %collective-permute-start.73) | collective-permute-done | bytes 65568 | tf_op jit(solution)/shard_map/ppermute | solution.py:2173
  492.1 5.4 %collective-permute-done.77.refs_2_ = f32[96,256]{1,0:T(8,128)S(1)} collective-permute-done((f32[96,256]{1,0:T(8,128)S(1)}, f32[96,256]{1,0:T(8,128)S(1)}, u32[]{:S(2)}, u32[]{:S(2)}) %collective-permute-start.77) | collective-permute-done | bytes 98336 | tf_op jit(solution)/shard_map/ppermute | solution.py:1697
  501.7 3.6 tokens.3
  (416 shorter events, 167.8 us)
Async XLA Ops:
  7.0 19.0 %collective-permute-start.14 = (bf16[768,768]{1,0:T(8,128)(2,1)S(1)}, bf16[768,768]{1,0:T(8,128)(2,1)}, u32[]{:S(2)}, u32[]{:S(2)}) collective-permute-start(bf16[768,768]{1,0:T(8,128)(2,1)S(1)} %bitcast.59), channel_id=1, source_target_pairs={{0,16},{16,0},{1,17},{17,1},{2,18},{18,2},{3,19},{19,3},{4,20},{20... | collective-permute-start | bytes 3538952 | tf_op jit(solution)/shard_map/ppermute | solution.py:1631
  19.6 23.3 %collective-permute-start.6 = (bf16[384,1152]{1,0:T(8,128)(2,1)}, bf16[384,1152]{1,0:T(8,128)(2,1)}, u32[]{:S(2)}, u32[]{:S(2)}) collective-permute-start(bf16[384,1152]{1,0:T(8,128)(2,1)} %pieces.4), channel_id=1, source_target_pairs={{0,8},{8,0},{1,9},{9,1},{2,10},{10,2},{3,11},{11,3},{4,12},{12,4},... | collective-permute-start | bytes 2654216 | tf_op jit(solution)/shard_map/ppermute | solution.py:1631
  29.5 17.9 %collective-permute-start.4 = (f32[8]{0:T(128)S(1)}, f32[8]{0:T(128)S(1)}, u32[]{:S(2)}, u32[]{:S(2)}) collective-permute-start(f32[8]{0:T(128)S(1)} %get-tuple-element.358), channel_id=1, source_target_pairs={{0,4},{1,5},{2,6},{3,7},{8,12},{9,13},{10,14},{11,15},{16,20},{17,... | collective-permute-start | bytes 104 | tf_op jit(solution)/shard_map/ppermute | solution.py:1636
  32.9 14.5 %collective-permute-start.3 = (f32[8]{0:T(128)S(1)}, f32[8]{0:T(128)S(1)}, u32[]{:S(2)}, u32[]{:S(2)}) collective-permute-start(f32[8]{0:T(128)S(1)} %get-tuple-element.359), channel_id=1, source_target_pairs={{4,0},{5,1},{6,2},{7,3},{12,8},{13,9},{14,10},{15,11},{20,16},{21,... | collective-permute-start | bytes 104 | tf_op jit(solution)/shard_map/ppermute | solution.py:1636
  45.6 16.0 %collective-permute-start.8 = (bf16[384,768]{1,0:T(8,128)(2,1)}, bf16[384,768]{1,0:T(8,128)(2,1)}, u32[]{:S(2)}, u32[]{:S(2)}) collective-permute-start(bf16[384,768]{1,0:T(8,128)(2,1)} %broadcast_add_fusion.4), channel_id=1, source_target_pairs={{0,8},{8,0},{1,9},{9,1},{2,10},{10,2},{3,11},{11,3},{4,12},{12,4},... | collective-permute-start | bytes 1769480 | tf_op jit(solution)/shard_map/ppermute | solution.py:1631
  64.1 18.0 %collective-permute-start.15 = (bf16[384,768]{1,0:T(8,128)(2,1)S(1)}, bf16[384,768]{1,0:T(8,128)(2,1)S(1)}, u32[]{:S(2)}, u32[]{:S(2)}) collective-permute-start(bf16[384,768]{1,0:T(8,128)(2,1)S(1)} %broadcast_add_fusion.2), channel_id=1, source_target_pairs={{0,8},{8,0},{1,9},{9,1},{2,10},{10,2},{3,11},{11,3},{4,12},{12,4},... | collective-permute-start | bytes 1769480 | tf_op jit(solution)/shard_map/ppermute | solution.py:1631
  84.5 46.8 %collective-permute-start.21 = (bf16[384,2688]{1,0:T(8,128)(2,1)S(1)}, bf16[384,2688]{1,0:T(8,128)(2,1)S(1)}, u32[]{:S(2)}, u32[]{:S(2)}) collective-permute-start(bf16[384,2688]{1,0:T(8,128)(2,1)S(1)} %pieces.7.refs_8_), channel_id=1, source_target_pairs={{0,8},{8,0},{1,9},{9,1},{2,10},{10,2},{3,11},{11,3},{4,12},{12,4},... | collective-permute-start | bytes 6193160 | tf_op jit(solution)/shard_map/ppermute | solution.py:1631
  98.5 17.9 %collective-permute-start.22 = (f16[128,1536]{1,0:T(8,128)(2,1)S(1)}, f16[128,1536]{1,0:T(8,128)(2,1)S(1)}, u32[]{:S(2)}, u32[]{:S(2)}) collective-permute-start(f16[128,1536]{1,0:T(8,128)(2,1)S(1)} %convert_element_type.137), channel_id=1, source_target_pairs={{0,2},{2,0},{1,3},{3,1},{4,6},{6,4},{5,7},{7,5},{8,10},{10,8},{9,1... | collective-permute-start | bytes 1179656 | tf_op jit(solution)/shard_map/ppermute | solution.py:1697
  116.6 19.4 %collective-permute-start.25 = (f16[128,1536]{1,0:T(8,128)(2,1)S(1)}, f16[128,1536]{1,0:T(8,128)(2,1)S(1)}, u32[]{:S(2)}, u32[]{:S(2)}) collective-permute-start(f16[128,1536]{1,0:T(8,128)(2,1)S(1)} %convert_element_type.146), channel_id=1, source_target_pairs={{0,1},{1,0},{2,3},{3,2},{4,5},{5,4},{6,7},{7,6},{8,9},{9,8},{10,11... | collective-permute-start | bytes 1179656 | tf_op jit(solution)/shard_map/ppermute | solution.py:1697
  131.5 52.7 %collective-permute-start.24 = (bf16[384,2688]{1,0:T(8,128)(2,1)S(1)}, bf16[384,2688]{1,0:T(8,128)(2,1)S(1)}, u32[]{:S(2)}, u32[]{:S(2)}) collective-permute-start(bf16[384,2688]{1,0:T(8,128)(2,1)S(1)} %broadcast_add_fusion.refs_10_.refs_4_.refs_6_.refs_20_.refs_24_), channel_id=1, source_target_pairs={{0,16},{16,0},{1,17},{17,1},{2,18},{18,2},{3,19},{19,3},{4,20},{20... | collective-permute-start | bytes 6193160 | tf_op jit(solution)/shard_map/ppermute | solution.py:1631
  136.1 21.8 %collective-permute-start.26 = (f16[128,1536]{1,0:T(8,128)(2,1)S(1)}, f16[128,1536]{1,0:T(8,128)(2,1)S(1)}, u32[]{:S(2)}, u32[]{:S(2)}) collective-permute-start(f16[128,1536]{1,0:T(8,128)(2,1)S(1)} %add_convert_fusion.1), channel_id=1, source_target_pairs={{0,2},{2,0},{1,3},{3,1},{4,6},{6,4},{5,7},{7,5},{8,10},{10,8},{9,1... | collective-permute-start | bytes 1179656 | tf_op jit(solution)/shard_map/ppermute | solution.py:1697
  136.2 21.9 %collective-permute-start.19 = (f32[8,1536]{1,0:T(8,128)S(1)}, f32[8,1536]{1,0:T(8,128)S(1)}, u32[]{:S(2)}, u32[]{:S(2)}) collective-permute-start(f32[8,1536]{1,0:T(8,128)S(1)} %get-tuple-element.167.refs_2_), channel_id=1, source_target_pairs={{0,3},{1,0},{2,1},{3,2},{4,7},{5,4},{6,5},{7,6},{8,11},{9,8},{10,9... | collective-permute-start | bytes 147464 | tf_op jit(solution)/shard_map/ppermute | solution.py:1679
  138.9 28.9 %collective-permute-start.18 = (f32[8,1536]{1,0:T(8,128)S(1)}, f32[8,1536]{1,0:T(8,128)S(1)}, u32[]{:S(2)}, u32[]{:S(2)}) collective-permute-start(f32[8,1536]{1,0:T(8,128)S(1)} %get-tuple-element.167.refs_2_), channel_id=1, source_target_pairs={{0,2},{1,3},{2,0},{3,1},{4,6},{5,7},{6,4},{7,5},{8,10},{9,11},{10,... | collective-permute-start | bytes 147464 | tf_op jit(solution)/shard_map/ppermute | solution.py:1679
  139.1 28.7 %collective-permute-start.17 = (f32[8,1536]{1,0:T(8,128)S(1)}, f32[8,1536]{1,0:T(8,128)S(1)}, u32[]{:S(2)}, u32[]{:S(2)}) collective-permute-start(f32[8,1536]{1,0:T(8,128)S(1)} %get-tuple-element.167.refs_2_), channel_id=1, source_target_pairs={{0,1},{1,2},{2,3},{3,0},{4,5},{5,6},{6,7},{7,4},{8,9},{9,10},{10,1... | collective-permute-start | bytes 147464 | tf_op jit(solution)/shard_map/ppermute | solution.py:1679
  158.0 26.1 %collective-permute-start.28 = (f16[128,1536]{1,0:T(8,128)(2,1)S(1)}, f16[128,1536]{1,0:T(8,128)(2,1)S(1)}, u32[]{:S(2)}, u32[]{:S(2)}) collective-permute-start(f16[128,1536]{1,0:T(8,128)(2,1)S(1)} %get-tuple-element.341), channel_id=1, source_target_pairs={{0,2},{2,0},{1,3},{3,1},{4,6},{6,4},{5,7},{7,5},{8,10},{10,8},{9,1... | collective-permute-start | bytes 1179656 | tf_op jit(solution)/shard_map/ppermute | solution.py:1697
  158.1 25.8 %collective-permute-start.27 = (f16[128,1536]{1,0:T(8,128)(2,1)S(1)}, f16[128,1536]{1,0:T(8,128)(2,1)S(1)}, u32[]{:S(2)}, u32[]{:S(2)}) collective-permute-start(f16[128,1536]{1,0:T(8,128)(2,1)S(1)} %get-tuple-element.343), channel_id=1, source_target_pairs={{0,1},{1,0},{2,3},{3,2},{4,5},{5,4},{6,7},{7,6},{8,9},{9,8},{10,11... | collective-permute-start | bytes 1179656 | tf_op jit(solution)/shard_map/ppermute | solution.py:1697
  168.6 15.6 %collective-permute-start.20 = (f32[8,1536]{1,0:T(8,128)S(1)}, f32[8,1536]{1,0:T(8,128)S(1)}, u32[]{:S(2)}, u32[]{:S(2)}) collective-permute-start(f32[8,1536]{1,0:T(8,128)S(1)} %convert_add_fusion), channel_id=1, source_target_pairs={{0,4},{1,5},{2,6},{3,7},{8,12},{9,13},{10,14},{11,15},{16,20},{17,... | collective-permute-start | bytes 147464 | tf_op jit(solution)/shard_map/ppermute | solution.py:1636
  194.7 71.8 %collective-permute-start.29 = (f32[512,1536]{1,0:T(8,128)}, f32[512,1536]{1,0:T(8,128)S(1)}, u32[]{:S(2)}, u32[]{:S(2)}) collective-permute-start(f32[512,1536]{1,0:T(8,128)} %get-tuple-element.172.refs_10_.refs_2_.refs_1_.own0), channel_id=1, source_target_pairs={{0,16},{16,0},{1,17},{17,1},{2,18},{18,2},{3,19},{19,3},{4,20},{20... | collective-permute-start | bytes 9437192 | tf_op jit(solution)/shard_map/ppermute | solution.py:1631
  194.7 15.9 %collective-permute-start.30 = (f32[128,768]{1,0:T(8,128)S(1)}, f32[128,768]{1,0:T(8,128)S(1)}, u32[]{:S(2)}, u32[]{:S(2)}) collective-permute-start(f32[128,768]{1,0:T(8,128)S(1)} %get-tuple-element.180), channel_id=1, source_target_pairs={{0,4},{1,5},{2,6},{3,7},{8,12},{9,13},{10,14},{11,15},{16,20},{17,... | collective-permute-start | bytes 1179656 | tf_op jit(solution)/shard_map/ppermute | solution.py:1636
  223.0 17.2 %collective-permute-start.35 = (f32[128,768]{1,0:T(8,128)S(1)}, f32[128,768]{1,0:T(8,128)S(1)}, u32[]{:S(2)}, u32[]{:S(2)}) collective-permute-start(f32[128,768]{1,0:T(8,128)S(1)} %get-tuple-element.189), channel_id=1, source_target_pairs={{4,0},{5,1},{6,2},{7,3},{12,8},{13,9},{14,10},{15,11},{20,16},{21,... | collective-permute-start | bytes 1179656 | tf_op jit(solution)/shard_map/ppermute | solution.py:1636
  229.0 17.1 %collective-permute-start.34 = (bf16[128,1536]{1,0:T(8,128)(2,1)S(1)}, bf16[128,1536]{1,0:T(8,128)(2,1)S(1)}, u32[]{:S(2)}, u32[]{:S(2)}) collective-permute-start(bf16[128,1536]{1,0:T(8,128)(2,1)S(1)} %get-tuple-element.184), channel_id=1, source_target_pairs={{0,1},{1,0},{2,3},{3,2},{4,5},{5,4},{6,7},{7,6},{8,9},{9,8},{10,11... | collective-permute-start | bytes 1179656 | tf_op jit(solution)/shard_map/ppermute | solution.py:1697
  229.2 18.9 %collective-permute-start.38 = (bf16[128,1536]{1,0:T(8,128)(2,1)S(1)}, bf16[128,1536]{1,0:T(8,128)(2,1)S(1)}, u32[]{:S(2)}, u32[]{:S(2)}) collective-permute-start(bf16[128,1536]{1,0:T(8,128)(2,1)S(1)} %get-tuple-element.206), channel_id=1, source_target_pairs={{0,1},{1,0},{2,3},{3,2},{4,5},{5,4},{6,7},{7,6},{8,9},{9,8},{10,11... | collective-permute-start | bytes 1179656 | tf_op jit(solution)/shard_map/ppermute | solution.py:1697
  246.2 19.9 %collective-permute-start.36 = (bf16[128,1536]{1,0:T(8,128)(2,1)S(1)}, bf16[128,1536]{1,0:T(8,128)(2,1)S(1)}, u32[]{:S(2)}, u32[]{:S(2)}) collective-permute-start(bf16[128,1536]{1,0:T(8,128)(2,1)S(1)} %merge.13.refs_26_.refs_0_), channel_id=1, source_target_pairs={{0,2},{2,0},{1,3},{3,1},{4,6},{6,4},{5,7},{7,5},{8,10},{10,8},{9,1... | collective-permute-start | bytes 1179656 | tf_op jit(solution)/shard_map/ppermute | solution.py:1697
  278.4 41.8 %collective-permute-start.47 = (bf16[2,192,1536]{2,1,0:T(8,128)(2,1)S(1)}, bf16[2,192,1536]{2,1,0:T(8,128)(2,1)S(1)}, u32[]{:S(2)}, u32[]{:S(2)}) collective-permute-start(bf16[2,192,1536]{2,1,0:T(8,128)(2,1)S(1)} %get-tuple-element.223), channel_id=1, source_target_pairs={{0,4},{4,0},{1,5},{5,1},{2,6},{6,2},{3,7},{7,3},{8,12},{12,8},{9,1... | collective-permute-start | bytes 3538952 | tf_op jit(solution)/shard_map/ppermute | solution.py:1631
  278.5 41.8 %collective-permute-start.46 = (bf16[2,192,1536]{2,1,0:T(8,128)(2,1)S(1)}, bf16[2,192,1536]{2,1,0:T(8,128)(2,1)S(1)}, u32[]{:S(2)}, u32[]{:S(2)}) collective-permute-start(bf16[2,192,1536]{2,1,0:T(8,128)(2,1)S(1)} %get-tuple-element.216.refs_4_), channel_id=1, source_target_pairs={{0,8},{8,0},{1,9},{9,1},{2,10},{10,2},{3,11},{11,3},{4,12},{12,4},... | collective-permute-start | bytes 3538952 | tf_op jit(solution)/shard_map/ppermute | solution.py:1631
  281.3 19.0 %collective-permute-start.39 = (bf16[128,1536]{1,0:T(8,128)(2,1)S(1)}, bf16[128,1536]{1,0:T(8,128)(2,1)S(1)}, u32[]{:S(2)}, u32[]{:S(2)}) collective-permute-start(bf16[128,1536]{1,0:T(8,128)(2,1)S(1)} %get-tuple-element.213), channel_id=1, source_target_pairs={{0,1},{1,0},{2,3},{3,2},{4,5},{5,4},{6,7},{7,6},{8,9},{9,8},{10,11... | collective-permute-start | bytes 1179656 | tf_op jit(solution)/shard_map/ppermute | solution.py:1697
  282.9 20.0 %collective-permute-start.40 = (bf16[128,1536]{1,0:T(8,128)(2,1)S(1)}, bf16[128,1536]{1,0:T(8,128)(2,1)S(1)}, u32[]{:S(2)}, u32[]{:S(2)}) collective-permute-start(bf16[128,1536]{1,0:T(8,128)(2,1)S(1)} %get-tuple-element.214), channel_id=1, source_target_pairs={{0,2},{2,0},{1,3},{3,1},{4,6},{6,4},{5,7},{7,5},{8,10},{10,8},{9,1... | collective-permute-start | bytes 1179656 | tf_op jit(solution)/shard_map/ppermute | solution.py:1697
  303.0 17.0 %collective-permute-start.42 = (bf16[128,1536]{1,0:T(8,128)(2,1)S(1)}, bf16[128,1536]{1,0:T(8,128)(2,1)S(1)}, u32[]{:S(2)}, u32[]{:S(2)}) collective-permute-start(bf16[128,1536]{1,0:T(8,128)(2,1)S(1)} %get-tuple-element.217.refs_0_), channel_id=1, source_target_pairs={{0,2},{2,0},{1,3},{3,1},{4,6},{6,4},{5,7},{7,5},{8,10},{10,8},{9,1... | collective-permute-start | bytes 1179656 | tf_op jit(solution)/shard_map/ppermute | solution.py:1697
  303.4 16.6 %collective-permute-start.43 = (bf16[128,1536]{1,0:T(8,128)(2,1)S(1)}, bf16[128,1536]{1,0:T(8,128)(2,1)S(1)}, u32[]{:S(2)}, u32[]{:S(2)}) collective-permute-start(bf16[128,1536]{1,0:T(8,128)(2,1)S(1)} %get-tuple-element.218.refs_1_), channel_id=1, source_target_pairs={{0,1},{1,0},{2,3},{3,2},{4,5},{5,4},{6,7},{7,6},{8,9},{9,8},{10,11... | collective-permute-start | bytes 1179656 | tf_op jit(solution)/shard_map/ppermute | solution.py:1697
  322.9 16.6 %collective-permute-start.44 = (bf16[128,1536]{1,0:T(8,128)(2,1)S(1)}, bf16[128,1536]{1,0:T(8,128)(2,1)S(1)}, u32[]{:S(2)}, u32[]{:S(2)}) collective-permute-start(bf16[128,1536]{1,0:T(8,128)(2,1)S(1)} %get-tuple-element.219.refs_5_), channel_id=1, source_target_pairs={{0,1},{1,0},{2,3},{3,2},{4,5},{5,4},{6,7},{7,6},{8,9},{9,8},{10,11... | collective-permute-start | bytes 1179656 | tf_op jit(solution)/shard_map/ppermute | solution.py:1697
  324.6 17.6 %collective-permute-start.45 = (bf16[128,1536]{1,0:T(8,128)(2,1)S(1)}, bf16[128,1536]{1,0:T(8,128)(2,1)S(1)}, u32[]{:S(2)}, u32[]{:S(2)}) collective-permute-start(bf16[128,1536]{1,0:T(8,128)(2,1)S(1)} %get-tuple-element.220.refs_4_.refs_7_), channel_id=1, source_target_pairs={{0,2},{2,0},{1,3},{3,1},{4,6},{6,4},{5,7},{7,5},{8,10},{10,8},{9,1... | collective-permute-start | bytes 1179656 | tf_op jit(solution)/shard_map/ppermute | solution.py:1697
  349.8 31.5 %collective-permute-start.55 = (f32[512,1536]{1,0:T(8,128)S(1)}, f32[512,1536]{1,0:T(8,128)S(1)}, u32[]{:S(2)}, u32[]{:S(2)}) collective-permute-start(f32[512,1536]{1,0:T(8,128)S(1)} %get-tuple-element.250.refs_1_.own1), channel_id=1, source_target_pairs={{0,16},{16,0},{1,17},{17,1},{2,18},{18,2},{3,19},{19,3},{4,20},{20... | collective-permute-start | bytes 9437192 | tf_op jit(solution)/shard_map/ppermute | solution.py:1631
  354.6 20.7 %collective-permute-start.51 = (bf16[128,1536]{1,0:T(8,128)(2,1)S(1)}, bf16[128,1536]{1,0:T(8,128)(2,1)S(1)}, u32[]{:S(2)}, u32[]{:S(2)}) collective-permute-start(bf16[128,1536]{1,0:T(8,128)(2,1)S(1)} %hold.7.refs_12_), channel_id=1, source_target_pairs={{0,2},{2,0},{1,3},{3,1},{4,6},{6,4},{5,7},{7,5},{8,10},{10,8},{9,1... | collective-permute-start | bytes 1179656 | tf_op jit(solution)/shard_map/ppermute | solution.py:1697
  355.1 21.7 %collective-permute-start.50 = (bf16[128,1536]{1,0:T(8,128)(2,1)S(1)}, bf16[128,1536]{1,0:T(8,128)(2,1)S(1)}, u32[]{:S(2)}, u32[]{:S(2)}) collective-permute-start(bf16[128,1536]{1,0:T(8,128)(2,1)S(1)} %hold.6.refs_13_), channel_id=1, source_target_pairs={{0,1},{1,0},{2,3},{3,2},{4,5},{5,4},{6,7},{7,6},{8,9},{9,8},{10,11... | collective-permute-start | bytes 1179656 | tf_op jit(solution)/shard_map/ppermute | solution.py:1697
  375.4 17.0 %collective-permute-start.53 = (bf16[128,1536]{1,0:T(8,128)(2,1)S(1)}, bf16[128,1536]{1,0:T(8,128)(2,1)S(1)}, u32[]{:S(2)}, u32[]{:S(2)}) collective-permute-start(bf16[128,1536]{1,0:T(8,128)(2,1)S(1)} %merge.18.refs_27_.refs_4_), channel_id=1, source_target_pairs={{0,1},{1,0},{2,3},{3,2},{4,5},{5,4},{6,7},{7,6},{8,9},{9,8},{10,11... | collective-permute-start | bytes 1179656 | tf_op jit(solution)/shard_map/ppermute | solution.py:1697
  393.6 16.8 %collective-permute-start.59 = (bf16[512,1536]{1,0:T(8,128)(2,1)S(1)}, bf16[512,1536]{1,0:T(8,128)(2,1)S(1)}, u32[]{:S(2)}, u32[]{:S(2)}) collective-permute-start(bf16[512,1536]{1,0:T(8,128)(2,1)S(1)} %get-tuple-element.260), channel_id=1, source_target_pairs={{0,16},{16,0},{1,17},{17,1},{2,18},{18,2},{3,19},{19,3},{4,20},{20... | collective-permute-start | bytes 4718600 | tf_op jit(solution)/shard_map/ppermute | solution.py:1631
  393.7 71.3 %collective-permute-start.56 = (f32[512,1536]{1,0:T(8,128)S(1)}, f32[512,1536]{1,0:T(8,128)S(1)}, u32[]{:S(2)}, u32[]{:S(2)}) collective-permute-start(f32[512,1536]{1,0:T(8,128)S(1)} %join.1.refs_3_.own1), channel_id=1, source_target_pairs={{0,16},{16,0},{1,17},{17,1},{2,18},{18,2},{3,19},{19,3},{4,20},{20... | collective-permute-start | bytes 9437192 | tf_op jit(solution)/shard_map/ppermute | solution.py:1631
  419.1 27.9 %collective-permute-start.66 = (bf16[2,192,1536]{2,1,0:T(8,128)(2,1)S(1)}, bf16[2,192,1536]{2,1,0:T(8,128)(2,1)S(1)}, u32[]{:S(2)}, u32[]{:S(2)}) collective-permute-start(bf16[2,192,1536]{2,1,0:T(8,128)(2,1)S(1)} %get-tuple-element.268), channel_id=1, source_target_pairs={{0,4},{4,0},{1,5},{5,1},{2,6},{6,2},{3,7},{7,3},{8,12},{12,8},{9,1... | collective-permute-start | bytes 3538952 | tf_op jit(solution)/shard_map/ppermute | solution.py:1631
  419.1 27.8 %collective-permute-start.65 = (bf16[2,192,1536]{2,1,0:T(8,128)(2,1)S(1)}, bf16[2,192,1536]{2,1,0:T(8,128)(2,1)S(1)}, u32[]{:S(2)}, u32[]{:S(2)}) collective-permute-start(bf16[2,192,1536]{2,1,0:T(8,128)(2,1)S(1)} %get-tuple-element.263.refs_4_), channel_id=1, source_target_pairs={{0,8},{8,0},{1,9},{9,1},{2,10},{10,2},{3,11},{11,3},{4,12},{12,4},... | collective-permute-start | bytes 3538952 | tf_op jit(solution)/shard_map/ppermute | solution.py:1631
  420.3 16.3 %collective-permute-start.57 = (bf16[128,1536]{1,0:T(8,128)(2,1)S(1)}, bf16[128,1536]{1,0:T(8,128)(2,1)S(1)}, u32[]{:S(2)}, u32[]{:S(2)}) collective-permute-start(bf16[128,1536]{1,0:T(8,128)(2,1)S(1)} %get-tuple-element.257), channel_id=1, source_target_pairs={{0,1},{1,0},{2,3},{3,2},{4,5},{5,4},{6,7},{7,6},{8,9},{9,8},{10,11... | collective-permute-start | bytes 1179656 | tf_op jit(solution)/shard_map/ppermute | solution.py:1697
  422.3 23.0 %collective-permute-start.58 = (bf16[128,1536]{1,0:T(8,128)(2,1)S(1)}, bf16[128,1536]{1,0:T(8,128)(2,1)S(1)}, u32[]{:S(2)}, u32[]{:S(2)}) collective-permute-start(bf16[128,1536]{1,0:T(8,128)(2,1)S(1)} %get-tuple-element.258), channel_id=1, source_target_pairs={{0,2},{2,0},{1,3},{3,1},{4,6},{6,4},{5,7},{7,5},{8,10},{10,8},{9,1... | collective-permute-start | bytes 1179656 | tf_op jit(solution)/shard_map/ppermute | solution.py:1697
  445.5 17.0 %collective-permute-start.64 = (bf16[128,1536]{1,0:T(8,128)(2,1)S(1)}, bf16[128,1536]{1,0:T(8,128)(2,1)S(1)}, u32[]{:S(2)}, u32[]{:S(2)}) collective-permute-start(bf16[128,1536]{1,0:T(8,128)(2,1)S(1)} %get-tuple-element.265.refs_4_.refs_1_), channel_id=1, source_target_pairs={{0,1},{1,0},{2,3},{3,2},{4,5},{5,4},{6,7},{7,6},{8,9},{9,8},{10,11... | collective-permute-start | bytes 1179656 | tf_op jit(solution)/shard_map/ppermute | solution.py:1697
  447.4 23.4 %collective-permute-start.70 = (bf16[192,1536]{1,0:T(8,128)(2,1)S(1)}, bf16[192,1536]{1,0:T(8,128)(2,1)S(1)}, u32[]{:S(2)}, u32[]{:S(2)}) collective-permute-start(bf16[192,1536]{1,0:T(8,128)(2,1)S(1)} %get-tuple-element.275), channel_id=1, source_target_pairs={{0,8},{8,0},{1,9},{9,1},{2,10},{10,2},{3,11},{11,3},{4,12},{12,4},... | collective-permute-start | bytes 1769480 | tf_op jit(solution)/shard_map/ppermute | solution.py:1631
  448.4 22.4 %collective-permute-start.69 = (bf16[192,1536]{1,0:T(8,128)(2,1)S(1)}, bf16[192,1536]{1,0:T(8,128)(2,1)S(1)}, u32[]{:S(2)}, u32[]{:S(2)}) collective-permute-start(bf16[192,1536]{1,0:T(8,128)(2,1)S(1)} %get-tuple-element.269.refs_4_), channel_id=1, source_target_pairs={{0,4},{4,0},{1,5},{5,1},{2,6},{6,2},{3,7},{7,3},{8,12},{12,8},{9,1... | collective-permute-start | bytes 1769480 | tf_op jit(solution)/shard_map/ppermute | solution.py:1631
  462.8 24.6 %collective-permute-start.67 = (bf16[128,1536]{1,0:T(8,128)(2,1)S(1)}, bf16[128,1536]{1,0:T(8,128)(2,1)S(1)}, u32[]{:S(2)}, u32[]{:S(2)}) collective-permute-start(bf16[128,1536]{1,0:T(8,128)(2,1)S(1)} %get-tuple-element.272.refs_5_), channel_id=1, source_target_pairs={{0,1},{1,0},{2,3},{3,2},{4,5},{5,4},{6,7},{7,6},{8,9},{9,8},{10,11... | collective-permute-start | bytes 1179656 | tf_op jit(solution)/shard_map/ppermute | solution.py:1697
  462.9 24.5 %collective-permute-start.68 = (bf16[128,1536]{1,0:T(8,128)(2,1)S(1)}, bf16[128,1536]{1,0:T(8,128)(2,1)S(1)}, u32[]{:S(2)}, u32[]{:S(2)}) collective-permute-start(bf16[128,1536]{1,0:T(8,128)(2,1)S(1)} %get-tuple-element.270.refs_0_.refs_7_), channel_id=1, source_target_pairs={{0,2},{2,0},{1,3},{3,1},{4,6},{6,4},{5,7},{7,5},{8,10},{10,8},{9,1... | collective-permute-start | bytes 1179656 | tf_op jit(solution)/shard_map/ppermute | solution.py:1697
  471.7 15.6 %collective-permute-start.71 = (f32[96,256]{1,0:T(8,128)S(1)}, f32[96,256]{1,0:T(8,128)S(1)}, u32[]{:S(2)}, u32[]{:S(2)}) collective-permute-start(f32[96,256]{1,0:T(8,128)S(1)} %get-tuple-element.280), channel_id=1, source_target_pairs={{0,1},{1,0},{2,3},{3,2},{4,5},{5,4},{6,7},{7,6},{8,9},{9,8},{10,11... | collective-permute-start | bytes 294920 | tf_op jit(solution)/shard_map/ppermute | solution.py:1697
  492.1 16.7 %collective-permute-start.80 = (bf16[384,1152]{1,0:T(8,128)(2,1)S(1)}, bf16[384,1152]{1,0:T(8,128)(2,1)S(1)}, u32[]{:S(2)}, u32[]{:S(2)}) collective-permute-start(bf16[384,1152]{1,0:T(8,128)(2,1)S(1)} %copy-done.66), channel_id=1, source_target_pairs={{0,16},{16,0},{1,17},{17,1},{2,18},{18,2},{3,19},{19,3},{4,20},{20... | collective-permute-start | bytes 2654216 | tf_op jit(solution)/shard_map/ppermute | solution.py:1631
  (126 other events, 1375.3 us)

commit v3 on v2

--- a/solution.py
+++ b/solution.py
@@ -303,9 +303,10 @@
     out_ref[...] = jnp.where(mask_ref[...] > 0.0, total, a_ref[...])
 
 
-def vector_call(mask, values):
-    return pl.pallas_call(
+def vector_call(mask, values, *ahead):
+    return ordered_call(
         vector_kernel,
+        ahead,
         in_specs=[pl.BlockSpec(memory_space=pltpu.VMEM)] * 5,
         out_specs=pl.BlockSpec(memory_space=pltpu.VMEM),
         out_shape=shape(*mask.shape),
@@ -885,12 +886,13 @@
     total[...] = total[...] * jnp.exp(cum[rows - 1 : rows, :])
 
 
-def gate_back_call(grad_scaled, comb, z, conv_s, cum, sums, pack, spread_matrix):
+def gate_back_call(grad_scaled, comb, z, conv_s, cum, sums, pack, spread_matrix, *ahead):
     length, width = z.shape
     rows = min(SPAN, length)
     chunks = length // rows
-    return pl.pallas_call(
+    return ordered_call(
         gate_back_kernel,
+        ahead,
         grid=(chunks,),
         in_specs=[
             chunk_of(rows, width, chunks),
@@ -1468,17 +1470,19 @@
     refs[-1][0] = block_grads(*refs[:-1])
 
 
-def wgrad_relative_kernel(extra, where_ref, *refs):
+def wgrad_relative_kernel(extra, alike, where_ref, *refs):
     value = block_grads(*refs[:6])
     first_give, first_keep, second_give, second_keep = refs[6 + extra :]
     half = value.shape[0] // 2
     step = pl.program_id(0)
 
-    @pl.when(step < 2)
+    first_sent = step % 2 == 1 if alike else step < 2
+
+    @pl.when(first_sent)
     def _():
         first_give[0] = value[:half]
 
-    @pl.when(step >= 2)
+    @pl.when(jnp.logical_not(first_sent))
     def _():
         first_keep[0] = value[:half]
 
@@ -1491,7 +1495,7 @@
         second_keep[0] = value[half:]
 
 
-def wgrad_call(where, spans, normed, normed_other, g_low, g_other, keep, got, *ahead):
+def wgrad_call(where, spans, alike, normed, normed_other, g_low, g_other, keep, got, *ahead):
     length, model = normed.shape
     size = keep.shape[1]
     blocks = spans[0] * spans[1]
@@ -1526,8 +1530,10 @@
         lambda b, where_ref: (1 - b // 2, 0, 0),
         lambda b, where_ref: (1 - b // 2, 0, 0),
     ]
+    if alike:
+        maps = maps[2:] * 2
     return pl.pallas_call(
-        functools.partial(wgrad_relative_kernel, len(ahead)),
+        functools.partial(wgrad_relative_kernel, len(ahead), alike),
         grid_spec=pltpu.PrefetchScalarGridSpec(
             num_scalar_prefetch=1,
             grid=(4,),
@@ -1569,35 +1575,41 @@
 
 def summed_kernel(where_ref, first_keep, first_got, second_keep, second_got, *refs):
     rows = first_keep.shape[0]
-    above, (matrices_ref, steps_ref, *states_refs) = (None, refs) if len(refs) == 3 else (refs[0], refs[1:])
+    above, outs = (None, refs) if len(refs) == 3 else (refs[:2], refs[2:])
+    matrices_ref, steps_ref = outs[:2]
     width = matrices_ref.shape[1]
+    lower = where_ref[CORE] == 0
     states = []
     for at, keep, got in ((slice(0, rows), first_keep, first_got), (slice(rows, 2 * rows), second_keep, second_got)):
         total = keep[...] + whole_states(got[...], width)
-        matrices_ref[at, :] = total[:, :width].astype(BF16)
+        matrices = total[:, :width].astype(BF16)
         states.append(total[:, width : width + NSTATE])
         steps_ref[at, :] = total[:, width + NSTATE :]
+        if above is None:
+            matrices_ref[at, :] = matrices
+        else:
+            other = above[0][at, :]
+            matrices_ref[at, :] = jnp.where(lower, matrices, other)
+            outs[2][at, :] = jnp.where(lower, other, matrices)
     states = jnp.concatenate(states, axis=0)
     if above is None:
-        states_refs[0][...] = states
+        outs[2][...] = states
     else:
-        put_quarters(where_ref, jnp.concatenate([states, above[...]], axis=1), states_refs)
+        put_quarters(where_ref, jnp.concatenate([states, above[1][...]], axis=1), outs[3:])
 
 
 def summed_call(where, operands, above, *ahead):
     rows, size = operands[1].shape
     width = size - 2 * NSTATE - LANES
-    states = quarter_shapes(2 * rows, 2 * NSTATE, F32) if above else [shape(2 * rows, NSTATE)]
+    matrices = shape(2 * rows, width, dtype=BF16)
+    more = [matrices] + quarter_shapes(2 * rows, 2 * NSTATE, F32) if above else [shape(2 * rows, NSTATE)]
+    outs = [matrices, shape(2 * rows, LANES)] + more
     return ordered_call(
         summed_kernel,
         ahead,
         in_specs=[scalars_of()] + [pl.BlockSpec(memory_space=pltpu.VMEM)] * (4 + len(above)),
-        out_specs=[pl.BlockSpec(memory_space=pltpu.VMEM)] * (2 + len(states)),
-        out_shape=[
-            shape(2 * rows, width, dtype=BF16),
-            shape(2 * rows, LANES),
-        ]
-        + states,
+        out_specs=[pl.BlockSpec(memory_space=pltpu.VMEM)] * len(outs),
+        out_shape=outs,
         compiler_params=pltpu.CompilerParams(vmem_limit_bytes=16 * 1024 * 1024),
         cost_estimate=cost(0, 0),
         name="summed",
@@ -1660,7 +1672,7 @@
 def carried_state(state, rate_wide, axis, backward):
     count = lax.axis_size(axis)
     if count == 2:
-        return shifted_along(state, axis, -1 if backward else 1)
+        return shifted_along(state.astype(BF16), axis, -1 if backward else 1).astype(F32)
     here = lax.axis_index(axis)
     states = lax.all_gather(state, axis)
     rates = lax.all_gather(rate_wide, axis)
@@ -1700,7 +1712,10 @@
 
     def _merge(self, firsts, seconds, ahead):
         if self.kind == jnp.float16:
-            return [(a.astype(F32) + b.astype(F32)).astype(self.kind) for a, b in zip(firsts, seconds)]
+            firsts, seconds = [v.astype(F32) for v in firsts], [v.astype(F32) for v in seconds]
+            merged = merge_call(firsts, seconds, F32, *ahead)
+            self.event = merged[-1]
+            return [v.astype(self.kind) for v in merged]
         return merge_call(firsts, seconds, self.kind, *ahead)
 
     def add(self, *ahead):
@@ -1736,19 +1751,21 @@
 
 
 class ScatterSum:
-    def __init__(self, value):
+    def __init__(self, value, alike, *ahead):
         self.whole = None
+        self.orders = (("context", "fsdp") if alike else ("fsdp", "context"), ("context", "fsdp"))
         if not isinstance(value, (list, tuple)):
             self.whole = lax.psum_scatter(value, ("fsdp", "context"), scatter_dimension=0, tiled=False)
             return
         self.keeps = [value[1], value[3]]
-        self.given = [swap(value[0], "fsdp"), swap(value[2], "context")]
+        gives = hold_call([value[0], value[2]], *ahead)
+        self.given = [swap(give, order[0]) for give, order in zip(gives, self.orders)]
 
     def turn(self, *ahead):
         if self.whole is not None:
             return self.whole
         gives, self.keeps = turn_call(self.keeps, self.given, *ahead)
-        self.given = [swap(gives[0], "context"), swap(gives[1], "fsdp")]
+        self.given = [swap(give, order[1]) for give, order in zip(gives, self.orders)]
         return gives[0]
 
     def result(self, where, above, *ahead):
@@ -1761,12 +1778,14 @@
         return summed_call(where, operands, above, *ahead)
 
 
-def rest_kernel(where_ref, t0, o0, t1, o1, steps0, steps1, out_ref):
+def rest_kernel(where_ref, t0, o0, t1, o1, steps0, steps1, own_ref, send_ref):
     rows = steps0.shape[0]
     states = joined(where_ref, (t0, o0, t1, o1), slice(0, rows))
-    out_ref[...] = jnp.concatenate(
-        [states[:, :NSTATE], steps0[...], states[:, NSTATE:], steps1[...]], axis=1
-    )
+    first = jnp.concatenate([states[:, :NSTATE], steps0[...]], axis=1)
+    second = jnp.concatenate([states[:, NSTATE:], steps1[...]], axis=1)
+    lower = where_ref[CORE] == 0
+    own_ref[...] = jnp.where(lower, first, second)
+    send_ref[...] = jnp.where(lower, second, first)
 
 
 def rest_call(where, quarters, steps0, steps1, *ahead):
@@ -1774,32 +1793,31 @@
         rest_kernel,
         ahead,
         in_specs=[scalars_of()] + [pl.BlockSpec(memory_space=pltpu.VMEM)] * 6,
-        out_specs=pl.BlockSpec(memory_space=pltpu.VMEM),
-        out_shape=shape(steps0.shape[0], 2 * (NSTATE + LANES)),
+        out_specs=[pl.BlockSpec(memory_space=pltpu.VMEM)] * 2,
+        out_shape=[shape(steps0.shape[0], NSTATE + LANES)] * 2,
         compiler_params=pltpu.CompilerParams(vmem_limit_bytes=8 * 1024 * 1024),
         cost_estimate=cost(0, 0),
         name="rest",
     )(where, *quarters, steps0, steps1)
 
 
-def matrices_kernel(where_ref, m0, r0, m1, r1, rest, rest_got, main_ref, states_ref, step_ref, out_ref):
-    def put(lower, upper, lower_rest, upper_rest, column):
+def matrices_kernel(where_ref, own, got, rest, rest_got, main_ref, states_ref, step_ref, out_ref):
+    def put(lower, upper, lower_rest, upper_rest):
         half = main_ref.shape[3] // 2
         a, b = lower[...].astype(F32), upper[...].astype(F32)
         main_ref[0, :, 0, :] = jnp.concatenate([a[:, :half], b[:, :half]], axis=1)
         main_ref[0, :, 1, :] = jnp.concatenate([a[:, half : 2 * half], b[:, half : 2 * half]], axis=1)
         out_ref[0] = jnp.concatenate([a[:, 2 * half :], b[:, 2 * half :]], axis=1)
-        states = slice(column, column + NSTATE)
-        states_ref[0] = jnp.concatenate([lower_rest[:, states], upper_rest[:, states]], axis=1)
-        step_ref[0] = lower_rest[:, column + NSTATE : column + NSTATE + step_ref.shape[2]]
+        states_ref[0] = jnp.concatenate([lower_rest[:, :NSTATE], upper_rest[:, :NSTATE]], axis=1)
+        step_ref[0] = lower_rest[:, NSTATE : NSTATE + step_ref.shape[2]]
 
     @pl.when(where_ref[CORE] == 0)
     def _():
-        put(m0, r0, rest, rest_got, 0)
+        put(own, got, rest, rest_got)
 
     @pl.when(where_ref[CORE] == 1)
     def _():
-        put(r1, m1, rest_got, rest, NSTATE + LANES)
+        put(got, own, rest_got, rest)
 
 
 def matrices_call(where, heads, *arrays):
@@ -2009,10 +2027,10 @@
         )
         return comb, gated, small_sum(sums)
 
-    def layer_gate_back(grad_scaled, sums, comb, z, front, rate_wide, layer):
+    def layer_gate_back(grad_scaled, sums, comb, z, front, rate_wide, layer, *ahead):
         _, _, _, _, _, conv_s, _, _, cum, _, _, _, _ = front
         dmix, dz, adj, adj_rate, begin, gained = gate_back_call(
-            grad_scaled, comb, z, conv_s, cum, sums, packs[layer], spread_matrix
+            grad_scaled, comb, z, conv_s, cum, sums, packs[layer], spread_matrix, *ahead
         )
         adj_in = carried_state(begin, rate_wide, "context", True)
         return dmix, dz, adj, adj_rate, adj_in, gained
@@ -2060,27 +2078,29 @@
         tokens, halo0, 0, fronts0, (), packs[1]
     )
     normed0 = front0[1]
-    gate_far0 = after(gate_far0, front0[-1])
+    y0 = mix_call(front0[4], front0[5], front0[7], front0[8], front0[9], spread_matrix)
+    gate_far0 = after(gate_far0, y0)
     gates0 = weights_of(0, (gate_far0, swap(gate_far0, "section")), 0, 0, 0)[1]
     out_far0 = swap(after(out_piece0, gate_far0), "fsdp")
-    y0 = mix_call(front0[4], front0[5], front0[7], front0[8], front0[9], spread_matrix)
     z0 = project_call(place, normed0, gates0)
     comb0, gated0, sums0 = layer_rest(front0, entry0, y0, z0, 0)
     out_far0 = after(out_far0, comb0)
     outs0 = weights_of(0, (out_far0, swap(out_far0, "section")), 0, 0, 0)[2]
-    pieces1 = pieces_call(place, 1, front_part + gate_part + out_part, held, out_far0)
-    far1 = swap(pieces1, "fsdp")
+    pieces1 = pieces_call(place, 1, front_part, held[:4], out_far0)
+    front_far1 = swap(pieces1, "fsdp")
+    rest_piece1 = pieces_call(place, 1, gate_part + out_part, held)
     low0, g0, k0, g1, k1, edge0 = out_call(place, gated0, sums0, packs[0], outs0, F32, pieces1)
 
     half16 = jnp.float16
     total0 = TensorSum([(0, g0.astype(half16), k0), (1, g1.astype(half16), k1)])
-    halo1 = shifted_along(tokens[length - 8 :].astype(F32) + small_sum(edge0), "context", 1)
-    total0.across()
-    event = total0.back()
-    fronts1, gates1, outs1 = weights_of(
-        1, both_halves_of(far1, event), 0, front_width, front_width + width
-    )
-    grad_scaled1 = project_call(place, cot, outs1)
+    event = total0.across()
+    edge0, rest_piece1 = hold_call([edge0, rest_piece1], total0.event)
+    rest_far1 = swap(rest_piece1, "fsdp")
+    edge0 = tokens[length - 8 :].astype(F32) + small_sum(edge0)
+    halo1 = shifted_along(edge0, "context", 1)
+    front_far1 = after(front_far1, event)
+    fronts1 = weights_of(1, (front_far1, swap(front_far1, "section")), 0, 0, 0)[0]
+    total0.back()
     normed_other0 = renorm_call(tokens_other, packs[0], edge0)
     branch0 = [v.astype(F32) for v in total0.quarters()]
 
@@ -2088,6 +2108,9 @@
         tokens, halo1, 1, fronts1, branch0
     )
     x1, normed1 = front1[:2]
+    rest_far1 = after(rest_far1, edge0)
+    _, gates1, outs1 = weights_of(1, (rest_far1, swap(rest_far1, "section")), 0, 0, width)
+    grad_scaled1 = project_call(place, cot, outs1)
     y1 = mix_call(front1[4], front1[5], front1[7], front1[8], front1[9], spread_matrix)
     z1 = project_call(place, normed1, gates1)
     comb1, gated1, sums1 = layer_rest(front1, entry1, y1, z1, 1, grad_scaled1)
@@ -2114,19 +2137,19 @@
     received1 = swap(send1, "section")
     x1_other = swap(x1, "section")
     normed_other1 = renorm_call(x1_other, packs[1], keep1)
-    matrices1 = wgrad_call(place, spans, normed1, normed_other1, cot, cot_other, keep1, received1)
-    scatter1 = ScatterSum(matrices1)
-    total1.across(jax.tree.leaves(matrices1)[0])
+    matrices1 = wgrad_call(place, spans, False, normed1, normed_other1, cot, cot_other, keep1, received1)
+    event = total1.across(jax.tree.leaves(matrices1)[0])
+    scatter1 = ScatterSum(matrices1, False, event)
     event = scatter1.turn(total1.back())
-    matrices1, steps1, states1 = scatter1.result(place, (), event)
     grad1, g_low0, grad_scaled0, sums0_back = finish_call(
-        place, total1.quarters(), cot, x1, front1[2], packs[1], (steps1,), branch0, sums0, outs0
-    )
-
+        place, total1.quarters(), cot, x1, front1[2], packs[1], (event,), branch0, sums0, outs0
+    )
+
+    matrices1, steps1, states1 = scatter1.result(place, (), sums0_back)
     gate_back0 = layer_gate_back(grad_scaled0, sums0_back, comb0, z0, front0, rate_wide0, 0)
     ahead = half_b.hold(sums0_back), half_a.spread(sums0_back)
     back0 = layer_mix_back(
-        gate_back0, front0, entry0, 0, ahead, lambda tick: ()
+        gate_back0, front0, entry0, 0, ahead, lambda tick: (steps1,)
     )
     tick = back0[3]
     grad_got1 = swap(grad1, "section")
@@ -2147,27 +2170,27 @@
     *gives, send0 = hold_call([give for _, give, _ in pieces] + [send0], x2)
     total0 = TensorSum([(half, give, keep) for (half, _, keep), give in zip(pieces, gives)])
     received0 = swap(send0, "section")
-    (vector,) = merge_call([vector], [swap(vector_send, "section")], F32)
-    (vector,) = merge_call([vector], [sum_given(vector, "fsdp")], F32)
-    (vector,) = merge_call([vector], [sum_given(vector, "context")], F32)
     matrices0 = wgrad_call(
         place,
         spans,
+        False,
         normed0,
         normed_other0,
         g_low0,
         grad_got1,
         keep0,
         received0,
-        vector,
-    )
-    scatter0 = ScatterSum(matrices0)
+    )
     event = total0.across(jax.tree.leaves(matrices0)[0])
+    scatter0 = ScatterSum(matrices0, False, event)
+    (vector,) = merge_call([vector], [swap(vector_send, "section")], F32, event)
+    vector_got = sum_given(vector, "fsdp")
     x2_other = swap(x2, "section")
-    event = scatter0.turn(event)
-    event = total0.back(event)
+    event = scatter0.turn(total0.back(vector))
     layer_out, event = tokens_call(place, x1, x1_other, x2, x2_other, event)
-    (vector,) = hold_call([vector], event)
+    matrices, steps0, matrices_send, *states = scatter0.result(place, (matrices1, states1), event)
+    (vector,) = merge_call([vector], [vector_got], F32, steps0)
+    (vector,) = merge_call([vector], [sum_given(vector, "context")], F32)
     count = lax.axis_size("tensor")
     vectors = [vector] + [
         lax.ppermute(vector, "tensor", [(i, (i + by) % count) for i in range(count)])
@@ -2177,11 +2200,8 @@
     lane = np.arange(both)[None, :]
     shared = ((row < SKIP) & (lane >= width)) | (row == NORM) | (row == NORM + 1)
     shared = jnp.asarray(shared.astype(np.float32))
-    vector = vector_call(shared, vectors)
-    matrices0, steps0, *states = scatter0.result(place, (states1,), event)
     states = TensorSum([(0, *states[:2]), (1, *states[2:])])
-    matrices_got1 = swap(matrices1, "section")
-    matrices_got0 = swap(matrices0, "section")
+    matrices_got = swap(matrices_send, "section")
     grad0 = finish_call(
         place,
         total0.quarters(),
@@ -2189,21 +2209,15 @@
         tokens,
         front0[2],
         packs[0],
-        (states.across(vector),),
+        (states.across(steps0), vector),
     )[0]
     grad_got0 = swap(grad0.astype(BF16), "section")
     event = states.back(grad0)
     layer_in_grad, event = tokens_call(place, grad0, grad_got0, grad1, grad_got1, event)
-    rest = rest_call(place, states.quarters(), steps0, steps1, event)
+    vector = vector_call(shared, vectors, event)
+    rest, rest_send = rest_call(place, states.quarters(), steps0, steps1, event)
     grad_main, grad_states, grad_step, grad_out = matrices_call(
-        place,
-        heads,
-        matrices0,
-        matrices_got0,
-        matrices1,
-        matrices_got1,
-        rest,
-        swap(rest, "section"),
+        place, heads, matrices, matrices_got, rest, swap(rest_send, "section")
     )
     return (
         layer_out,

time: 522 us -> 496 us (0.950)
  waiting for transfers between devices: 208 us -> 154 us
  starting transfers between devices: 97.8 us -> 111 us
  Pallas kernels: 158 us -> 165 us
    ppermute x30, waiting for transfers between devices: 141 us -> 111 us  [_send(): lax.ppermute(v, 'tensor', self.STEPS[half][step])]
    ppermute x3, waiting for transfers between devices: 13.6 us -> 0.01 us  [shards(): lax.ppermute(vector, 'tensor', [(i, (i + by) % count) for i in range(coun...]
    pallas_call x47 -> x55, Pallas kernels: 119 us -> 129 us  [ordered_call(): return lambda *operands: call(*operands, *ahead)]
    ppermute x32 -> x33, waiting for transfers between devices: 30.1 us -> 19.6 us  [swap(): return lax.ppermute(value, axis, [(0, 1), (1, 0)])]
    ppermute x10, starting transfers between devices: 27.2 us -> 35.9 us  [shifted_along(): lax.ppermute(value, axis, [(i, i + by) for i in range(count) if 0 <= i +...]
    pallas_call x5 -> x2, Pallas kernels: 23.6 us -> 17.2 us  [wgrad_call(): pl.pallas_call(functools.partial(wgrad_relative_kernel, len(ahead), alike...]
    ppermute x30, starting transfers between devices: 36.6 us -> 42.5 us  [_send(): lax.ppermute(v, 'tensor', self.STEPS[half][step])]
    ppermute x32 -> x33, starting transfers between devices: 19.5 us -> 20.6 us  [swap(): return lax.ppermute(value, axis, [(0, 1), (1, 0)])]
  transfers between devices with their start and end apart: 84 -> 85, of which waited for: 40 -> 32; matrix products, arithmetic and copies ran while one was open for 5% -> 5% of each run, Pallas kernels for 25% -> 30%
where the time goes in v3:
time: 496 us; the launch traced here: 486 us
  Pallas kernels  165 us (33%)
  waiting for transfers between devices  154 us (31%)
  starting transfers between devices  111 us (22%)
  local copies, waits for them, and re-layouts  38.1 us (8%)
  other arithmetic  8.82 us (2%)
  between operations  7.69 us (2%)
    pallas_call x55, Pallas kernels, ordered_call(): return lambda *operands: call(*operands, *ahead)  129 us
    ppermute x30, waiting for transfers between devices, _send(): lax.ppermute(v, 'tensor', self.STEPS[half][step])  111 us
    ppermute x30, starting transfers between devices, _send(): lax.ppermute(v, 'tensor', self.STEPS[half][step])  42.5 us
    ppermute x10, starting transfers between devices, shifted_along(): lax.ppermute(value, axis, [(i, i + by) for i in range(count) if 0 <= i +...  35.9 us
    unnamed x185, local copies, waits for them, and re-layouts  22.4 us
    ppermute x33, starting transfers between devices, swap(): return lax.ppermute(value, axis, [(0, 1), (1, 0)])  20.6 us
    ppermute x33, waiting for transfers between devices, swap(): return lax.ppermute(value, axis, [(0, 1), (1, 0)])  19.6 us
    pallas_call x2, Pallas kernels, wgrad_call(): pl.pallas_call(functools.partial(wgrad_relative_kernel, len(ahead), alike...  17.2 us
  transfers between devices with their start and end apart: 85, of which 32 were waited for; matrix products, arithmetic and copies ran while one was open for 5% of the time, Pallas kernels for 30%

profile of v3, /device:TPU:0, one launch (start us, length us, event | category | flops | bytes accessed | tf_op | source)
XLA Modules:
  0.0 485.8 jit_solution(14903719476066008932)
XLA Ops:
  19.6 3.0 collective-permute-start.6
  29.5 3.4 collective-permute-start.4
  35.0 4.5 collective-permute-start.2
  50.9 9.3 %front.2 = (f32[8,1536]{1,0:T(8,128)}, bf16[512,1536]{1,0:T(8,128)(2,1)S(1)}, f32[512,128]{1,0:T(8,128)S(1)}, f32[512,1024]{1,0:T(8,128)S(1)}, f32[512,768]{1,0:...) custom-call(s32[6]{0:T(128)S(1)} %stack.42.refs_0_.where_ref, ...), custom_call_target="tpu_custom_call" | custom-call | flops 1 | bytes 1 | tf_op jit(solution)/shard_map/front/pallas_call | solution.py:142
  68.8 3.7 collective-permute-start.10
  72.5 4.0 collective-permute-done.10
  84.4 3.7 collective-permute-start.13
  93.7 4.1 out.2
  102.6 14.9 %collective-permute-done.18 = f16[128,1536]{1,0:T(8,128)(2,1)S(1)} collective-permute-done((f16[128,1536]{1,0:T(8,128)(2,1)S(1)}, f16[128,1536]{1,0:T(8,128)(2,1)S(1)}, u32[]{:S(2)}, u32[]{:S(2)}) %collective-permute-start.18) | collective-permute-done | bytes 393248 | tf_op jit(solution)/shard_map/ppermute | solution.py:1709
  129.1 14.9 %collective-permute-done.25 = f16[128,1536]{1,0:T(8,128)(2,1)S(1)} collective-permute-done((f16[128,1536]{1,0:T(8,128)(2,1)S(1)}, f16[128,1536]{1,0:T(8,128)(2,1)S(1)}, u32[]{:S(2)}, u32[]{:S(2)}) %collective-permute-start.25) | collective-permute-done | bytes 393248 | tf_op jit(solution)/shard_map/ppermute | solution.py:1709
  144.5 5.3 %collective-permute-done.30 = bf16[384,1536]{1,0:T(8,128)(2,1)S(1)} collective-permute-done((bf16[384,1536]{1,0:T(8,128)(2,1)S(1)}, bf16[384,1536]{1,0:T(8,128)(2,1)S(1)}, u32[]{:S(2)}, u32[]{:S(2)}) %collective-permute-start.30) | collective-permute-done | bytes 1179680 | tf_op jit(solution)/shard_map/ppermute | solution.py:1643
  151.6 4.6 collective-permute-start.22
  156.4 14.6 %collective-permute-done.28 = f16[128,1536]{1,0:T(8,128)(2,1)S(1)} collective-permute-done((f16[128,1536]{1,0:T(8,128)(2,1)S(1)}, f16[128,1536]{1,0:T(8,128)(2,1)S(1)}, u32[]{:S(2)}, u32[]{:S(2)}) %collective-permute-start.28) | collective-permute-done | bytes 393248 | tf_op jit(solution)/shard_map/ppermute | solution.py:1709
  171.2 10.5 %front.3 = (f32[512,1536]{1,0:T(8,128)}, bf16[512,1536]{1,0:T(8,128)(2,1)S(1)}, f32[512,128]{1,0:T(8,128)S(1)}, f32[512,1024]{1,0:T(8,128)S(1)}, f32[512,768]{1,...) custom-call(s32[6]{0:T(128)S(1)} %stack.42.refs_0_.where_ref, ...), custom_call_target="tpu_custom_call" | custom-call | flops 1 | bytes 1 | tf_op jit(solution)/shard_map/front/pallas_call | solution.py:142
  181.9 4.4 collective-permute-start.32
  191.1 3.7 project.5.refs_0_
  194.8 3.7 project.4.z_ref.refs_2_
  205.2 3.2 collective-permute-done.34
  209.3 4.6 out.3
  214.0 3.2 gate_back.2
  220.5 8.9 %mix_back.2 = (f32[512,768]{1,0:T(8,128)S(1)}, f32[512,128]{1,0:T(8,128)S(1)}, f32[512,128]{1,0:T(8,128)S(1)}, f32[512,128]{1,0:T(8,128)S(1)}, f32[8,768]{1,0:T(8,128)S(1)}) custom-call(f32[512,768]{1,0:T(8,128)S(1)} %get-tuple-element.189.refs_0_.conv_x_ref, f32[512,256]{1,0:T(8,128)S(1)} %get-tuple-element.190.refs_1_.conv_s_ref.refs_3_, ...), custom_call_target="tpu_custom_call" | custom-call | flops 1 | bytes 1 | tf_op jit(solution)/shard_map/mix_back/pallas_call | solution.py:142
  229.4 5.6 %later.2 = (f32[512,1024]{1,0:T(8,128)S(1)}, bf16[512,128]{1,0:T(8,128)(2,1)S(1)}, f32[8,128]{1,0:T(8,128)S(1)}) custom-call(f32[512,768]{1,0:T(8,128)S(1)} %get-tuple-element.189.refs_0_.conv_x_ref, f32[512,256]{1,0:T(8,128)S(1)} %get-tuple-element.190.refs_1_.conv_s_ref.refs_3_, f32[512,768]{1,0:T(8,128)S(1)} %get-tuple-element.203.refs_2_, ...), custom_call_target="tpu_custom_call" | custom-call | flops 1 | bytes 1 | tf_op jit(solution)/shard_map/later/pallas_call | solution.py:142
  236.3 10.0 %collective-permute-start.39 = (f32[8,1024]{1,0:T(8,128)S(1)}, f32[8,1024]{1,0:T(8,128)S(1)}, u32[]{:S(2)}, u32[]{:S(2)}) collective-permute-start(f32[8,1024]{1,0:T(8,128)S(1)} %slice.100), channel_id=1, source_target_pairs={{4,0},{5,1},{6,2},{7,3},{12,8},{13,9},{14,10},{15,11},{20,16},{21,... | collective-permute-start | bytes 98312 | tf_op jit(solution)/shard_map/ppermute | solution.py:1648
  246.6 11.7 %conv_back.2 = (bf16[512,1536]{1,0:T(8,128)(2,1)S(1)}, bf16[512,1536]{1,0:T(8,128)(2,1)S(1)}, bf16[128,1536]{1,0:T(8,128)(2,1)S(1)}, f32[128,1536]{1,0:T(8,128)S...) custom-call(s32[6]{0:T(128)S(1)} %stack.42.refs_0_.where_ref, ...), custom_call_target="tpu_custom_call" | custom-call | flops 1 | bytes 1 | tf_op jit(solution)/shard_map/conv_back/pallas_call | solution.py:142
  260.9 2.9 renorm.2.refs_1_
  263.8 8.6 %wgrad.2 = (bf16[2,192,1536]{2,1,0:T(8,128)(2,1)S(1)}, bf16[2,192,1536]{2,1,0:T(8,128)(2,1)S(1)}, bf16[2,192,1536]{2,1,0:T(8,128)(2,1)S(1)}, bf16[2,192,1536]{2,1,0:T(8,128)(2,1)S(1)}) custom-call(s32[6]{0:T(128)S(1)} %stack.42.refs_0_.where_ref, bf16[512,1536]{1,0:T(8,128)(2,1)S(1)} %copy-done.31, bf16[512,1536]{1,0:T(8,128)(2,1)S(1)} %renorm.2.refs_1_, ...), custom_call_target="tpu_custom_call" | custom-call | flops 1 | bytes 1 | tf_op jit(solution)/shard_map/wgrad/pallas_call | solution.py:1535
  272.4 6.5 %collective-permute-done.41.refs_2_ = bf16[128,1536]{1,0:T(8,128)(2,1)S(1)} collective-permute-done((bf16[128,1536]{1,0:T(8,128)(2,1)S(1)}, bf16[128,1536]{1,0:T(8,128)(2,1)S(1)}, u32[]{:S(2)}, u32[]{:S(2)}) %collective-permute-start.41) | collective-permute-done | bytes 393248 | tf_op jit(solution)/shard_map/ppermute | solution.py:1709
  284.8 3.2 collective-permute-start.45
  288.0 15.0 %collective-permute-done.44.refs_2_ = bf16[128,1536]{1,0:T(8,128)(2,1)S(1)} collective-permute-done((bf16[128,1536]{1,0:T(8,128)(2,1)S(1)}, bf16[128,1536]{1,0:T(8,128)(2,1)S(1)}, u32[]{:S(2)}, u32[]{:S(2)}) %collective-permute-start.44) | collective-permute-done | bytes 393248 | tf_op jit(solution)/shard_map/ppermute | solution.py:1709
  303.7 3.0 collective-permute-start.47
  311.5 9.7 %collective-permute-done.46.refs_6_ = bf16[128,1536]{1,0:T(8,128)(2,1)S(1)} collective-permute-done((bf16[128,1536]{1,0:T(8,128)(2,1)S(1)}, bf16[128,1536]{1,0:T(8,128)(2,1)S(1)}, u32[]{:S(2)}, u32[]{:S(2)}) %collective-permute-start.46) | collective-permute-done | bytes 393248 | tf_op jit(solution)/shard_map/ppermute | solution.py:1709
  323.7 6.4 %finish.2 = (f32[512,1536]{1,0:T(8,128)S(1)}, bf16[512,1536]{1,0:T(8,128)(2,1)S(1)}, f32[512,768]{1,0:T(8,128)S(1)}, f32[8,512]{1,0:T(8,128)S(1)}) custom-call(s32[6]{0:T(128)S(1)} %stack.42.refs_0_.where_ref, bf16[512,1536]{1,0:T(8,128)(2,1)S(1)} %get-tuple-element.377.refs_1_.refs_2_, f32[512,1536]{1,0:T(8,128)S(1)} %copy-done.1, ...), custom_call_target="tpu_custom_call" | custom-call | flops 1 | bytes 1 | tf_op jit(solution)/shard_map/finish/pallas_call | solution.py:142
  331.2 3.3 gate_back.3
  336.1 9.1 %mix_back.3 = (f32[512,768]{1,0:T(8,128)S(1)}, f32[512,128]{1,0:T(8,128)S(1)}, f32[512,128]{1,0:T(8,128)S(1)}, f32[512,128]{1,0:T(8,128)S(1)}, f32[8,768]{1,0:T(8,128)S(1)}) custom-call(f32[512,768]{1,0:T(8,128)S(1)} %get-tuple-element.167.refs_0_.conv_x_ref, f32[512,256]{1,0:T(8,128)S(1)} %copy-done.12, f32[512,768]{1,0:T(8,128)S(1)} %get-tuple-element.246.refs_2_, ...), custom_call_target="tpu_custom_call" | custom-call | flops 1 | bytes 1 | tf_op jit(solution)/shard_map/mix_back/pallas_call | solution.py:142
  345.2 5.4 %collective-permute-done.52 = bf16[128,768]{1,0:T(8,128)(2,1)S(1)} collective-permute-done((bf16[128,768]{1,0:T(8,128)(2,1)S(1)}, bf16[128,768]{1,0:T(8,128)(2,1)S(1)}, u32[]{:S(2)}, u32[]{:S(2)}) %collective-permute-start.52) | collective-permute-done | bytes 196640 | tf_op jit(solution)/shard_map/ppermute | solution.py:1648
  352.0 5.8 %later.3 = (f32[512,1024]{1,0:T(8,128)S(1)}, bf16[512,128]{1,0:T(8,128)(2,1)S(1)}, f32[8,128]{1,0:T(8,128)S(1)}) custom-call(f32[512,768]{1,0:T(8,128)S(1)} %get-tuple-element.167.refs_0_.conv_x_ref, f32[512,256]{1,0:T(8,128)S(1)} %copy-done.12, f32[512,768]{1,0:T(8,128)S(1)} %get-tuple-element.246.refs_2_, f32[512,128]{1,0:T(8,128)S(1)} %copy-done.43, ...), custom_call_target="tpu_custom_call" | custom-call | flops 1 | bytes 1 | tf_op jit(solution)/shard_map/later/pallas_call | solution.py:142
  362.3 4.5 collective-permute-done.56.refs_7_
  370.0 10.9 %conv_back.3 = (bf16[512,1536]{1,0:T(8,128)(2,1)S(1)}, bf16[512,1536]{1,0:T(8,128)(2,1)S(1)}, bf16[128,1536]{1,0:T(8,128)(2,1)S(1)}, f32[128,1536]{1,0:T(8,128)S...) custom-call(s32[6]{0:T(128)S(1)} %stack.42.refs_0_.where_ref, ...), custom_call_target="tpu_custom_call" | custom-call | flops 1 | bytes 1 | tf_op jit(solution)/shard_map/conv_back/pallas_call | solution.py:142
  387.1 8.6 %wgrad.3 = (bf16[2,192,1536]{2,1,0:T(8,128)(2,1)S(1)}, bf16[2,192,1536]{2,1,0:T(8,128)(2,1)S(1)}, bf16[2,192,1536]{2,1,0:T(8,128)(2,1)S(1)}, bf16[2,192,1536]{2,1,0:T(8,128)(2,1)S(1)}) custom-call(s32[6]{0:T(128)S(1)} %stack.42.refs_0_.where_ref, bf16[512,1536]{1,0:T(8,128)(2,1)S(1)} %copy-done.33, bf16[512,1536]{1,0:T(8,128)(2,1)S(1)} %renorm.3.refs_1_, ...), custom_call_target="tpu_custom_call" | custom-call | flops 1 | bytes 1 | tf_op jit(solution)/shard_map/wgrad/pallas_call | solution.py:1535
  395.7 6.2 %collective-permute-done.60.refs_2_ = bf16[128,1536]{1,0:T(8,128)(2,1)S(1)} collective-permute-done((bf16[128,1536]{1,0:T(8,128)(2,1)S(1)}, bf16[128,1536]{1,0:T(8,128)(2,1)S(1)}, u32[]{:S(2)}, u32[]{:S(2)}) %collective-permute-start.60) | collective-permute-done | bytes 393248 | tf_op jit(solution)/shard_map/ppermute | solution.py:1709
  408.1 17.8 %collective-permute-done.64.refs_2_ = bf16[128,1536]{1,0:T(8,128)(2,1)S(1)} collective-permute-done((bf16[128,1536]{1,0:T(8,128)(2,1)S(1)}, bf16[128,1536]{1,0:T(8,128)(2,1)S(1)}, u32[]{:S(2)}, u32[]{:S(2)}) %collective-permute-start.64) | collective-permute-done | bytes 393248 | tf_op jit(solution)/shard_map/ppermute | solution.py:1709
  426.2 3.3 collective-permute-done.62.refs_2_
  437.7 6.4 %tokens.2 = (f32[1,2,512,1536]{3,2,1,0:T(8,128)}, f32[8,128]{1,0:T(8,128)S(1)}) custom-call(s32[6]{0:T(128)S(1)} %stack.42.refs_0_.where_ref, f32[512,1536]{1,0:T(8,128)S(1)} %copy-done.1, f32[512,1536]{1,0:T(8,128)} %collective-permute-done.29.refs_0_.got0, f32[512,1536]{1,0:T(8,128)S(1)} %join.1.refs_3_.own1, ...), custom_call_target="tpu_custom_call" | custom-call | flops 1 | bytes 1 | tf_op jit(solution)/shard_map/tokens/pallas_call | solution.py:1885
  445.3 3.2 collective-permute-start.71
  451.2 3.7 collective-permute-done.74.refs_1_
  463.6 3.1 collective-permute-done.76.refs_2_
  469.9 3.6 tokens.3
  481.8 2.8 matrices.1
  (437 shorter events, 165.3 us)
Async XLA Ops:
  2.9 13.9 %collective-permute-start = (bf16[768,1536]{1,0:T(8,128)(2,1)S(1)}, bf16[768,1536]{1,0:T(8,128)(2,1)}, u32[]{:S(2)}, u32[]{:S(2)}) collective-permute-start(bf16[768,1536]{1,0:T(8,128)(2,1)S(1)} %bitcast.48), channel_id=1, source_target_pairs={{0,16},{16,0},{1,17},{17,1},{2,18},{18,2},{3,19},{19,3},{4,20},{20... | collective-permute-start | bytes 7077896 | tf_op jit(solution)/shard_map/ppermute | solution.py:1643
  7.0 19.1 %collective-permute-start.14 = (bf16[768,768]{1,0:T(8,128)(2,1)S(1)}, bf16[768,768]{1,0:T(8,128)(2,1)}, u32[]{:S(2)}, u32[]{:S(2)}) collective-permute-start(bf16[768,768]{1,0:T(8,128)(2,1)S(1)} %bitcast.61), channel_id=1, source_target_pairs={{0,16},{16,0},{1,17},{17,1},{2,18},{18,2},{3,19},{19,3},{4,20},{20... | collective-permute-start | bytes 3538952 | tf_op jit(solution)/shard_map/ppermute | solution.py:1643
  19.6 23.3 %collective-permute-start.6 = (bf16[384,1152]{1,0:T(8,128)(2,1)}, bf16[384,1152]{1,0:T(8,128)(2,1)}, u32[]{:S(2)}, u32[]{:S(2)}) collective-permute-start(bf16[384,1152]{1,0:T(8,128)(2,1)} %pieces.5), channel_id=1, source_target_pairs={{0,8},{8,0},{1,9},{9,1},{2,10},{10,2},{3,11},{11,3},{4,12},{12,4},... | collective-permute-start | bytes 2654216 | tf_op jit(solution)/shard_map/ppermute | solution.py:1643
  29.5 17.9 %collective-permute-start.4 = (f32[8]{0:T(128)S(1)}, f32[8]{0:T(128)S(1)}, u32[]{:S(2)}, u32[]{:S(2)}) collective-permute-start(f32[8]{0:T(128)S(1)} %get-tuple-element.386), channel_id=1, source_target_pairs={{0,4},{1,5},{2,6},{3,7},{8,12},{9,13},{10,14},{11,15},{16,20},{17,... | collective-permute-start | bytes 104 | tf_op jit(solution)/shard_map/ppermute | solution.py:1648
  32.9 14.5 %collective-permute-start.3 = (f32[8]{0:T(128)S(1)}, f32[8]{0:T(128)S(1)}, u32[]{:S(2)}, u32[]{:S(2)}) collective-permute-start(f32[8]{0:T(128)S(1)} %get-tuple-element.387), channel_id=1, source_target_pairs={{4,0},{5,1},{6,2},{7,3},{12,8},{13,9},{14,10},{15,11},{20,16},{21,... | collective-permute-start | bytes 104 | tf_op jit(solution)/shard_map/ppermute | solution.py:1648
  35.0 14.5 %collective-permute-start.2 = (bf16[8,1536]{1,0:T(8,128)(2,1)S(1)}, bf16[8,1536]{1,0:T(8,128)(2,1)S(1)}, u32[]{:S(2)}, u32[]{:S(2)}) collective-permute-start(bf16[8,1536]{1,0:T(8,128)(2,1)S(1)} %add_bitcast_fusion), channel_id=1, source_target_pairs={{0,4},{1,5},{2,6},{3,7},{8,12},{9,13},{10,14},{11,15},{16,20},{17,... | collective-permute-start | bytes 73736 | tf_op jit(solution)/shard_map/ppermute | solution.py:1648
  45.6 19.8 %collective-permute-start.8 = (bf16[384,768]{1,0:T(8,128)(2,1)}, bf16[384,768]{1,0:T(8,128)(2,1)}, u32[]{:S(2)}, u32[]{:S(2)}) collective-permute-start(bf16[384,768]{1,0:T(8,128)(2,1)} %broadcast_add_fusion.5), channel_id=1, source_target_pairs={{0,8},{8,0},{1,9},{9,1},{2,10},{10,2},{3,11},{11,3},{4,12},{12,4},... | collective-permute-start | bytes 1769480 | tf_op jit(solution)/shard_map/ppermute | solution.py:1643
  68.4 15.8 %collective-permute-start.15 = (bf16[384,768]{1,0:T(8,128)(2,1)S(1)}, bf16[384,768]{1,0:T(8,128)(2,1)S(1)}, u32[]{:S(2)}, u32[]{:S(2)}) collective-permute-start(bf16[384,768]{1,0:T(8,128)(2,1)S(1)} %broadcast_add_fusion.3), channel_id=1, source_target_pairs={{0,8},{8,0},{1,9},{9,1},{2,10},{10,2},{3,11},{11,3},{4,12},{12,4},... | collective-permute-start | bytes 1769480 | tf_op jit(solution)/shard_map/ppermute | solution.py:1643
  97.9 19.6 %collective-permute-start.18 = (f16[128,1536]{1,0:T(8,128)(2,1)S(1)}, f16[128,1536]{1,0:T(8,128)(2,1)S(1)}, u32[]{:S(2)}, u32[]{:S(2)}) collective-permute-start(f16[128,1536]{1,0:T(8,128)(2,1)S(1)} %convert_element_type.171), channel_id=1, source_target_pairs={{0,2},{2,0},{1,3},{3,1},{4,6},{6,4},{5,7},{7,5},{8,10},{10,8},{9,1... | collective-permute-start | bytes 1179656 | tf_op jit(solution)/shard_map/ppermute | solution.py:1709
  99.1 18.4 %collective-permute-start.17 = (f16[128,1536]{1,0:T(8,128)(2,1)S(1)}, f16[128,1536]{1,0:T(8,128)(2,1)S(1)}, u32[]{:S(2)}, u32[]{:S(2)}) collective-permute-start(f16[128,1536]{1,0:T(8,128)(2,1)S(1)} %convert_element_type.169), channel_id=1, source_target_pairs={{0,1},{1,0},{2,3},{3,2},{4,5},{5,4},{6,7},{7,6},{8,9},{9,8},{10,11... | collective-permute-start | bytes 1179656 | tf_op jit(solution)/shard_map/ppermute | solution.py:1709
  99.2 24.7 %collective-permute-start.23 = (bf16[384,1152]{1,0:T(8,128)(2,1)S(1)}, bf16[384,1152]{1,0:T(8,128)(2,1)S(1)}, u32[]{:S(2)}, u32[]{:S(2)}) collective-permute-start(bf16[384,1152]{1,0:T(8,128)(2,1)S(1)} %pieces.8.refs_8_), channel_id=1, source_target_pairs={{0,8},{8,0},{1,9},{9,1},{2,10},{10,2},{3,11},{11,3},{4,12},{12,4},... | collective-permute-start | bytes 2654216 | tf_op jit(solution)/shard_map/ppermute | solution.py:1643
  121.0 23.1 %collective-permute-start.26 = (f16[128,1536]{1,0:T(8,128)(2,1)S(1)}, f16[128,1536]{1,0:T(8,128)(2,1)S(1)}, u32[]{:S(2)}, u32[]{:S(2)}) collective-permute-start(f16[128,1536]{1,0:T(8,128)(2,1)S(1)} %get-tuple-element.369), channel_id=1, source_target_pairs={{0,1},{1,0},{2,3},{3,2},{4,5},{5,4},{6,7},{7,6},{8,9},{9,8},{10,11... | collective-permute-start | bytes 1179656 | tf_op jit(solution)/shard_map/ppermute | solution.py:1709
  123.9 26.0 %collective-permute-start.30 = (bf16[384,1536]{1,0:T(8,128)(2,1)S(1)}, bf16[384,1536]{1,0:T(8,128)(2,1)S(1)}, u32[]{:S(2)}, u32[]{:S(2)}) collective-permute-start(bf16[384,1536]{1,0:T(8,128)(2,1)S(1)} %get-tuple-element.195), channel_id=1, source_target_pairs={{0,8},{8,0},{1,9},{9,1},{2,10},{10,2},{3,11},{11,3},{4,12},{12,4},... | collective-permute-start | bytes 3538952 | tf_op jit(solution)/shard_map/ppermute | solution.py:1643
  125.7 18.3 %collective-permute-start.25 = (f16[128,1536]{1,0:T(8,128)(2,1)S(1)}, f16[128,1536]{1,0:T(8,128)(2,1)S(1)}, u32[]{:S(2)}, u32[]{:S(2)}) collective-permute-start(f16[128,1536]{1,0:T(8,128)(2,1)S(1)} %get-tuple-element.371), channel_id=1, source_target_pairs={{0,2},{2,0},{1,3},{3,1},{4,6},{6,4},{5,7},{7,5},{8,10},{10,8},{9,1... | collective-permute-start | bytes 1179656 | tf_op jit(solution)/shard_map/ppermute | solution.py:1709
  127.2 44.0 %collective-permute-start.24 = (bf16[384,1152]{1,0:T(8,128)(2,1)S(1)}, bf16[384,1152]{1,0:T(8,128)(2,1)S(1)}, u32[]{:S(2)}, u32[]{:S(2)}) collective-permute-start(bf16[384,1152]{1,0:T(8,128)(2,1)S(1)} %broadcast_add_fusion.1.refs_10_.refs_20_), channel_id=1, source_target_pairs={{0,16},{16,0},{1,17},{17,1},{2,18},{18,2},{3,19},{19,3},{4,20},{20... | collective-permute-start | bytes 2654216 | tf_op jit(solution)/shard_map/ppermute | solution.py:1643
  150.0 41.1 %collective-permute-start.31 = (bf16[384,1536]{1,0:T(8,128)(2,1)S(1)}, bf16[384,1536]{1,0:T(8,128)(2,1)S(1)}, u32[]{:S(2)}, u32[]{:S(2)}) collective-permute-start(bf16[384,1536]{1,0:T(8,128)(2,1)S(1)} %broadcast_add_fusion.refs_4_.refs_6_.refs_24_), channel_id=1, source_target_pairs={{0,16},{16,0},{1,17},{17,1},{2,18},{18,2},{3,19},{19,3},{4,20},{20... | collective-permute-start | bytes 3538952 | tf_op jit(solution)/shard_map/ppermute | solution.py:1643
  150.2 20.8 %collective-permute-start.28 = (f16[128,1536]{1,0:T(8,128)(2,1)S(1)}, f16[128,1536]{1,0:T(8,128)(2,1)S(1)}, u32[]{:S(2)}, u32[]{:S(2)}) collective-permute-start(f16[128,1536]{1,0:T(8,128)(2,1)S(1)} %get-tuple-element.365), channel_id=1, source_target_pairs={{0,2},{2,0},{1,3},{3,1},{4,6},{6,4},{5,7},{7,5},{8,10},{10,8},{9,1... | collective-permute-start | bytes 1179656 | tf_op jit(solution)/shard_map/ppermute | solution.py:1709
  151.6 19.5 %collective-permute-start.22 = (f32[8,1536]{1,0:T(8,128)S(1)}, f32[8,1536]{1,0:T(8,128)S(1)}, u32[]{:S(2)}, u32[]{:S(2)}) collective-permute-start(f32[8,1536]{1,0:T(8,128)S(1)} %convert_add_fusion.refs_2_), channel_id=1, source_target_pairs={{0,4},{1,5},{2,6},{3,7},{8,12},{9,13},{10,14},{11,15},{16,20},{17,... | collective-permute-start | bytes 147464 | tf_op jit(solution)/shard_map/ppermute | solution.py:1648
  181.8 79.1 %collective-permute-start.29 = (f32[512,1536]{1,0:T(8,128)}, f32[512,1536]{1,0:T(8,128)}, u32[]{:S(2)}, u32[]{:S(2)}) collective-permute-start(f32[512,1536]{1,0:T(8,128)} %get-tuple-element.188.refs_10_.refs_2_.refs_1_.own0), channel_id=1, source_target_pairs={{0,16},{16,0},{1,17},{17,1},{2,18},{18,2},{3,19},{19,3},{4,20},{20... | collective-permute-start | bytes 9437192 | tf_op jit(solution)/shard_map/ppermute | solution.py:1643
  213.9 21.2 %collective-permute-start.36 = (bf16[128,1536]{1,0:T(8,128)(2,1)S(1)}, bf16[128,1536]{1,0:T(8,128)(2,1)S(1)}, u32[]{:S(2)}, u32[]{:S(2)}) collective-permute-start(bf16[128,1536]{1,0:T(8,128)(2,1)S(1)} %get-tuple-element.201), channel_id=1, source_target_pairs={{0,1},{1,0},{2,3},{3,2},{4,5},{5,4},{6,7},{7,6},{8,9},{9,8},{10,11... | collective-permute-start | bytes 1179656 | tf_op jit(solution)/shard_map/ppermute | solution.py:1709
  218.5 27.9 %collective-permute-start.40 = (bf16[128,1536]{1,0:T(8,128)(2,1)S(1)}, bf16[128,1536]{1,0:T(8,128)(2,1)S(1)}, u32[]{:S(2)}, u32[]{:S(2)}) collective-permute-start(bf16[128,1536]{1,0:T(8,128)(2,1)S(1)} %get-tuple-element.223), channel_id=1, source_target_pairs={{0,1},{1,0},{2,3},{3,2},{4,5},{5,4},{6,7},{7,6},{8,9},{9,8},{10,11... | collective-permute-start | bytes 1179656 | tf_op jit(solution)/shard_map/ppermute | solution.py:1709
  235.2 23.2 %collective-permute-start.38 = (bf16[128,1536]{1,0:T(8,128)(2,1)S(1)}, bf16[128,1536]{1,0:T(8,128)(2,1)S(1)}, u32[]{:S(2)}, u32[]{:S(2)}) collective-permute-start(bf16[128,1536]{1,0:T(8,128)(2,1)S(1)} %merge.17.refs_26_.refs_0_), channel_id=1, source_target_pairs={{0,2},{2,0},{1,3},{3,1},{4,6},{6,4},{5,7},{7,5},{8,10},{10,8},{9,1... | collective-permute-start | bytes 1179656 | tf_op jit(solution)/shard_map/ppermute | solution.py:1709
  259.0 20.0 %collective-permute-start.41 = (bf16[128,1536]{1,0:T(8,128)(2,1)S(1)}, bf16[128,1536]{1,0:T(8,128)(2,1)S(1)}, u32[]{:S(2)}, u32[]{:S(2)}) collective-permute-start(bf16[128,1536]{1,0:T(8,128)(2,1)S(1)} %get-tuple-element.230), channel_id=1, source_target_pairs={{0,1},{1,0},{2,3},{3,2},{4,5},{5,4},{6,7},{7,6},{8,9},{9,8},{10,11... | collective-permute-start | bytes 1179656 | tf_op jit(solution)/shard_map/ppermute | solution.py:1709
  259.1 19.9 %collective-permute-start.42 = (bf16[128,1536]{1,0:T(8,128)(2,1)S(1)}, bf16[128,1536]{1,0:T(8,128)(2,1)S(1)}, u32[]{:S(2)}, u32[]{:S(2)}) collective-permute-start(bf16[128,1536]{1,0:T(8,128)(2,1)S(1)} %get-tuple-element.231), channel_id=1, source_target_pairs={{0,2},{2,0},{1,3},{3,1},{4,6},{6,4},{5,7},{7,5},{8,10},{10,8},{9,1... | collective-permute-start | bytes 1179656 | tf_op jit(solution)/shard_map/ppermute | solution.py:1709
  279.3 27.7 %collective-permute-start.48 = (bf16[2,192,1536]{2,1,0:T(8,128)(2,1)S(1)}, bf16[2,192,1536]{2,1,0:T(8,128)(2,1)S(1)}, u32[]{:S(2)}, u32[]{:S(2)}) collective-permute-start(bf16[2,192,1536]{2,1,0:T(8,128)(2,1)S(1)} %get-tuple-element.241), channel_id=1, source_target_pairs={{0,8},{8,0},{1,9},{9,1},{2,10},{10,2},{3,11},{11,3},{4,12},{12,4},... | collective-permute-start | bytes 3538952 | tf_op jit(solution)/shard_map/ppermute | solution.py:1643
  280.8 28.2 %collective-permute-start.49 = (bf16[2,192,1536]{2,1,0:T(8,128)(2,1)S(1)}, bf16[2,192,1536]{2,1,0:T(8,128)(2,1)S(1)}, u32[]{:S(2)}, u32[]{:S(2)}) collective-permute-start(bf16[2,192,1536]{2,1,0:T(8,128)(2,1)S(1)} %get-tuple-element.242), channel_id=1, source_target_pairs={{0,4},{4,0},{1,5},{5,1},{2,6},{6,2},{3,7},{7,3},{8,12},{12,8},{9,1... | collective-permute-start | bytes 3538952 | tf_op jit(solution)/shard_map/ppermute | solution.py:1643
  283.5 19.5 %collective-permute-start.44 = (bf16[128,1536]{1,0:T(8,128)(2,1)S(1)}, bf16[128,1536]{1,0:T(8,128)(2,1)S(1)}, u32[]{:S(2)}, u32[]{:S(2)}) collective-permute-start(bf16[128,1536]{1,0:T(8,128)(2,1)S(1)} %get-tuple-element.234.refs_0_), channel_id=1, source_target_pairs={{0,2},{2,0},{1,3},{3,1},{4,6},{6,4},{5,7},{7,5},{8,10},{10,8},{9,1... | collective-permute-start | bytes 1179656 | tf_op jit(solution)/shard_map/ppermute | solution.py:1709
  284.8 18.2 %collective-permute-start.45 = (bf16[128,1536]{1,0:T(8,128)(2,1)S(1)}, bf16[128,1536]{1,0:T(8,128)(2,1)S(1)}, u32[]{:S(2)}, u32[]{:S(2)}) collective-permute-start(bf16[128,1536]{1,0:T(8,128)(2,1)S(1)} %get-tuple-element.235.refs_1_.refs_2_), channel_id=1, source_target_pairs={{0,1},{1,0},{2,3},{3,2},{4,5},{5,4},{6,7},{7,6},{8,9},{9,8},{10,11... | collective-permute-start | bytes 1179656 | tf_op jit(solution)/shard_map/ppermute | solution.py:1709
  303.2 18.0 %collective-permute-start.46 = (bf16[128,1536]{1,0:T(8,128)(2,1)S(1)}, bf16[128,1536]{1,0:T(8,128)(2,1)S(1)}, u32[]{:S(2)}, u32[]{:S(2)}) collective-permute-start(bf16[128,1536]{1,0:T(8,128)(2,1)S(1)} %get-tuple-element.236.refs_5_), channel_id=1, source_target_pairs={{0,1},{1,0},{2,3},{3,2},{4,5},{5,4},{6,7},{7,6},{8,9},{9,8},{10,11... | collective-permute-start | bytes 1179656 | tf_op jit(solution)/shard_map/ppermute | solution.py:1709
  303.7 19.9 %collective-permute-start.47 = (bf16[128,1536]{1,0:T(8,128)(2,1)S(1)}, bf16[128,1536]{1,0:T(8,128)(2,1)S(1)}, u32[]{:S(2)}, u32[]{:S(2)}) collective-permute-start(bf16[128,1536]{1,0:T(8,128)(2,1)S(1)} %get-tuple-element.237.refs_4_.refs_7_), channel_id=1, source_target_pairs={{0,2},{2,0},{1,3},{3,1},{4,6},{6,4},{5,7},{7,5},{8,10},{10,8},{9,1... | collective-permute-start | bytes 1179656 | tf_op jit(solution)/shard_map/ppermute | solution.py:1709
  330.1 36.7 %collective-permute-start.57 = (f32[512,1536]{1,0:T(8,128)S(1)}, f32[512,1536]{1,0:T(8,128)S(1)}, u32[]{:S(2)}, u32[]{:S(2)}) collective-permute-start(f32[512,1536]{1,0:T(8,128)S(1)} %get-tuple-element.269.refs_1_.own1), channel_id=1, source_target_pairs={{0,16},{16,0},{1,17},{17,1},{2,18},{18,2},{3,19},{19,3},{4,20},{20... | collective-permute-start | bytes 9437192 | tf_op jit(solution)/shard_map/ppermute | solution.py:1643
  330.2 20.8 %collective-permute-start.54 = (bf16[192,1536]{1,0:T(8,128)(2,1)S(1)}, bf16[192,1536]{1,0:T(8,128)(2,1)S(1)}, u32[]{:S(2)}, u32[]{:S(2)}) collective-permute-start(bf16[192,1536]{1,0:T(8,128)(2,1)S(1)} %copy-done.84), channel_id=1, source_target_pairs={{0,8},{8,0},{1,9},{9,1},{2,10},{10,2},{3,11},{11,3},{4,12},{12,4},... | collective-permute-start | bytes 1769480 | tf_op jit(solution)/shard_map/ppermute | solution.py:1643
  330.8 20.2 %collective-permute-start.53 = (bf16[192,1536]{1,0:T(8,128)(2,1)}, bf16[192,1536]{1,0:T(8,128)(2,1)S(1)}, u32[]{:S(2)}, u32[]{:S(2)}) collective-permute-start(bf16[192,1536]{1,0:T(8,128)(2,1)} %copy-done.67), channel_id=1, source_target_pairs={{0,4},{4,0},{1,5},{5,1},{2,6},{6,2},{3,7},{7,3},{8,12},{12,8},{9,1... | collective-permute-start | bytes 1769480 | tf_op jit(solution)/shard_map/ppermute | solution.py:1643
  331.1 26.7 %collective-permute-start.51 = (bf16[128,1536]{1,0:T(8,128)(2,1)S(1)}, bf16[128,1536]{1,0:T(8,128)(2,1)S(1)}, u32[]{:S(2)}, u32[]{:S(2)}) collective-permute-start(bf16[128,1536]{1,0:T(8,128)(2,1)S(1)} %hold.11.refs_12_), channel_id=1, source_target_pairs={{0,2},{2,0},{1,3},{3,1},{4,6},{6,4},{5,7},{7,5},{8,10},{10,8},{9,1... | collective-permute-start | bytes 1179656 | tf_op jit(solution)/shard_map/ppermute | solution.py:1709
  334.6 16.0 %collective-permute-start.52 = (bf16[128,768]{1,0:T(8,128)(2,1)S(1)}, bf16[128,768]{1,0:T(8,128)(2,1)S(1)}, u32[]{:S(2)}, u32[]{:S(2)}) collective-permute-start(bf16[128,768]{1,0:T(8,128)(2,1)S(1)} %convert_element_type.194), channel_id=1, source_target_pairs={{4,0},{5,1},{6,2},{7,3},{12,8},{13,9},{14,10},{15,11},{20,16},{21,... | collective-permute-start | bytes 589832 | tf_op jit(solution)/shard_map/ppermute | solution.py:1648
  357.9 23.0 %collective-permute-start.55 = (bf16[128,1536]{1,0:T(8,128)(2,1)S(1)}, bf16[128,1536]{1,0:T(8,128)(2,1)S(1)}, u32[]{:S(2)}, u32[]{:S(2)}) collective-permute-start(bf16[128,1536]{1,0:T(8,128)(2,1)S(1)} %merge.22.refs_27_.refs_4_), channel_id=1, source_target_pairs={{0,1},{1,0},{2,3},{3,2},{4,5},{5,4},{6,7},{7,6},{8,9},{9,8},{10,11... | collective-permute-start | bytes 1179656 | tf_op jit(solution)/shard_map/ppermute | solution.py:1709
  382.2 54.1 %collective-permute-start.58 = (f32[512,1536]{1,0:T(8,128)S(1)}, f32[512,1536]{1,0:T(8,128)S(1)}, u32[]{:S(2)}, u32[]{:S(2)}) collective-permute-start(f32[512,1536]{1,0:T(8,128)S(1)} %join.1.refs_3_.own1), channel_id=1, source_target_pairs={{0,16},{16,0},{1,17},{17,1},{2,18},{18,2},{3,19},{19,3},{4,20},{20... | collective-permute-start | bytes 9437192 | tf_op jit(solution)/shard_map/ppermute | solution.py:1643
  382.7 19.3 %collective-permute-start.60 = (bf16[128,1536]{1,0:T(8,128)(2,1)S(1)}, bf16[128,1536]{1,0:T(8,128)(2,1)S(1)}, u32[]{:S(2)}, u32[]{:S(2)}) collective-permute-start(bf16[128,1536]{1,0:T(8,128)(2,1)S(1)} %get-tuple-element.282), channel_id=1, source_target_pairs={{0,1},{1,0},{2,3},{3,2},{4,5},{5,4},{6,7},{7,6},{8,9},{9,8},{10,11... | collective-permute-start | bytes 1179656 | tf_op jit(solution)/shard_map/ppermute | solution.py:1709
  383.0 20.2 %collective-permute-start.61 = (bf16[128,1536]{1,0:T(8,128)(2,1)S(1)}, bf16[128,1536]{1,0:T(8,128)(2,1)S(1)}, u32[]{:S(2)}, u32[]{:S(2)}) collective-permute-start(bf16[128,1536]{1,0:T(8,128)(2,1)S(1)} %get-tuple-element.283), channel_id=1, source_target_pairs={{0,2},{2,0},{1,3},{3,1},{4,6},{6,4},{5,7},{7,5},{8,10},{10,8},{9,1... | collective-permute-start | bytes 1179656 | tf_op jit(solution)/shard_map/ppermute | solution.py:1709
  403.5 25.9 %collective-permute-start.62 = (bf16[2,192,1536]{2,1,0:T(8,128)(2,1)S(1)}, bf16[2,192,1536]{2,1,0:T(8,128)(2,1)S(1)}, u32[]{:S(2)}, u32[]{:S(2)}) collective-permute-start(bf16[2,192,1536]{2,1,0:T(8,128)(2,1)S(1)} %get-tuple-element.285), channel_id=1, source_target_pairs={{0,8},{8,0},{1,9},{9,1},{2,10},{10,2},{3,11},{11,3},{4,12},{12,4},... | collective-permute-start | bytes 3538952 | tf_op jit(solution)/shard_map/ppermute | solution.py:1643
  405.1 25.6 %collective-permute-start.63 = (bf16[2,192,1536]{2,1,0:T(8,128)(2,1)S(1)}, bf16[2,192,1536]{2,1,0:T(8,128)(2,1)S(1)}, u32[]{:S(2)}, u32[]{:S(2)}) collective-permute-start(bf16[2,192,1536]{2,1,0:T(8,128)(2,1)S(1)} %get-tuple-element.286), channel_id=1, source_target_pairs={{0,4},{4,0},{1,5},{5,1},{2,6},{6,2},{3,7},{7,3},{8,12},{12,8},{9,1... | collective-permute-start | bytes 3538952 | tf_op jit(solution)/shard_map/ppermute | solution.py:1643
  405.1 20.7 %collective-permute-start.64 = (bf16[128,1536]{1,0:T(8,128)(2,1)S(1)}, bf16[128,1536]{1,0:T(8,128)(2,1)S(1)}, u32[]{:S(2)}, u32[]{:S(2)}) collective-permute-start(bf16[128,1536]{1,0:T(8,128)(2,1)S(1)} %get-tuple-element.287.refs_0_), channel_id=1, source_target_pairs={{0,2},{2,0},{1,3},{3,1},{4,6},{6,4},{5,7},{7,5},{8,10},{10,8},{9,1... | collective-permute-start | bytes 1179656 | tf_op jit(solution)/shard_map/ppermute | solution.py:1709
  406.4 19.6 %collective-permute-start.65 = (bf16[128,1536]{1,0:T(8,128)(2,1)S(1)}, bf16[128,1536]{1,0:T(8,128)(2,1)S(1)}, u32[]{:S(2)}, u32[]{:S(2)}) collective-permute-start(bf16[128,1536]{1,0:T(8,128)(2,1)S(1)} %get-tuple-element.284.refs_2_.refs_1_), channel_id=1, source_target_pairs={{0,1},{1,0},{2,3},{3,2},{4,5},{5,4},{6,7},{7,6},{8,9},{9,8},{10,11... | collective-permute-start | bytes 1179656 | tf_op jit(solution)/shard_map/ppermute | solution.py:1709
  431.2 13.0 %collective-permute-start.70 = (bf16[192,1536]{1,0:T(8,128)(2,1)S(1)}, bf16[192,1536]{1,0:T(8,128)(2,1)S(1)}, u32[]{:S(2)}, u32[]{:S(2)}) collective-permute-start(bf16[192,1536]{1,0:T(8,128)(2,1)S(1)} %get-tuple-element.296), channel_id=1, source_target_pairs={{0,8},{8,0},{1,9},{9,1},{2,10},{10,2},{3,11},{11,3},{4,12},{12,4},... | collective-permute-start | bytes 1769480 | tf_op jit(solution)/shard_map/ppermute | solution.py:1643
  432.1 24.2 %collective-permute-start.67 = (bf16[128,1536]{1,0:T(8,128)(2,1)S(1)}, bf16[128,1536]{1,0:T(8,128)(2,1)S(1)}, u32[]{:S(2)}, u32[]{:S(2)}) collective-permute-start(bf16[128,1536]{1,0:T(8,128)(2,1)S(1)} %get-tuple-element.293.refs_5_), channel_id=1, source_target_pairs={{0,1},{1,0},{2,3},{3,2},{4,5},{5,4},{6,7},{7,6},{8,9},{9,8},{10,11... | collective-permute-start | bytes 1179656 | tf_op jit(solution)/shard_map/ppermute | solution.py:1709
  433.9 22.4 %collective-permute-start.68 = (bf16[128,1536]{1,0:T(8,128)(2,1)S(1)}, bf16[128,1536]{1,0:T(8,128)(2,1)S(1)}, u32[]{:S(2)}, u32[]{:S(2)}) collective-permute-start(bf16[128,1536]{1,0:T(8,128)(2,1)S(1)} %get-tuple-element.290.refs_4_.refs_7_), channel_id=1, source_target_pairs={{0,2},{2,0},{1,3},{3,1},{4,6},{6,4},{5,7},{7,5},{8,10},{10,8},{9,1... | collective-permute-start | bytes 1179656 | tf_op jit(solution)/shard_map/ppermute | solution.py:1709
  436.2 14.3 %collective-permute-start.73 = (f32[16,1024]{1,0:T(8,128)S(1)}, f32[16,1024]{1,0:T(8,128)S(1)}, u32[]{:S(2)}, u32[]{:S(2)}) collective-permute-start(f32[16,1024]{1,0:T(8,128)S(1)} %merge.24.refs_4_.refs_0_), channel_id=1, source_target_pairs={{0,8},{8,0},{1,9},{9,1},{2,10},{10,2},{3,11},{11,3},{4,12},{12,4},... | collective-permute-start | bytes 196616 | tf_op jit(solution)/shard_map/ppermute | solution.py:1643
  467.3 14.6 %collective-permute-start.81 = (bf16[384,1152]{1,0:T(8,128)(2,1)S(1)}, bf16[384,1152]{1,0:T(8,128)(2,1)S(1)}, u32[]{:S(2)}, u32[]{:S(2)}) collective-permute-start(bf16[384,1152]{1,0:T(8,128)(2,1)S(1)} %get-tuple-element.311), channel_id=1, source_target_pairs={{0,16},{16,0},{1,17},{17,1},{2,18},{18,2},{3,19},{19,3},{4,20},{20... | collective-permute-start | bytes 2654216 | tf_op jit(solution)/shard_map/ppermute | solution.py:1643
  (127 other events, 1137.8 us)
